TPU v7x, 32 devices: a whole 2x2x4 slice. The times are simulated.
32 devices in a mesh: section: 2 (over x), dp: 4 (over z), tensor: 4 (over y, core).
Axes of the slice: x: 2, y: 2, z: 4, core: 2. Of those that a mesh axis runs over, the one named last changes fastest.
Arguments:
- tokens: bfloat16 [4, 8, 256, 1152], P(None, 'dp', 'tensor'), may hold values from -110 to 110
- velocity_grad: bfloat16 [4, 8, 256, 1152], P(None, 'dp', 'tensor'), may hold values from -6 to 6
- bins: int32 [4, 8], P(None, 'dp'), may hold values from 0 to 999
- labels: int32 [4, 8], P(None, 'dp'), may hold values from 0 to 999
- places: int32 [4, 8, 256], P(None, 'dp'), may hold values from 0 to 255, each once within a row
- class_table: bfloat16 [1000, 1152], replicated, may hold values from -6 to 6
- mod_weight: bfloat16 [2, 1152, 6, 1152], P('section', None, None, 'tensor'), may hold values from -0.1875 to 0.1875
- qkv_weight: bfloat16 [2, 3, 1152, 1152], P('section', None, None, 'tensor'), may hold values from -0.1875 to 0.1875
- out_weight: bfloat16 [2, 1152, 1152], P('section', 'tensor'), may hold values from -0.75 to 0.75
- gate_up_weight: bfloat16 [2, 2, 1152, 3072], P('section', None, None, 'tensor'), may hold values from -0.1875 to 0.1875
- down_weight: bfloat16 [2, 3072, 1152], P('section', 'tensor'), may hold values from -0.109375 to 0.109375
- q_gain: bfloat16 [2, 1152], P('section', 'tensor'), may hold values from 1 to 2
- k_gain: bfloat16 [2, 1152], P('section', 'tensor'), may hold values from 1 to 2
Outputs:
- block_outputs: bfloat16 [2, 4, 8, 256, 1152], P('section', None, 'dp', 'tensor')
- input_grads: float32 [2, 4, 8, 256, 1152], P('section', None, 'dp', 'tensor')
- mod_grad: float32 [2, 1152, 6, 1152], P('section', None, None, 'tensor')
- qkv_grad: float32 [2, 3, 1152, 1152], P('section', None, None, 'tensor')
- out_grad: float32 [2, 1152, 1152], P('section', 'tensor')
- gate_up_grad: float32 [2, 2, 1152, 3072], P('section', None, None, 'tensor')
- down_grad: float32 [2, 3072, 1152], P('section', 'tensor')
- q_gain_grad: float32 [2, 1152], P('section', 'tensor')
- k_gain_grad: float32 [2, 1152], P('section', 'tensor')
- class_grad: float32 [1000, 1152], replicated
- stats: float32 [2, 3], P('section')
Inputs may be any that keep to these rules, and one draw needn't show every extreme that they name: Each image's row holds each of its 256 patch places once.
All inputs are finite; a program needn't handle non-finite values.
Results may differ from a plain program's by a relative error of at most 0.028.
Values may be sent and summed in bfloat16 or wider, within the bound.
A program may use at most 320 MiB of HBM per device.

v0:
```python
import math

import jax
import jax.numpy as jnp
from jax import lax
from jax.sharding import PartitionSpec as P

HEAD_DIM = 72
NBINS = 1000
GRID = 16


epsilon = 1e-06


def from_behind(value, axis, steps):
    count = lax.axis_size(axis)
    first, last = (max(0, -steps), min(count, count - steps))
    return lax.ppermute(value, axis, [(source, source + steps) for source in range(first, last)])


def rms_scale(values):
    return values * lax.rsqrt(jnp.mean(values * values, axis=-1, keepdims=True) + epsilon)


def norm_modulate(values, shifted, scaled):
    return rms_scale(values) * (1.0 + scaled) + shifted


def gating(gate_values, up_values):
    return jax.nn.silu(gate_values) * up_values


def time_embed(bin_row, feature_count):
    halfway = feature_count // 2
    frequency = jnp.exp(-math.log(10000.0) * jnp.arange(halfway, dtype=jnp.float32) / halfway)
    moment = (bin_row.astype(jnp.float32) + 0.5) * (1000.0 / NBINS)
    angles = moment[:, None] * frequency[None, :]
    return jnp.concatenate([jnp.cos(angles), jnp.sin(angles)], axis=-1)


def rope_tables(place_row):
    quarter = HEAD_DIM // 4
    frequency = 10000.0 ** (-jnp.arange(quarter, dtype=jnp.float32) / quarter)
    row_pos = (place_row // GRID).astype(jnp.float32)
    col_pos = (place_row % GRID).astype(jnp.float32)
    angles = jnp.stack([row_pos[..., None] * frequency, col_pos[..., None] * frequency], axis=-2)
    return (jnp.cos(angles), jnp.sin(angles))


def rotate(values, cosine, sine_table):
    layout = values.shape
    pieces = values.reshape(layout[:-1] + (2, 2, layout[-1] // 4))
    former = pieces[..., 0, :]
    latter = pieces[..., 1, :]
    cos_wide = cosine[:, :, None]
    sin_wide = sine_table[:, :, None]
    turned = jnp.stack(
        [former * cos_wide - latter * sin_wide, latter * cos_wide + former * sin_wide], axis=-2
    )
    return turned.reshape(layout)


def head_prepare(raw_values, gain_values, cosine, sine_table):
    return rotate(rms_scale(raw_values) * gain_values, cosine, sine_table)


def softmax_rows(scores):
    shifted = scores - jnp.max(scores, axis=-1, keepdims=True)
    powered = jnp.exp(shifted)
    return powered / jnp.sum(powered, axis=-1, keepdims=True)


def spread_rows(activation):
    return lax.all_gather(activation, "tensor", axis=1, tiled=True)


def collect_rows(partial_rows):
    return lax.psum_scatter(
        partial_rows.astype(jnp.bfloat16), "tensor", scatter_dimension=1, tiled=True
    ).astype(jnp.float32)


def spread_grads(gradient):
    return lax.all_gather(gradient, "tensor", axis=1, tiled=True)


def collect_grads(partial_rows):
    return lax.psum_scatter(
        partial_rows.astype(jnp.bfloat16), "tensor", scatter_dimension=1, tiled=True
    ).astype(jnp.float32)


def modulation_of(silu_low, mod_weight):
    columns = jnp.einsum("id,djf->ijf", silu_low, mod_weight, preferred_element_type=jnp.float32)
    return lax.all_gather(columns, "tensor", axis=2, tiled=True)


def condition(bins, labels, class_table, micro_index):
    bin_row = lax.dynamic_index_in_dim(bins, micro_index, 0, keepdims=False)
    label_row = lax.dynamic_index_in_dim(labels, micro_index, 0, keepdims=False)
    one_hot = label_row[:, None] == jnp.arange(class_table.shape[0], dtype=jnp.int32)[None, :]
    picked = jnp.dot(one_hot.astype(jnp.bfloat16), class_table, preferred_element_type=jnp.float32)
    cond_vec = time_embed(bin_row, class_table.shape[1]) + picked
    return (cond_vec, one_hot.astype(jnp.float32))


def split_modulation(modulation):
    return (
        modulation[:, 0:1, :],
        modulation[:, 1:2, :],
        modulation[:, 2:3, :],
        modulation[:, 3:4, :],
        modulation[:, 4:5, :],
        modulation[:, 5:6, :],
    )


def block_forward(stream, modulation, weights, cosine, sine_table):
    mod_weight, qkv_weight, out_weight, gate_up_weight, down_weight, query_gain, key_gain = weights
    shift_one, scale_one, gate_one, shift_two, scale_two, gate_two = split_modulation(modulation)
    heads_local = query_gain.shape[0] // HEAD_DIM
    gain_query = query_gain.astype(jnp.float32).reshape(heads_local, HEAD_DIM)
    gain_key = key_gain.astype(jnp.float32).reshape(heads_local, HEAD_DIM)
    normed_one = norm_modulate(stream, shift_one, scale_one).astype(jnp.bfloat16)
    spread_one = spread_rows(normed_one)
    images = spread_one.shape[0]
    tokens_all = spread_one.shape[1]
    projected = jnp.einsum(
        "ipd,kde->kipe", spread_one, qkv_weight, preferred_element_type=jnp.float32
    )
    projected = projected.reshape(3, images, tokens_all, heads_local, HEAD_DIM)
    query = head_prepare(projected[0], gain_query, cosine, sine_table).astype(jnp.bfloat16)
    keyed = head_prepare(projected[1], gain_key, cosine, sine_table).astype(jnp.bfloat16)
    valued = projected[2].astype(jnp.bfloat16)
    scores = jnp.einsum(
        "iphe,iqhe->ihpq", query, keyed, preferred_element_type=jnp.float32
    ) * HEAD_DIM ** (-0.5)
    attn_probs = softmax_rows(scores)
    mixed_heads = jnp.einsum(
        "ihpq,iqhe->iphe",
        attn_probs.astype(jnp.bfloat16),
        valued,
        preferred_element_type=jnp.float32,
    )
    mixed_heads = mixed_heads.reshape(images, tokens_all, heads_local * HEAD_DIM).astype(
        jnp.bfloat16
    )
    attended = collect_rows(
        jnp.einsum("ipe,ed->ipd", mixed_heads, out_weight, preferred_element_type=jnp.float32)
    )
    middle = stream + gate_one * attended
    normed_two = norm_modulate(middle, shift_two, scale_two).astype(jnp.bfloat16)
    spread_two = spread_rows(normed_two)
    gate_up = jnp.einsum(
        "ipd,kdf->kipf", spread_two, gate_up_weight, preferred_element_type=jnp.float32
    )
    hidden = gating(gate_up[0], gate_up[1]).astype(jnp.bfloat16)
    feedfwd = collect_rows(
        jnp.einsum("ipf,fd->ipd", hidden, down_weight, preferred_element_type=jnp.float32)
    )
    result = middle + gate_two * feedfwd
    saved = (
        stream,
        modulation,
        spread_one,
        projected,
        query,
        keyed,
        valued,
        attn_probs,
        mixed_heads,
        attended,
        middle,
        spread_two,
        gate_up,
        hidden,
        feedfwd,
    )
    return (result, saved)


def block_backward(saved, grad_result, weights, cosine, sine_table):
    mod_weight, qkv_weight, out_weight, gate_up_weight, down_weight, query_gain, key_gain = weights
    (
        stream,
        modulation,
        spread_one,
        projected,
        query,
        keyed,
        valued,
        attn_probs,
        mixed_heads,
        attended,
        middle,
        spread_two,
        gate_up,
        hidden,
        feedfwd,
    ) = saved
    shift_one, scale_one, gate_one, shift_two, scale_two, gate_two = split_modulation(modulation)
    heads_local = query_gain.shape[0] // HEAD_DIM
    gain_query = query_gain.astype(jnp.float32).reshape(heads_local, HEAD_DIM)
    gain_key = key_gain.astype(jnp.float32).reshape(heads_local, HEAD_DIM)
    images = spread_one.shape[0]
    tokens_all = spread_one.shape[1]
    d_gate_two = jnp.sum(grad_result * feedfwd, axis=1)
    grad_ffn = spread_grads((gate_two * grad_result).astype(jnp.bfloat16))
    grad_hidden = jnp.einsum(
        "ipd,fd->ipf", grad_ffn, down_weight, preferred_element_type=jnp.float32
    )
    grad_down = jnp.einsum("ipf,ipd->fd", hidden, grad_ffn, preferred_element_type=jnp.float32)
    unused, pull_gate = jax.vjp(gating, gate_up[0], gate_up[1])
    grad_gate, grad_up = pull_gate(grad_hidden)
    grad_both = jnp.stack([grad_gate, grad_up]).astype(jnp.bfloat16)
    grad_gate_up = jnp.einsum(
        "ipd,kipf->kdf", spread_two, grad_both, preferred_element_type=jnp.float32
    )
    grad_norm_two = collect_grads(
        jnp.einsum("kipf,kdf->ipd", grad_both, gate_up_weight, preferred_element_type=jnp.float32)
    )
    unused, pull_two = jax.vjp(norm_modulate, middle, shift_two, scale_two)
    grad_middle, grad_shift_two, grad_scale_two = pull_two(grad_norm_two)
    grad_middle = grad_result + grad_middle
    d_gate_one = jnp.sum(grad_middle * attended, axis=1)
    grad_attn = spread_grads((gate_one * grad_middle).astype(jnp.bfloat16))
    grad_mixed = jnp.einsum(
        "ipd,ed->ipe", grad_attn, out_weight, preferred_element_type=jnp.float32
    ).astype(jnp.bfloat16)
    grad_mixed = grad_mixed.reshape(images, tokens_all, heads_local, HEAD_DIM)
    grad_out_w = jnp.einsum(
        "ipe,ipd->ed", mixed_heads, grad_attn, preferred_element_type=jnp.float32
    )
    grad_probs = jnp.einsum(
        "iphe,iqhe->ihpq", grad_mixed, valued, preferred_element_type=jnp.float32
    )
    grad_value = jnp.einsum(
        "ihpq,iphe->iqhe",
        attn_probs.astype(jnp.bfloat16),
        grad_mixed,
        preferred_element_type=jnp.float32,
    ).astype(jnp.bfloat16)
    grad_scores = (
        attn_probs * (grad_probs - jnp.sum(attn_probs * grad_probs, axis=-1, keepdims=True))
    ).astype(jnp.bfloat16)
    grad_query = jnp.einsum(
        "ihpq,iqhe->iphe", grad_scores, keyed, preferred_element_type=jnp.float32
    ) * HEAD_DIM ** (-0.5)
    grad_key = jnp.einsum(
        "ihpq,iphe->iqhe", grad_scores, query, preferred_element_type=jnp.float32
    ) * HEAD_DIM ** (-0.5)

    def prepare_here(raw_values, gain_values):
        return head_prepare(raw_values, gain_values, cosine, sine_table)

    unused, pull_query = jax.vjp(prepare_here, projected[0], gain_query)
    grad_raw_query, grad_gain_query = pull_query(grad_query)
    unused, pull_key = jax.vjp(prepare_here, projected[1], gain_key)
    grad_raw_key, grad_gain_key = pull_key(grad_key)
    grad_raw = jnp.stack(
        [grad_raw_query.astype(jnp.bfloat16), grad_raw_key.astype(jnp.bfloat16), grad_value]
    )
    grad_raw = grad_raw.reshape(3, images, tokens_all, heads_local * HEAD_DIM)
    grad_qkv = jnp.einsum("ipd,kipe->kde", spread_one, grad_raw, preferred_element_type=jnp.float32)
    grad_norm_one = collect_grads(
        jnp.einsum("kipe,kde->ipd", grad_raw, qkv_weight, preferred_element_type=jnp.float32)
    )
    unused, pull_one = jax.vjp(norm_modulate, stream, shift_one, scale_one)
    grad_stream, grad_shift_one, grad_scale_one = pull_one(grad_norm_one)
    grad_stream = grad_middle + grad_stream
    grad_mod = jnp.stack(
        [
            grad_shift_one[:, 0],
            grad_scale_one[:, 0],
            d_gate_one,
            grad_shift_two[:, 0],
            grad_scale_two[:, 0],
            d_gate_two,
        ],
        axis=1,
    )
    weight_terms = (
        grad_qkv,
        grad_out_w,
        grad_gate_up,
        grad_down,
        grad_gain_query.reshape(-1),
        grad_gain_key.reshape(-1),
    )
    return (grad_stream, grad_mod, weight_terms)


def per_device(
    tokens,
    velocity_grad,
    bins,
    labels,
    places,
    class_table,
    mod_weight,
    qkv_weight,
    out_weight,
    gate_up_weight,
    down_weight,
    q_gain,
    k_gain,
):
    micro_count = tokens.shape[0]
    section_idx = lax.axis_index("section")
    leading = section_idx == 0
    weights = (
        mod_weight[0],
        qkv_weight[0],
        out_weight[0],
        gate_up_weight[0],
        down_weight[0],
        q_gain[0],
        k_gain[0],
    )
    empty_rows = jnp.zeros(tokens.shape[1:], jnp.bfloat16)
    received = empty_rows
    kept_inputs = []
    produced = []
    square_sums = jnp.zeros((3,), jnp.float32)
    for forward_step in range(micro_count + 1):
        offset = forward_step - section_idx
        is_valid = (offset >= 0) & (offset < micro_count)
        micro_index = jnp.clip(offset, 0, micro_count - 1)
        own_rows = tokens[min(forward_step, micro_count - 1)]
        block_in = jnp.where(leading, own_rows, received)
        stream = block_in.astype(jnp.float32)
        cond_vec, one_hot = condition(bins, labels, class_table, micro_index)
        place_row = lax.dynamic_index_in_dim(places, micro_index, 0, keepdims=False)
        cosine, sine_table = rope_tables(place_row)
        modulation = modulation_of(jax.nn.silu(cond_vec).astype(jnp.bfloat16), weights[0])
        result, saved = block_forward(stream, modulation, weights, cosine, sine_table)
        middle = saved[10]
        partial_squares = jnp.stack(
            [jnp.sum(stream * stream), jnp.sum(middle * middle), jnp.sum(result * result)]
        )
        square_sums = square_sums + jnp.where(is_valid, partial_squares, 0.0)
        result_low = result.astype(jnp.bfloat16)
        produced.append(result_low)
        kept_inputs.append(block_in)
        if forward_step < micro_count:
            received = from_behind(result_low, "section", 1)
    mod_weight_wide = weights[0].astype(jnp.float32)
    grad_totals = tuple((jnp.zeros(weight_item.shape, jnp.float32) for weight_item in weights[1:]))
    mod_total = jnp.zeros(weights[0].shape, jnp.float32)
    class_total = jnp.zeros(class_table.shape, jnp.float32)
    sent_back = empty_rows
    stream_grads = []
    for back_step in range(micro_count + 1):
        forward_step = micro_count - back_step
        offset = forward_step - section_idx
        is_valid = (offset >= 0) & (offset < micro_count)
        micro_index = jnp.clip(offset, 0, micro_count - 1)
        cot_rows = velocity_grad[max(micro_count - 1 - back_step, 0)]
        grad_result = jnp.where(leading, sent_back, cot_rows).astype(jnp.float32)
        cond_vec, one_hot = condition(bins, labels, class_table, micro_index)
        place_row = lax.dynamic_index_in_dim(places, micro_index, 0, keepdims=False)
        cosine, sine_table = rope_tables(place_row)
        silu_low = jax.nn.silu(cond_vec).astype(jnp.bfloat16)
        modulation = modulation_of(silu_low, weights[0])
        unused, saved = block_forward(
            kept_inputs[forward_step].astype(jnp.float32), modulation, weights, cosine, sine_table
        )
        grad_stream, grad_mod, weight_terms = block_backward(
            saved, grad_result, weights, cosine, sine_table
        )
        grad_mod_local = lax.psum_scatter(
            grad_mod.astype(jnp.bfloat16), "tensor", scatter_dimension=2, tiled=True
        ).astype(jnp.float32)
        mod_term = jnp.einsum(
            "id,ijf->djf",
            silu_low.astype(jnp.float32),
            grad_mod_local,
            precision=lax.Precision.HIGHEST,
        )
        grad_silu = jnp.einsum(
            "ijf,djf->id", grad_mod_local, mod_weight_wide, precision=lax.Precision.HIGHEST
        )
        unused, pull_silu = jax.vjp(jax.nn.silu, cond_vec)
        grad_cond = pull_silu(grad_silu)[0]
        grad_totals = jax.tree.map(
            lambda running, fresh_term: running + jnp.where(is_valid, fresh_term, 0.0),
            grad_totals,
            weight_terms,
        )
        mod_total = mod_total + jnp.where(is_valid, mod_term, 0.0)
        class_term = jnp.dot(one_hot.T, grad_cond, precision=lax.Precision.HIGHEST)
        class_total = class_total + jnp.where(is_valid, class_term, 0.0)
        stream_grads.append(grad_stream)
        if back_step < micro_count:
            sent_back = from_behind(grad_stream.astype(jnp.bfloat16), "section", -1)
    summed = (
        lax.psum(mod_total.astype(jnp.bfloat16), "dp").astype(jnp.float32),
        lax.psum(grad_totals[0].astype(jnp.bfloat16), "dp").astype(jnp.float32),
        lax.psum(grad_totals[1].astype(jnp.bfloat16), "dp").astype(jnp.float32),
        lax.psum(grad_totals[2].astype(jnp.bfloat16), "dp").astype(jnp.float32),
        lax.psum(grad_totals[3].astype(jnp.bfloat16), "dp").astype(jnp.float32),
        lax.psum(grad_totals[4].astype(jnp.bfloat16), "dp").astype(jnp.float32),
        lax.psum(grad_totals[5].astype(jnp.bfloat16), "dp").astype(jnp.float32),
    )
    class_grad = lax.psum(class_total, ("section", "dp", "tensor"))
    square_totals = lax.psum(square_sums, ("dp", "tensor"))
    element_count = (
        micro_count
        * tokens.shape[1]
        * tokens.shape[2]
        * tokens.shape[3]
        * lax.axis_size("dp")
        * lax.axis_size("tensor")
    )
    stats = jnp.sqrt(square_totals / element_count)[None, :]
    block_outputs = jnp.stack(
        [jnp.where(leading, produced[slot], produced[slot + 1]) for slot in range(micro_count)]
    )[None]
    input_grads = jnp.stack(
        [
            jnp.where(
                leading, stream_grads[micro_count - slot], stream_grads[micro_count - 1 - slot]
            )
            for slot in range(micro_count)
        ]
    )[None]
    return (
        block_outputs,
        input_grads,
        summed[0][None],
        summed[1][None],
        summed[2][None],
        summed[3][None],
        summed[4][None],
        summed[5][None],
        summed[6][None],
        class_grad,
        stats,
    )


def solution(mesh):
    return jax.shard_map(
        per_device,
        mesh=mesh,
        in_specs=(
            P(None, "dp", "tensor", None),
            P(None, "dp", "tensor", None),
            P(None, "dp"),
            P(None, "dp"),
            P(None, "dp", None),
            P(),
            P("section", None, None, "tensor"),
            P("section", None, None, "tensor"),
            P("section", "tensor", None),
            P("section", None, None, "tensor"),
            P("section", "tensor", None),
            P("section", "tensor"),
            P("section", "tensor"),
        ),
        out_specs=(
            P("section", None, "dp", "tensor", None),
            P("section", None, "dp", "tensor", None),
            P("section", None, None, "tensor"),
            P("section", None, None, "tensor"),
            P("section", "tensor", None),
            P("section", None, None, "tensor"),
            P("section", "tensor", None),
            P("section", "tensor"),
            P("section", "tensor"),
            P(),
            P("section", None),
        ),
        check_vma=False,
    )
```

profile of v0, /device:TPU:0, one launch (start us, length us, event | category | flops | bytes accessed | tf_op | source)
XLA Modules:
  0.0 2111.2 jit_solution(5880352822062797367)
XLA Ops:
  93.6 18.7 reduce-scatter.36.cloned.1.call-done
  116.8 17.6 all-gather.23.cloned.1.call-done
  153.3 14.1 all_gather.93
  198.1 15.0 all-gather.25.cloned.1.call-done
  239.3 18.7 reduce-scatter.40.cloned.1.call-done
  262.3 17.6 all-gather.27.cloned.1.call-done
  298.3 14.0 all_gather.96
  340.2 18.6 all-gather.29.cloned.1.call-done
  385.0 18.7 reduce-scatter.44.cloned.1.call-done
  408.3 17.4 all-gather.31.cloned.1.call-done
  489.8 14.3 all-gather.33.cloned.1.call-done
  530.3 18.7 reduce-scatter.48.cloned.1.call-done
  553.5 17.6 all-gather.35.cloned.1.call-done
  589.4 13.9 all_gather.102
  631.4 18.6 all-gather.37.cloned.1.call-done
  676.1 18.7 reduce-scatter.52.cloned.1.call-done
  722.0 14.4 all-gather.41.cloned.1.call-done
  745.2 25.8 %reduce-scatter.56.cloned.1.call-done = bf16[2,64,1152]{2,1,0:T(8,128)(2,1)} async-done(((bf16[2,256,1152]{2,1,0:T(8,128)(2,1)}), bf16[2,64,1152]{2,1,0:T(8,128)(2,1)}) %reduce-scatter.56.cloned.1.call-update) | async-done | bytes 294928 | tf_op jit(solution)/shard_map/reduce_scatter | solution.py:89
  822.5 28.9 %reduce-scatter.58.cloned.1.call-done = bf16[2,64,1152]{2,1,0:T(8,128)(2,1)} async-done(((bf16[2,256,1152]{2,1,0:T(8,128)(2,1)}), bf16[2,64,1152]{2,1,0:T(8,128)(2,1)}) %reduce-scatter.58.cloned.1.call-update) | async-done | bytes 294928 | tf_op jit(solution)/shard_map/reduce_scatter | solution.py:89
  869.7 16.5 all-gather.45.cloned.1.call-done
  895.0 25.8 %reduce-scatter.60.cloned.1.call-done = bf16[2,64,1152]{2,1,0:T(8,128)(2,1)} async-done(((bf16[2,256,1152]{2,1,0:T(8,128)(2,1)}), bf16[2,64,1152]{2,1,0:T(8,128)(2,1)}) %reduce-scatter.60.cloned.1.call-update) | async-done | bytes 294928 | tf_op jit(solution)/shard_map/reduce_scatter | solution.py:89
  926.4 17.6 all-gather.47.cloned.1.call-done
  962.9 25.8 %reduce-scatter.62.cloned.1.call-done = bf16[2,64,1152]{2,1,0:T(8,128)(2,1)} async-done(((bf16[2,256,1152]{2,1,0:T(8,128)(2,1)}), bf16[2,64,1152]{2,1,0:T(8,128)(2,1)}) %reduce-scatter.62.cloned.1.call-update) | async-done | bytes 294928 | tf_op jit(solution)/shard_map/reduce_scatter | solution.py:89
  1007.4 16.3 all-gather.49.cloned.1.call-done
  1032.5 25.8 %reduce-scatter.64.cloned.1.call-done = bf16[2,64,1152]{2,1,0:T(8,128)(2,1)} async-done(((bf16[2,256,1152]{2,1,0:T(8,128)(2,1)}), bf16[2,64,1152]{2,1,0:T(8,128)(2,1)}) %reduce-scatter.64.cloned.1.call-update) | async-done | bytes 294928 | tf_op jit(solution)/shard_map/reduce_scatter | solution.py:89
  1063.9 17.6 all-gather.51.cloned.1.call-done
  1110.1 16.1 reduce-scatter.66.cloned.1.call-done
  1457.8 15.8 fusion.40
  1504.9 17.2 reduce-scatter.84.cloned.1.call-done
  1592.2 32.6 %psum.71 = f32[3]{0:T(128)} all-reduce(f32[3]{0:T(128)} %fusion.646), channel_id=1, replica_groups=mesh['section'=2,'dp'=4,'tensor'=4] {'dp','tensor'}, use_global_device_ids=true, to_apply=%region_143.144 | all-reduce | flops 3 | bytes 24 | tf_op jit(solution)/shard_map/psum | solution.py:407
  1630.2 320.3 %all-reduce.27.cloned.1.call-done = (bf16[1,2,1152,768]{2,3,1,0:T(8,128)(2,1)}, bf16[1,1152,6,288]{1,3,2,0:T(8,128)(2,1)}, bf16[1,3,1152,288]{2,3,1,0:T(8,128)(2...) async-done(((bf16[1,2,1152,768]{2,3,1,0:T(8,128)(2,1)}, bf16[1,1152,6,288]{1,3,2,0:T(8,128)(2,1)}, bf16[1,3,1152,288]{2,3,1,0:T(8,128)(2,1)}, ...) | async-done | bytes 11943952 | tf_op jit(solution)/shard_map/psum | solution.py:401
  1969.4 130.0 %all-reduce.25.cloned.1.call-done = f32[1000,1152]{1,0:T(8,128)} async-done(((f32[1000,1152]{1,0:T(8,128)}), f32[1000,1152]{1,0:T(8,128)}) %all-reduce.25.cloned.1.call-update) | async-done | bytes 4608016 | tf_op jit(solution)/shard_map/psum | solution.py:406
  (1440 shorter events, 1073.3 us)
Async XLA Ops:
  7.2 60.3 %all-gather.21.cloned.1.call-start = ((), (), s32[]{:S(2)}) async-start(), calls=%async_computation.25 | async-start | bytes 1474560 | tf_op jit(solution)/shard_map/all_gather | solution.py:75
  49.0 63.3 %reduce-scatter.36.cloned.1.call-start = ((), (), s32[]{:S(2)}) async-start(), calls=%async_computation.26 | async-start | bytes 1474560 | tf_op jit(solution)/shard_map/reduce_scatter | solution.py:79
  116.8 62.8 %reduce-scatter.38.cloned.1.call-start = ((), (), s32[]{:S(2)}) async-start(), calls=%async_computation.28 | async-start | bytes 1474560 | tf_op jit(solution)/shard_map/reduce_scatter | solution.py:79
  142.2 70.9 %all-gather.25.cloned.1.call-start = ((), (), s32[]{:S(2)}) async-start(), calls=%async_computation.29 | async-start | bytes 1474560 | tf_op jit(solution)/shard_map/all_gather | solution.py:75
  194.2 63.7 %reduce-scatter.40.cloned.1.call-start = ((), (), s32[]{:S(2)}) async-start(), calls=%async_computation.30 | async-start | bytes 1474560 | tf_op jit(solution)/shard_map/reduce_scatter | solution.py:79
  262.3 62.2 %reduce-scatter.42.cloned.1.call-start = ((), (), s32[]{:S(2)}) async-start(), calls=%async_computation.32 | async-start | bytes 1474560 | tf_op jit(solution)/shard_map/reduce_scatter | solution.py:79
  287.7 71.1 %all-gather.29.cloned.1.call-start = ((), (), s32[]{:S(2)}) async-start(), calls=%async_computation.33 | async-start | bytes 1474560 | tf_op jit(solution)/shard_map/all_gather | solution.py:75
  340.2 63.5 %reduce-scatter.44.cloned.1.call-start = ((), (), s32[]{:S(2)}) async-start(), calls=%async_computation.34 | async-start | bytes 1474560 | tf_op jit(solution)/shard_map/reduce_scatter | solution.py:79
  408.0 61.8 %reduce-scatter.46.cloned.1.call-start = ((), (), s32[]{:S(2)}) async-start(), calls=%async_computation.36 | async-start | bytes 1474560 | tf_op jit(solution)/shard_map/reduce_scatter | solution.py:79
  433.4 70.8 %all-gather.33.cloned.1.call-start = ((), (), s32[]{:S(2)}) async-start(), calls=%async_computation.37 | async-start | bytes 1474560 | tf_op jit(solution)/shard_map/all_gather | solution.py:75
  485.5 63.5 %reduce-scatter.48.cloned.1.call-start = ((), (), s32[]{:S(2)}) async-start(), calls=%async_computation.38 | async-start | bytes 1474560 | tf_op jit(solution)/shard_map/reduce_scatter | solution.py:79
  553.4 62.2 %reduce-scatter.50.cloned.1.call-start = ((), (), s32[]{:S(2)}) async-start(), calls=%async_computation.40 | async-start | bytes 1474560 | tf_op jit(solution)/shard_map/reduce_scatter | solution.py:79
  578.8 71.2 %all-gather.37.cloned.1.call-start = ((), (), s32[]{:S(2)}) async-start(), calls=%async_computation.41 | async-start | bytes 1474560 | tf_op jit(solution)/shard_map/all_gather | solution.py:75
  631.3 63.5 %reduce-scatter.52.cloned.1.call-start = ((), (), s32[]{:S(2)}) async-start(), calls=%async_computation.42 | async-start | bytes 1474560 | tf_op jit(solution)/shard_map/reduce_scatter | solution.py:79
  703.2 67.9 %reduce-scatter.56.cloned.1.call-start = ((), (), s32[]{:S(2)}) async-start(), calls=%async_computation.46 | async-start | bytes 1474560 | tf_op jit(solution)/shard_map/reduce_scatter | solution.py:89
  785.9 65.5 %reduce-scatter.58.cloned.1.call-start = ((), (), s32[]{:S(2)}) async-start(), calls=%async_computation.48 | async-start | bytes 1474560 | tf_op jit(solution)/shard_map/reduce_scatter | solution.py:89
  812.5 73.7 %all-gather.45.cloned.1.call-start = ((), (), s32[]{:S(2)}) async-start(), calls=%async_computation.49 | async-start | bytes 1474560 | tf_op jit(solution)/shard_map/all_gather | solution.py:85
  926.3 62.4 %reduce-scatter.62.cloned.1.call-start = ((), (), s32[]{:S(2)}) async-start(), calls=%async_computation.52 | async-start | bytes 1474560 | tf_op jit(solution)/shard_map/reduce_scatter | solution.py:89
  962.9 60.8 %all-gather.49.cloned.1.call-start = ((), (), s32[]{:S(2)}) async-start(), calls=%async_computation.53 | async-start | bytes 1474560 | tf_op jit(solution)/shard_map/all_gather | solution.py:85
  1007.0 51.3 %reduce-scatter.64.cloned.1.call-start = ((), (), s32[]{:S(2)}) async-start(), calls=%async_computation.54 | async-start | bytes 1474560 | tf_op jit(solution)/shard_map/reduce_scatter | solution.py:89
  1063.8 62.4 %reduce-scatter.66.cloned.1.call-start = ((), (), s32[]{:S(2)}) async-start(), calls=%async_computation.56 | async-start | bytes 1474560 | tf_op jit(solution)/shard_map/reduce_scatter | solution.py:89
  1100.4 63.1 %reduce-scatter.76.cloned.1.call-start = ((), (), s32[]{:S(2)}) async-start(), calls=%async_computation.66 | async-start | bytes 368640
  1145.0 72.8 %reduce-scatter.68.cloned.1.call-start = ((), (), s32[]{:S(2)}) async-start(), calls=%async_computation.58 | async-start | bytes 1474560 | tf_op jit(solution)/shard_map/reduce_scatter | solution.py:89
  1206.7 53.2 %all-gather.55.cloned.1.call-start = ((), (), s32[]{:S(2)}) async-start(), calls=%async_computation.59 | async-start | bytes 1474560 | tf_op jit(solution)/shard_map/all_gather | solution.py:85
  1223.2 81.7 %reduce-scatter.70.cloned.1.call-start = ((), (), s32[]{:S(2)}) async-start(), calls=%async_computation.60 | async-start | bytes 1474560 | tf_op jit(solution)/shard_map/reduce_scatter | solution.py:89
  1279.0 62.9 %reduce-scatter.80.cloned.1.call-start = ((), (), s32[]{:S(2)}) async-start(), calls=%async_computation.68 | async-start | bytes 368640
  1325.7 70.6 %reduce-scatter.72.cloned.1.call-start = ((), (), s32[]{:S(2)}) async-start(), calls=%async_computation.62 | async-start | bytes 1474560 | tf_op jit(solution)/shard_map/reduce_scatter | solution.py:89
  1385.3 53.4 %all-gather.59.cloned.1.call-start = ((), (), s32[]{:S(2)}) async-start(), calls=%async_computation.63 | async-start | bytes 1474560 | tf_op jit(solution)/shard_map/all_gather | solution.py:85
  1402.1 82.3 %reduce-scatter.74.cloned.1.call-start = ((), (), s32[]{:S(2)}) async-start(), calls=%async_computation.64 | async-start | bytes 1474560 | tf_op jit(solution)/shard_map/reduce_scatter | solution.py:89
  1457.8 64.4 %reduce-scatter.84.cloned.1.call-start = ((), (), s32[]{:S(2)}) async-start(), calls=%async_computation.70 | async-start | bytes 368640
  1501.7 448.8 %all-reduce.27.cloned.1.call-start = ((), (), s32[]{:S(2)}) async-start(), calls=%async_computation.71 | async-start | bytes 23887872 | tf_op jit(solution)/shard_map/psum | solution.py:401
  1538.8 560.6 %all-reduce.25.cloned.1.call-start = ((), (), s32[]{:S(2)}) async-start(), calls=%async_computation.65 | async-start | bytes 9216000 | tf_op jit(solution)/shard_map/psum | solution.py:406
  (423 other events, 2388.5 us)
Sparse Core Ops, SparseCore 0:
  49.2 18.3 all-gather.20
  86.5 25.7 reduce-scatter.35
  142.3 28.3 reduce-scatter.37
  194.3 18.6 all-gather.24
  232.2 25.7 reduce-scatter.39
  287.8 27.9 reduce-scatter.41
  340.3 18.4 all-gather.28
  377.9 25.7 reduce-scatter.43
  433.5 27.8 reduce-scatter.45
  485.7 18.4 all-gather.32
  523.3 25.7 reduce-scatter.47
  578.9 27.9 reduce-scatter.49
  631.4 18.4 all-gather.36
  669.1 25.7 reduce-scatter.51
  745.3 25.7 reduce-scatter.55
  796.7 25.7 reduce-scatter.53
  825.7 25.7 reduce-scatter.57
  895.1 25.7 reduce-scatter.59
  963.0 25.7 reduce-scatter.61
  1032.6 25.7 reduce-scatter.63
  1100.5 25.7 reduce-scatter.65
  1141.3 22.1 reduce-scatter.75
  1192.0 25.7 reduce-scatter.67
  1220.1 20.2 reduce-scatter.77
  1279.2 25.7 reduce-scatter.69
  1319.8 22.1 reduce-scatter.79
  1370.6 25.7 reduce-scatter.71
  1398.8 20.2 reduce-scatter.81
  1457.9 25.7 reduce-scatter.73
  1501.8 20.2 reduce-scatter.83
  1538.9 411.5 all-reduce.26
  1956.6 142.7 all-reduce.24
  (15 shorter events, 259.2 us)
where the time goes:
time: 2120 us; the launch traced here: 2110 us
  waiting for transfers between devices  1090 us (51%)
  matrix products  344 us (16%)
  local copies, waits for them, and re-layouts  310 us (15%)
  other arithmetic  210 us (10%)
  blocking collectives  113 us (5%)
  starting transfers between devices  24.5 us (1%)
    psum x1, waiting for transfers between devices, per_device(): lax.psum(grad_totals[2].astype(jnp.bfloat16), 'dp').astype(jnp.float32)  320 us
    unnamed x857, local copies, waits for them, and re-layouts  181 us
    reduce_scatter x10, waiting for transfers between devices, collect_grads(): lax.psum_scatter(partial_rows.astype(jnp.bfloat16), 'tensor', scatter_dim...  179 us
    all_gather x10, waiting for transfers between devices, spread_rows(): return lax.all_gather(activation, 'tensor', axis=1, tiled=True)  161 us
    psum x1, waiting for transfers between devices, per_device(): class_grad = lax.psum(class_total, ('section', 'dp', 'tensor'))  130 us
    all_gather x10, waiting for transfers between devices, spread_grads(): return lax.all_gather(gradient, 'tensor', axis=1, tiled=True)  117 us
    reduce_scatter x10, waiting for transfers between devices, collect_rows(): lax.psum_scatter(partial_rows.astype(jnp.bfloat16), 'tensor', scatter_dim...  103 us
    all_gather x5, blocking collectives, modulation_of(): return lax.all_gather(columns, 'tensor', axis=2, tiled=True)  68 us
  transfers between devices with their start and end apart: 55, of which 50 were waited for; matrix products, arithmetic and copies ran while one was open for 22% of the time, Pallas kernels for 0%

commit v1 on v0

v1 whole, which is shorter than its diff:
```python
import functools
import math

import jax
import jax.numpy as jnp
import numpy as np
from jax import lax
from jax.experimental import pallas as pl
from jax.experimental.pallas import tpu as pltpu
from jax.sharding import PartitionSpec as P

MESH = pl.DeviceIdType.MESH
HEAD_DIM = 72
LANES = 128
NBINS = 1000
GRID = 16
EPS = 1e-06
BF = jnp.bfloat16
F32 = jnp.float32
SCALE = HEAD_DIM**-0.5


def lane_of():
    quarter = HEAD_DIM // 4
    lanes = np.zeros((HEAD_DIM,), np.int64)
    for half in range(2):
        for part in range(2):
            for i in range(quarter):
                lanes[half * 2 * quarter + part * quarter + i] = part * 64 + half * quarter + i
    return lanes


def head_select(heads):
    select = np.zeros((heads * HEAD_DIM, heads * LANES), np.float32)
    lanes = lane_of()
    for h in range(heads):
        for f in range(HEAD_DIM):
            select[h * HEAD_DIM + f, h * LANES + lanes[f]] = 1.0
    return select


def angle_table():
    quarter = HEAD_DIM // 4
    frequency = (10000.0 ** (-np.arange(quarter, dtype=np.float32) / np.float32(quarter))).astype(np.float32)
    lanes = lane_of().reshape(2, 2, quarter)
    table = np.zeros((2 * GRID, 2 * LANES), np.float32)
    for place in range(GRID):
        angle = np.float32(place) * frequency
        for half in range(2):
            for part in range(2):
                sign = -1.0 if part == 0 else 1.0
                table[half * GRID + place, lanes[half, part]] = np.cos(angle)
                table[half * GRID + place, LANES + lanes[half, part]] = sign * np.sin(angle)
    return table


def dot(a, b):
    return lax.dot_general(a, b, (((1,), (0,)), ((), ())), preferred_element_type=F32)


def dot_nt(a, b):
    return lax.dot_general(a, b, (((1,), (1,)), ((), ())), preferred_element_type=F32)


def dot_tn(a, b):
    return lax.dot_general(a, b, (((0,), (0,)), ((), ())), preferred_element_type=F32)


def chunks_of(size, width):
    return [(at, min(width, size - at)) for at in range(0, size, width)]


def main_kernel(
    images,
    heads,
    tok,
    vel,
    mod,
    cosine,
    sine,
    wqkv,
    wout,
    wgu,
    wdn,
    gains,
    zout,
    dxout,
    dmod,
    gacc,
    sacc,
    a1_hbm,
    a2_hbm,
    dffn_hbm,
    dattn_hbm,
    hid_hbm,
    mix_hbm,
    dgu_hbm,
    dqkv_hbm,
    xin,
    din,
    a1f,
    a2f,
    dffn,
    dattn,
    x1s,
    attns,
    ffns,
    keep,
    send_a,
    recv_a,
    send_y,
    recv_y,
    dx1s,
    mix_st,
    hid_st,
    dgu_st,
    dqkv_st,
    ag_sems,
    rs_sems,
    zx_sems,
    out_sems,
    in_sems,
):
    rows = tok.shape[1]
    width = tok.shape[2]
    hidden = wdn.shape[0]
    wide = chunks_of(width, 512)
    section = lax.axis_index("section")
    me = lax.axis_index("tensor")
    sib = me + 1 - 2 * lax.rem(me, 2)
    across = lax.rem(me + 2, 4)
    other = 1 - section
    enc = section == 0
    dec = section == 1

    load_x = pltpu.make_async_copy(tok, xin, in_sems.at[0])
    load_d = pltpu.make_async_copy(vel, din, in_sems.at[1])

    @pl.when(enc)
    def _():
        load_x.start()

    @pl.when(dec)
    def _():
        load_d.start()

    barrier = pltpu.get_barrier_semaphore()
    pl.semaphore_signal(barrier, inc=1, device_id={"tensor": sib}, device_id_type=MESH)
    pl.semaphore_signal(barrier, inc=1, device_id={"tensor": across}, device_id_type=MESH)
    pl.semaphore_signal(barrier, inc=1, device_id={"section": other}, device_id_type=MESH)

    gacc[...] = jnp.zeros_like(gacc)
    sacc[...] = jnp.zeros_like(sacc)
    dmod[...] = jnp.zeros_like(dmod)

    @pl.when(enc)
    def _():
        load_x.wait()

    @pl.when(dec)
    def _():
        load_d.wait()

    pl.semaphore_wait(barrier, 3)

    def remote(src, dst, send_sem, recv_sem, where):
        return pltpu.make_async_remote_copy(
            src_ref=src, dst_ref=dst, send_sem=send_sem, recv_sem=recv_sem, device_id=where, device_id_type=MESH
        )

    def gather(which, buf, n):
        over_y = remote(
            buf.at[n, pl.ds(0, rows)],
            buf.at[n, pl.ds(rows, rows)],
            ag_sems.at[which, 0, n],
            ag_sems.at[which, 1, n],
            {"tensor": across},
        )
        to_sib = remote(
            buf.at[n, pl.ds(0, rows)],
            buf.at[n, pl.ds(2 * rows, rows)],
            ag_sems.at[which, 2, n],
            ag_sems.at[which, 3, n],
            {"tensor": sib},
        )
        relay = remote(
            buf.at[n, pl.ds(rows, rows)],
            buf.at[n, pl.ds(3 * rows, rows)],
            ag_sems.at[which, 4, n],
            ag_sems.at[which, 5, n],
            {"tensor": sib},
        )
        return over_y, to_sib, relay

    def gather_start(which, buf, n):
        over_y, to_sib, relay = gather(which, buf, n)
        over_y.start()
        to_sib.start()

    def gather_relay(which, buf, n):
        over_y, to_sib, relay = gather(which, buf, n)
        over_y.wait_recv()
        relay.start()

    def gather_wait(which, buf, n):
        over_y, to_sib, relay = gather(which, buf, n)
        to_sib.wait_recv()
        relay.wait_recv()

    def gather_drain(which, buf, n):
        over_y, to_sib, relay = gather(which, buf, n)
        over_y.wait_send()
        to_sib.wait_send()
        relay.wait_send()

    def scatter(which, n):
        kind, slot = which % 2, lax.rem(n, 2)
        to_sib = remote(
            send_a.at[kind],
            recv_a.at[kind, slot],
            rs_sems.at[which, 0, n],
            rs_sems.at[which, 1, n],
            {"tensor": sib},
        )
        over_y = remote(
            send_y.at[kind],
            recv_y.at[kind, slot],
            rs_sems.at[which, 2, n],
            rs_sems.at[which, 3, n],
            {"tensor": across},
        )
        return kind, slot, to_sib, over_y

    def scatter_put(which, at, size, values):
        kind = which % 2
        keep[kind, :, pl.ds(at, size)] = values[0 : 2 * rows]
        send_a[kind, :, pl.ds(at, size)] = values[2 * rows : 4 * rows].astype(BF)

    def scatter_start(which, n):
        kind, slot, to_sib, over_y = scatter(which, n)
        to_sib.start()

    def scatter_middle(which, n):
        kind, slot, to_sib, over_y = scatter(which, n)
        to_sib.wait()
        send_y[kind] = (keep[kind, rows : 2 * rows] + recv_a[kind, slot, rows : 2 * rows].astype(F32)).astype(BF)
        over_y.start()

    def scatter_end(which, n):
        kind, slot, to_sib, over_y = scatter(which, n)
        over_y.wait()
        return (
            keep[kind, 0:rows] + recv_a[kind, slot, 0:rows].astype(F32) + recv_y[kind, slot].astype(F32)
        )

    def z_copy(n):
        return remote(zout.at[n], xin.at[n], zx_sems.at[0, n], zx_sems.at[1, n], {"section": other})

    def dz_copy(n):
        return remote(xin.at[n], din.at[n], zx_sems.at[2, n], zx_sems.at[3, n], {"section": other})

    def mod_row(n, row):
        return mod[n, pl.ds(row, 1), :]

    def inverse_rms(values):
        return lax.rsqrt(jnp.mean(values * values, axis=-1, keepdims=True) + EPS)

    def column_sum(values):
        return jnp.sum(values, axis=0, keepdims=True)

    def modulated(values, shift, scale):
        return (values * inverse_rms(values)) * (1.0 + scale) + shift

    def norm_back(values, grad, scale):
        inv = inverse_rms(values)
        normed = values * inv
        d_normed = grad * (1.0 + scale)
        d_values = inv * (d_normed - normed * jnp.mean(d_normed * normed, axis=-1, keepdims=True))
        return d_values, column_sum(grad), column_sum(grad * normed)

    def head_norm(raw):
        inv = lax.rsqrt(jnp.sum(raw * raw, axis=-1, keepdims=True) * (1.0 / HEAD_DIM) + EPS)
        return inv, raw * inv

    def turn(values, c, s):
        return values * c + pltpu.roll(values, 64, 1) * s

    def turn_back(values, c, s):
        return values * c - pltpu.roll(values, 64, 1) * s

    def softmax(scores):
        powered = jnp.exp(scores - jnp.max(scores, axis=-1, keepdims=True))
        return powered * (1.0 / jnp.sum(powered, axis=-1, keepdims=True))

    def out_copy(which, n):
        src, dst = (
            (a1f.at[n], a1_hbm.at[n]),
            (a2f.at[n], a2_hbm.at[n]),
            (dffn.at[n], dffn_hbm.at[n]),
            (dattn.at[n], dattn_hbm.at[n]),
            (hid_st, hid_hbm.at[n]),
            (mix_st, mix_hbm.at[n]),
            (dgu_st, dgu_hbm.at[n]),
            (dqkv_st, dqkv_hbm.at[n]),
        )[which]
        return pltpu.make_async_copy(src, dst, out_sems.at[which, n])

    def staged_ready(which, n):
        @pl.when(n > 0)
        def _():
            out_copy(which, n - 1).wait()

    def attn_in(n):
        @pl.when(dec)
        def _():
            z_copy(n).wait_recv()

        values = xin[n].astype(F32)
        sacc[0:1, :] += column_sum(values * values)
        a1f[n, 0:rows, :] = modulated(values, mod_row(n, 0), mod_row(n, 1)).astype(BF)
        gather_start(0, a1f, n)

    def attn_compute(n):
        gather_wait(0, a1f, n)
        staged_ready(5, n)
        a1 = a1f[n]
        c, s = cosine[n], sine[n]
        for pair in range(heads // 2):
            span = pl.ds(pair * 2 * LANES, 2 * LANES)
            q2 = dot(a1, wqkv[0, :, span])
            k2 = dot(a1, wqkv[1, :, span])
            v2 = dot(a1, wqkv[2, :, span]).astype(BF)
            for half in range(2):
                at = (pair * 2 + half) * LANES
                cut = slice(half * LANES, (half + 1) * LANES)
                q = turn(head_norm(q2[:, cut])[1] * gains[0:1, at : at + LANES], c, s).astype(BF)
                k = turn(head_norm(k2[:, cut])[1] * gains[1:2, at : at + LANES], c, s).astype(BF)
                probs = softmax(dot_nt(q, k) * SCALE).astype(BF)
                mix_st[:, at : at + LANES] = dot(probs, v2[:, cut]).astype(BF)
        mixed = mix_st[...]
        for at, size in wide:
            scatter_put(0, at, size, dot(mixed, wout[:, pl.ds(at, size)]))
        scatter_start(0, n)
        out_copy(5, n).start()
        out_copy(0, n).start()
        gather_drain(0, a1f, n)

    def ffn_in(n):
        attended = scatter_end(0, n)
        attns[n] = attended.astype(BF)
        values = xin[n].astype(F32) + mod_row(n, 2) * attended
        x1s[n] = values
        sacc[1:2, :] += column_sum(values * values)
        a2f[n, 0:rows, :] = modulated(values, mod_row(n, 3), mod_row(n, 4)).astype(BF)
        gather_start(1, a2f, n)

    def ffn_compute(n):
        gather_wait(1, a2f, n)
        a2 = a2f[n]
        for at, size in chunks_of(hidden, 256):
            span = pl.ds(at, size)
            gate_val = dot(a2, wgu[0, :, span])
            up_val = dot(a2, wgu[1, :, span])
            hid_st[:, span] = (gate_val * jax.nn.sigmoid(gate_val) * up_val).astype(BF)
        units = hid_st[...]
        for at, size in wide:
            scatter_put(1, at, size, dot(units, wdn[:, pl.ds(at, size)]))
        scatter_start(1, n)
        out_copy(1, n).start()
        gather_drain(1, a2f, n)

    def block_out(n):
        feedfwd = scatter_end(1, n)
        ffns[n] = feedfwd.astype(BF)
        values = x1s[n] + mod_row(n, 5) * feedfwd
        sacc[2:3, :] += column_sum(values * values)
        zout[n] = values.astype(BF)

        @pl.when(enc)
        def _():
            z_copy(n).start()

    def ffn_grad_in(n):
        @pl.when(enc)
        def _():
            dz_copy(n).wait_recv()

        grad = din[n].astype(F32)
        dffn[n, 0:rows, :] = (mod_row(n, 5) * grad).astype(BF)
        gather_start(2, dffn, n)
        dmod[n, 5:6, :] = column_sum(grad * ffns[n].astype(F32))

    def ffn_grad_compute(n):
        gather_wait(2, dffn, n)
        staged_ready(4, n)
        staged_ready(6, n)
        grad = dffn[n]
        a2 = a2f[n]
        for at, size in chunks_of(hidden, 256):
            span = pl.ds(at, size)
            gate_val = dot(a2, wgu[0, :, span])
            up_val = dot(a2, wgu[1, :, span])
            d_hidden = dot_nt(grad, wdn[span, :])
            sig = jax.nn.sigmoid(gate_val)
            act = gate_val * sig
            hid_st[:, span] = (act * up_val).astype(BF)
            dgu_st[:, span] = (d_hidden * up_val * (sig + act * (1.0 - sig))).astype(BF)
            dgu_st[:, pl.ds(hidden + at, size)] = (d_hidden * act).astype(BF)
        d_gate = dgu_st[:, 0:hidden]
        d_up = dgu_st[:, hidden : 2 * hidden]
        for at, size in wide:
            span = pl.ds(at, size)
            scatter_put(2, at, size, dot_nt(d_gate, wgu[0, span, :]) + dot_nt(d_up, wgu[1, span, :]))
        scatter_start(2, n)
        out_copy(4, n).start()
        out_copy(6, n).start()
        out_copy(2, n).start()
        gather_drain(2, dffn, n)

    def attn_grad_in(n):
        d_a2 = scatter_end(2, n)
        grad, d_shift, d_scale = norm_back(x1s[n], d_a2, mod_row(n, 4))
        grad = grad + din[n].astype(F32)
        dx1s[lax.rem(n, 2)] = grad
        dattn[n, 0:rows, :] = (mod_row(n, 2) * grad).astype(BF)
        gather_start(3, dattn, n)
        dmod[n, 2:3, :] = column_sum(grad * attns[n].astype(F32))
        dmod[n, 3:4, :] = d_shift
        dmod[n, 4:5, :] = d_scale

    def attn_grad_compute(n):
        gather_wait(3, dattn, n)
        staged_ready(7, n)
        grad = dattn[n]
        a1 = a1f[n]
        c, s = cosine[n], sine[n]
        lanes_all = heads * LANES
        for pair in range(heads // 2):
            span = pl.ds(pair * 2 * LANES, 2 * LANES)
            q2 = dot(a1, wqkv[0, :, span])
            k2 = dot(a1, wqkv[1, :, span])
            v2 = dot(a1, wqkv[2, :, span]).astype(BF)
            d_mix2 = dot_nt(grad, wout[span, :]).astype(BF)
            for half in range(2):
                at = (pair * 2 + half) * LANES
                cut = slice(half * LANES, (half + 1) * LANES)
                q_gain, k_gain = gains[0:1, at : at + LANES], gains[1:2, at : at + LANES]
                q_inv, q_norm = head_norm(q2[:, cut])
                k_inv, k_norm = head_norm(k2[:, cut])
                q = turn(q_norm * q_gain, c, s).astype(BF)
                k = turn(k_norm * k_gain, c, s).astype(BF)
                v, d_mix = v2[:, cut], d_mix2[:, cut]
                probs = softmax(dot_nt(q, k) * SCALE)
                d_probs = dot_nt(d_mix, v)
                d_v = dot_tn(probs.astype(BF), d_mix)
                d_scores = (probs * (d_probs - jnp.sum(probs * d_probs, axis=-1, keepdims=True))).astype(BF)
                d_q = turn_back(dot(d_scores, k) * SCALE, c, s)
                d_k = turn_back(dot_tn(d_scores, q) * SCALE, c, s)
                gacc[0:1, at : at + LANES] += column_sum(d_q * q_norm)
                gacc[1:2, at : at + LANES] += column_sum(d_k * k_norm)
                d_q = d_q * q_gain
                d_k = d_k * k_gain
                d_q = q_inv * (d_q - q_norm * (jnp.sum(d_q * q_norm, axis=-1, keepdims=True) * (1.0 / HEAD_DIM)))
                d_k = k_inv * (d_k - k_norm * (jnp.sum(d_k * k_norm, axis=-1, keepdims=True) * (1.0 / HEAD_DIM)))
                dqkv_st[:, at : at + LANES] = d_q.astype(BF)
                dqkv_st[:, lanes_all + at : lanes_all + at + LANES] = d_k.astype(BF)
                dqkv_st[:, 2 * lanes_all + at : 2 * lanes_all + at + LANES] = d_v.astype(BF)
        for at, size in wide:
            span = pl.ds(at, size)
            total = dot_nt(dqkv_st[:, 0:lanes_all], wqkv[0, span, :])
            total += dot_nt(dqkv_st[:, lanes_all : 2 * lanes_all], wqkv[1, span, :])
            total += dot_nt(dqkv_st[:, 2 * lanes_all : 3 * lanes_all], wqkv[2, span, :])
            scatter_put(3, at, size, total)
        scatter_start(3, n)
        out_copy(7, n).start()
        out_copy(3, n).start()
        gather_drain(3, dattn, n)

    def block_grad_out(n):
        d_a1 = scatter_end(3, n)
        grad, d_shift, d_scale = norm_back(xin[n].astype(F32), d_a1, mod_row(n, 1))
        grad = grad + dx1s[lax.rem(n, 2)]
        dxout[n] = grad
        dmod[n, 0:1, :] = d_shift
        dmod[n, 1:2, :] = d_scale

        @pl.when(dec)
        def _():
            xin[n] = grad.astype(BF)
            dz_copy(n).start()

    def stage(n, body):
        @pl.when((n >= 0) & (n < images))
        def _():
            body(n)

    def forward_step(step, carry):
        j = step - 1
        stage(j, attn_compute)
        stage(j - 1, lambda n: gather_relay(1, a2f, n))
        stage(j - 2, block_out)
        stage(j, lambda n: scatter_middle(0, n))
        stage(j + 1, attn_in)
        stage(j - 1, ffn_compute)
        stage(j + 1, lambda n: gather_relay(0, a1f, n))
        stage(j, ffn_in)
        stage(j - 1, lambda n: scatter_middle(1, n))
        return carry

    lax.fori_loop(0, images + 3, forward_step, 0)

    def backward_step(step, carry):
        j = step - 1
        stage(j, ffn_grad_compute)
        stage(j - 1, lambda n: gather_relay(3, dattn, n))
        stage(j - 2, block_grad_out)
        stage(j, lambda n: scatter_middle(2, n))
        stage(j + 1, ffn_grad_in)
        stage(j - 1, attn_grad_compute)
        stage(j + 1, lambda n: gather_relay(2, dffn, n))
        stage(j, attn_grad_in)
        stage(j - 1, lambda n: scatter_middle(3, n))
        return carry

    lax.fori_loop(0, images + 3, backward_step, 0)

    for which in (4, 5, 6, 7):
        out_copy(which, images - 1).wait()

    def drain(n, carry):
        for which in (0, 1, 2, 3):
            out_copy(which, n).wait()

        @pl.when(enc)
        def _():
            z_copy(n).wait_send()

        @pl.when(dec)
        def _():
            dz_copy(n).wait_send()

        return carry

    lax.fori_loop(0, images, drain, 0)


def run_main(tok, vel, mod, cosine, sine, wqkv, wout, wgu, wdn, gains):
    images, rows, width = tok.shape
    tokens = 4 * rows
    lanes_all = wout.shape[0]
    heads = lanes_all // LANES
    hidden = wdn.shape[0]
    vmem = pl.BlockSpec(memory_space=pltpu.VMEM)
    anywhere = pl.BlockSpec(memory_space=pl.ANY)

    def hbm(last):
        return jax.ShapeDtypeStruct((images, tokens, last), BF)

    out_shape = (
        jax.ShapeDtypeStruct((images, rows, width), BF),
        jax.ShapeDtypeStruct((images, rows, width), F32),
        jax.ShapeDtypeStruct((images, 8, width), F32),
        jax.ShapeDtypeStruct((8, lanes_all), F32),
        jax.ShapeDtypeStruct((8, width), F32),
        hbm(width),
        hbm(width),
        hbm(width),
        hbm(width),
        hbm(hidden),
        hbm(lanes_all),
        hbm(2 * hidden),
        hbm(3 * lanes_all),
    )
    scratch = [
        pltpu.VMEM((images, rows, width), BF),
        pltpu.VMEM((images, rows, width), BF),
        pltpu.VMEM((images, tokens, width), BF),
        pltpu.VMEM((images, tokens, width), BF),
        pltpu.VMEM((images, tokens, width), BF),
        pltpu.VMEM((images, tokens, width), BF),
        pltpu.VMEM((images, rows, width), F32),
        pltpu.VMEM((images, rows, width), BF),
        pltpu.VMEM((images, rows, width), BF),
        pltpu.VMEM((2, 2 * rows, width), F32),
        pltpu.VMEM((2, 2 * rows, width), BF),
        pltpu.VMEM((2, 2, 2 * rows, width), BF),
        pltpu.VMEM((2, rows, width), BF),
        pltpu.VMEM((2, 2, rows, width), BF),
        pltpu.VMEM((2, rows, width), F32),
        pltpu.VMEM((tokens, lanes_all), BF),
        pltpu.VMEM((tokens, hidden), BF),
        pltpu.VMEM((tokens, 2 * hidden), BF),
        pltpu.VMEM((tokens, 3 * lanes_all), BF),
        pltpu.SemaphoreType.DMA((4, 6, images)),
        pltpu.SemaphoreType.DMA((4, 4, images)),
        pltpu.SemaphoreType.DMA((4, images)),
        pltpu.SemaphoreType.DMA((8, images)),
        pltpu.SemaphoreType.DMA((2,)),
    ]
    return pl.pallas_call(
        functools.partial(main_kernel, images, heads),
        out_shape=out_shape,
        in_specs=[anywhere, anywhere] + [vmem] * 8,
        out_specs=[vmem] * 5 + [anywhere] * 8,
        scratch_shapes=scratch,
        compiler_params=pltpu.CompilerParams(
            collective_id=0, has_side_effects=True, vmem_limit_bytes=62 * 2**20
        ),
    )(tok, vel, mod, cosine, sine, wqkv, wout, wgu, wdn, gains)


def time_embed(bin_row, feature_count):
    halfway = feature_count // 2
    frequency = jnp.exp(-math.log(10000.0) * jnp.arange(halfway, dtype=F32) / halfway)
    moment = (bin_row.astype(F32) + 0.5) * (1000.0 / NBINS)
    angles = moment[:, None] * frequency[None, :]
    return jnp.concatenate([jnp.cos(angles), jnp.sin(angles)], axis=-1)


def per_device(
    tokens,
    velocity_grad,
    bins,
    labels,
    places,
    class_table,
    mod_weight,
    qkv_weight,
    out_weight,
    gate_up_weight,
    down_weight,
    q_gain,
    k_gain,
):
    micro, per_micro, rows, width = tokens.shape
    images = micro * per_micro
    dp = lax.axis_size("dp")
    me = lax.axis_index("tensor")
    heads = q_gain.shape[1] // HEAD_DIM
    select = jnp.asarray(head_select(heads), BF)

    bins_all = lax.all_gather(bins.reshape(images), "dp", axis=0, tiled=True)
    labels_all = lax.all_gather(labels.reshape(images), "dp", axis=0, tiled=True)
    one_hot = labels_all[:, None] == jnp.arange(class_table.shape[0], dtype=jnp.int32)[None, :]
    cond_all = time_embed(bins_all, width) + jnp.dot(one_hot.astype(BF), class_table, preferred_element_type=F32)
    silu_all = jax.nn.silu(cond_all).astype(BF)
    first = lax.axis_index("dp") * images
    cond = lax.dynamic_slice_in_dim(cond_all, first, images, 0)
    silu_low = lax.dynamic_slice_in_dim(silu_all, first, images, 0)
    mod_w = mod_weight[0]
    columns = jnp.einsum("id,djf->ijf", silu_low, mod_w, preferred_element_type=F32)
    modulation = lax.all_gather(columns, "tensor", axis=2, tiled=True)

    order = jnp.stack([me, (me + 2) % 4, me + 1 - 2 * (me % 2), (me + 2) % 4 + 1 - 2 * (me % 2)])
    placed = jnp.take(places.reshape(images, 4, rows), order, axis=1).reshape(images * 4 * rows)
    grid = jnp.arange(GRID, dtype=jnp.int32)[None, :]
    marks = jnp.concatenate([placed[:, None] // GRID == grid, placed[:, None] % GRID == grid], axis=1).astype(F32)
    angles = jnp.dot(marks, jnp.asarray(angle_table()), precision=lax.Precision.HIGHEST)
    angles = angles.reshape(images, 4 * rows, 2 * LANES)

    wqkv = jnp.einsum("jde,ef->jdf", qkv_weight[0], select, preferred_element_type=F32).astype(BF)
    wout = jnp.einsum("ef,ed->fd", select, out_weight[0], preferred_element_type=F32).astype(BF)
    gains = jnp.dot(jnp.concatenate([q_gain, k_gain], axis=0), select, preferred_element_type=F32)

    results = run_main(
        tokens.reshape(images, rows, width),
        velocity_grad.reshape(images, rows, width),
        modulation,
        angles[..., :LANES],
        angles[..., LANES:],
        wqkv,
        wout,
        gate_up_weight[0],
        down_weight[0],
        gains,
    )
    z_rows, dx_rows, dmod, gain_sums, squares, a1, a2, d_ffn, d_attn, units, mixed, d_gu, d_qkv = results

    def weight_grad(left, right):
        return jnp.einsum("ntd,ntf->df", left, right, preferred_element_type=F32).astype(BF)

    hidden = units.shape[2]
    lanes_all = heads * LANES
    g_gate = weight_grad(a2, d_gu[..., :hidden])
    g_up = weight_grad(a2, d_gu[..., hidden:])
    g_down = weight_grad(units, d_ffn)
    g_qkv = weight_grad(a1, d_qkv).reshape(width, 3, lanes_all)
    g_qkv = jnp.einsum("djf,ef->jde", g_qkv, select, preferred_element_type=F32).astype(BF)
    g_out = jnp.einsum("ef,fd->ed", select, weight_grad(mixed, d_attn), preferred_element_type=F32).astype(BF)
    g_gains = jnp.einsum("jf,ef->je", gain_sums[0:2], select.astype(F32), precision=lax.Precision.HIGHEST)
    summed = lax.psum((jnp.stack([g_gate, g_up]), g_down, g_qkv, g_out), "dp")
    gains_sum = lax.psum(g_gains, "dp")
    gate_up_grad, down_grad, qkv_grad, out_grad = [item.astype(F32)[None] for item in summed]

    dmod_low = lax.psum_scatter(dmod[:, 0:6].astype(BF), "tensor", scatter_dimension=2, tiled=True)
    dmod_all = lax.all_gather(dmod_low, "dp", axis=0, tiled=True)
    mod_grad = jnp.einsum("id,ijf->djf", silu_all, dmod_all, preferred_element_type=F32)[None]
    grad_silu = jnp.einsum("ijf,djf->id", dmod_low, mod_w, preferred_element_type=F32)
    sig = jax.nn.sigmoid(cond)
    grad_cond = grad_silu * (sig + cond * sig * (1.0 - sig))
    spread = lax.dynamic_update_slice_in_dim(jnp.zeros((dp * images, width), F32), grad_cond, first, 0)
    spread = lax.psum(spread, ("section", "dp", "tensor"))
    class_grad = jnp.dot(one_hot.astype(F32).T, spread, precision=lax.Precision.HIGHEST)

    square_totals = lax.psum(jnp.sum(squares[0:3], axis=1), ("dp", "tensor"))
    count = images * rows * width * dp * lax.axis_size("tensor")
    stats = jnp.sqrt(square_totals / count)[None, :]
    whole = (1, micro, per_micro, rows, width)
    return (
        z_rows.reshape(whole),
        dx_rows.reshape(whole),
        mod_grad,
        qkv_grad,
        out_grad,
        gate_up_grad,
        down_grad,
        gains_sum[0:1],
        gains_sum[1:2],
        class_grad,
        stats,
    )


def solution(mesh):
    return jax.shard_map(
        per_device,
        mesh=mesh,
        in_specs=(
            P(None, "dp", "tensor", None),
            P(None, "dp", "tensor", None),
            P(None, "dp"),
            P(None, "dp"),
            P(None, "dp", None),
            P(),
            P("section", None, None, "tensor"),
            P("section", None, None, "tensor"),
            P("section", "tensor", None),
            P("section", None, None, "tensor"),
            P("section", "tensor", None),
            P("section", "tensor"),
            P("section", "tensor"),
        ),
        out_specs=(
            P("section", None, "dp", "tensor", None),
            P("section", None, "dp", "tensor", None),
            P("section", None, None, "tensor"),
            P("section", None, None, "tensor"),
            P("section", "tensor", None),
            P("section", None, None, "tensor"),
            P("section", "tensor", None),
            P("section", "tensor"),
            P("section", "tensor"),
            P(),
            P("section", None),
        ),
        check_vma=False,
    )
```

time: 2120 us -> 954 us (0.45)
  waiting for transfers between devices: 1090 us -> 334 us
  Pallas kernels: 0 us -> 387 us
  local copies, waits for them, and re-layouts: 310 us -> 29.5 us
  matrix products: 344 us -> 74.2 us
  other arithmetic: 210 us -> 15.9 us
  starting transfers between devices: 24.5 us -> 0.29 us
    pallas_call x0 -> x1, Pallas kernels: none -> 387 us  [run_main(): pl.pallas_call(functools.partial(main_kernel, images, heads), out_shape=o...]
    reduce_scatter x20 -> x0, waiting for transfers between devices: 283 us -> none  [the longest x10 179 us: collect_grads(): lax.psum_scatter(partial_rows.astype(jnp.bfloat16), 'tensor', scatter_dim...]
    all_gather x20 -> x0, waiting for transfers between devices: 278 us -> none  [the longest x10 161 us: spread_rows(): return lax.all_gather(activation, 'tensor', axis=1, tiled=True)]
    dot_general x110 -> x17, matrix products: 327 us -> 74.2 us  [the longest x4 32.7 us: weight_grad(): jnp.einsum('ntd,ntf->df', left, right, preferred_element_type=F32)]
    unnamed x857 -> x68, local copies, waits for them, and re-layouts: 181 us -> 13.8 us
    psum x2, waiting for transfers between devices: 450 us -> 334 us  [the longest x1 280 us: per_device(): summed = lax.psum((jnp.stack([g_gate, g_up]), g_down, g_qkv, g_out), 'dp')]
    slice x45 -> x3, local copies, waits for them, and re-layouts: 89.1 us -> 3.09 us  [the longest x1 1.54 us: per_device(): angles[..., LANES:]]
    reduce_sum x60 -> x1, other arithmetic: 74 us -> 0.12 us  [per_device(): square_totals = lax.psum(jnp.sum(squares[0:3], axis=1), ('dp', 'tensor'))]
  transfers between devices with their start and end apart: 55 -> 3, of which waited for: 50 -> 2; matrix products, arithmetic and copies ran while one was open for 22% -> 7% of each run, Pallas kernels for 0% -> 0%
where the time goes in v1:
time: 954 us; the launch traced here: 949 us
  Pallas kernels  387 us (41%)
  waiting for transfers between devices  334 us (35%)
  blocking collectives  92.9 us (10%)
  matrix products  74.2 us (8%)
  local copies, waits for them, and re-layouts  29.5 us (3%)
  other arithmetic  15.9 us (2%)
  between operations  15 us (2%)
    pallas_call x1, Pallas kernels, run_main(): pl.pallas_call(functools.partial(main_kernel, images, heads), out_shape=o...  387 us
    psum x1, waiting for transfers between devices, per_device(): summed = lax.psum((jnp.stack([g_gate, g_up]), g_down, g_qkv, g_out), 'dp')  280 us
    psum x1, waiting for transfers between devices, per_device(): spread = lax.psum(spread, ('section', 'dp', 'tensor'))  54.5 us
    dot_general x4, matrix products, weight_grad(): jnp.einsum('ntd,ntf->df', left, right, preferred_element_type=F32)  32.7 us
    all_gather x1, blocking collectives, per_device(): modulation = lax.all_gather(columns, 'tensor', axis=2, tiled=True)  30.8 us
    psum x1, blocking collectives, per_device(): square_totals = lax.psum(jnp.sum(squares[0:3], axis=1), ('dp', 'tensor'))  30 us
  transfers between devices with their start and end apart: 3, of which 2 were waited for; matrix products, arithmetic and copies ran while one was open for 7% of the time, Pallas kernels for 0%

profile of v1, /device:TPU:0, one launch (start us, length us, event | category | flops | bytes accessed | tf_op | source)
XLA Modules:
  0.0 949.1 jit_solution(568410139176245086)
XLA Ops:
  9.1 1.8 fusion.31
  10.9 1.8 convolution_add_fusion
  12.7 1.5 fusion.49
  16.3 9.9 %all-reduce.2 = (s32[32]{0:T(128)S(1)}, s32[32]{0:T(128)S(1)}) all-reduce(s32[32]{0:T(128)S(1)} %dynamic-update-slice, s32[32]{0:T(128)S(1)} %dynamic-update-slice.1), channel_id=1, replica_groups=mesh['section'=2,'dp'=4,'tensor'=4] {'dp'}, use_global_device_ids=true, to_apply=%add | all-reduce | flops 64 | bytes 512
  26.6 2.9 multiply_convert_fusion
  30.1 3.4 fusion.3
  34.1 30.8 %all_gather.14 = f32[8,6,1152]{1,0,2:T(8,128)} all-gather(f32[8,6,288]{1,0,2:T(8,128)S(1)} %copy.64), channel_id=1, replica_groups=mesh['section'=2,'dp'=4,'tensor'=4] {'tensor'}, dimensions={2}, use_global_device_ids=true | all-gather | bytes 276480 | tf_op jit(solution)/shard_map/all_gather | solution.py:652
  64.8 4.0 copy.68.mod
  68.9 3.8 fusion.5.wqkv
  72.7 1.9 convolution_convert_fusion.2.wout
  75.4 386.8 %shard_map.230 = (bf16[8,64,1152]{2,1,0:T(8,128)(2,1)}, f32[8,64,1152]{2,1,0:T(8,128)}, f32[8,8,1152]{2,1,0:T(8,128)}, f32[8,512]{1,0:T(8,128)}, f32[8,1152]{1,0...) custom-call(bf16[8,64,1152]{2,1,0:T(8,128)(2,1)} %bitcast.132, ...), custom_call_target="tpu_custom_call" | custom-call | tf_op jit(solution)/shard_map/pallas_call | solution.py:600
  463.1 2.7 copy.85
  465.9 4.0 reshape.376
  470.1 7.4 fusion.16
  477.6 7.3 fusion.13
  484.9 9.2 fusion
  494.1 5.9 copy.71
  500.0 8.8 fusion.12
  508.9 7.7 fusion.20
  516.6 3.6 maximum_bitcast_fusion
  521.9 2.8 fusion.27
  525.5 4.5 fusion.11
  530.9 30.0 %psum.55 = f32[3]{0:T(128)S(1)} all-reduce(f32[3]{0:T(128)S(1)} %slice_reduce_fusion), channel_id=1, replica_groups=mesh['section'=2,'dp'=4,'tensor'=4] {'dp','tensor'}, use_global_device_ids=true, to_apply=%region_8.9 | all-reduce | flops 3 | bytes 24 | tf_op jit(solution)/shard_map/psum | solution.py:705
  561.3 8.4 psum.53
  570.7 13.9 %all_gather.15 = bf16[32,6,288]{2,0,1:T(8,128)(2,1)S(1)} all-gather(bf16[8,6,288]{2,0,1:T(8,128)(2,1)S(1)} %copy.69), channel_id=1, replica_groups=mesh['section'=2,'dp'=4,'tensor'=4] {'dp'}, dimensions={0}, use_global_device_ids=true | all-gather | bytes 138240 | tf_op jit(solution)/shard_map/all_gather | solution.py:696
  584.6 4.5 convolution_bitcast_fusion.1
  589.1 54.5 %all-reduce.7.cloned.1.call-done = f32[32,1152]{1,0:T(8,128)} async-done(((f32[32,1152]{1,0:T(8,128)}), f32[32,1152]{1,0:T(8,128)}) %all-reduce.7.cloned.1.call-update) | async-done | bytes 147472 | tf_op jit(solution)/shard_map/psum | solution.py:702
  643.6 5.3 fusion.35
  649.0 279.8 %all-reduce.9.cloned.1.call-done = (bf16[1,3,1152,288]{2,3,1,0:T(8,128)(2,1)}, bf16[1,288,1152]{2,1,0:T(8,128)(2,1)}, bf16[1,2,1152,768]{3,2,1,0:T(8,128)(2,1)}, bf16[1,768,1152]{2,1,0:T(8,128)(2,1)}) async-done(((bf16[1,3,1152,288]{2,3,1,0:T(8,128)(2,1)}, bf16[1,288,1152]{2,1,0:T(8,128)(2,1)}, bf16[1,2,1152,768]{3,2,1,0:T(8,128)(2,1)}, bf16[1,768,1152]{2,1,0:T(8,128)(2,1)}), ...) | async-done | bytes 7962640 | tf_op jit(solution)/shard_map/psum | solution.py:691
  928.8 5.7 broadcast_in_dim.56
  934.5 2.2 broadcast_in_dim.52
  936.7 2.0 broadcast_in_dim.58
  (101 shorter events, 15.2 us)
Async XLA Ops:
  7.2 61.7 %copy-start = (bf16[1,3,1152,288]{2,3,1,0:T(8,128)(2,1)S(1)}, bf16[1,3,1152,288]{2,3,1,0:T(8,128)(2,1)}, u32[]{:S(2)}) copy-start(bf16[1,3,1152,288]{2,3,1,0:T(8,128)(2,1)} %param.22) | copy-start | bytes 5971972
  7.2 513.0 %reduce-scatter.4.cloned.1.call-start = ((), (), s32[]{:S(2)}) async-start(), calls=%async_computation.2 | async-start | bytes 368640
  10.9 3.4 copy-start.18
  10.9 3.6 copy-start.19
  10.9 3.7 copy-start.21
  29.5 0.6 copy-start.10
  64.8 4.0 copy-start.12
  68.8 3.9 copy-start.6
  68.8 3.9 copy-start.20
  68.9 5.7 copy-start.16
  68.9 5.7 copy-start.17
  465.9 11.7 %slice-start.4 = ((s8[4718592]{0:T(1024)(128)(4,1)}), s8[524288]{0:T(1024)(128)(4,1)S(1)}, s32[]{:S(2)}) async-start(s8[4718592]{0:T(1024)(128)(4,1)} %bitcast.138), calls=%async_computation.8 | async-start | bytes 1048576
  469.9 173.8 %all-reduce.7.cloned.1.call-start = ((), (), s32[]{:S(2)}) async-start(), calls=%async_computation.1 | async-start | bytes 294912 | tf_op jit(solution)/shard_map/psum | solution.py:702
  470.1 7.5 slice-start.5
  470.1 14.7 %slice-start = ((s8[6291456]{0:T(1024)(128)(4,1)}), s8[4194304]{0:T(1024)(128)(4,1)S(1)}, s32[]{:S(2)}) async-start(s8[6291456]{0:T(1024)(128)(4,1)} %bitcast.134), calls=%async_computation.4 | async-start | bytes 8388608
  470.1 14.7 %slice-start.2 = ((s8[4718592]{0:T(1024)(128)(4,1)}), s8[4194304]{0:T(1024)(128)(4,1)S(1)}, s32[]{:S(2)}) async-start(s8[4718592]{0:T(1024)(128)(4,1)} %bitcast.136), calls=%async_computation.6 | async-start | bytes 8388608
  477.6 7.3 slice-start.1
  477.6 7.3 slice-start.3
  500.0 8.8 copy-start.7
  520.2 5.3 copy-start.13
  524.7 0.7 copy-start.9
  525.4 403.4 %all-reduce.9.cloned.1.call-start = ((), (), s32[]{:S(2)}) async-start(), calls=%async_computation.3 | async-start | bytes 15925248 | tf_op jit(solution)/shard_map/psum | solution.py:691
  530.0 0.8 copy-start.15
  530.0 30.9 %copy-start.14 = (f32[8,512]{1,0:T(8,128)S(1)}, f32[8,512]{1,0:T(8,128)}, u32[]{:S(2)}) copy-start(f32[8,512]{1,0:T(8,128)} %get-tuple-element.35) | copy-start | bytes 49156
  530.0 54.6 %copy-start.11 = (bf16[32,1152]{1,0:T(8,128)(2,1)S(1)}, bf16[32,1152]{1,0:T(8,128)(2,1)}, u32[]{:S(2)}) copy-start(bf16[32,1152]{1,0:T(8,128)(2,1)} %copy-done.10) | copy-start | bytes 221188
  928.8 5.7 copy-start.3
  934.5 2.2 copy-start.4
  936.7 2.0 copy-start.8
  936.7 3.2 copy-start.5
  936.7 4.2 copy-start.2
  939.9 2.4 copy-start.1
Sparse Core Ops, SparseCore 0:
  470.0 17.6 reduce-scatter.3
  525.5 118.0 all-reduce.6
  647.3 281.4 all-reduce.8

commit v2 on v1

--- a/solution.py
+++ b/solution.py
@@ -75,7 +75,7 @@
     heads,
     tok,
     vel,
-    mod,
+    mod_cols,
     cosine,
     sine,
     wqkv,
@@ -85,7 +85,7 @@
     gains,
     zout,
     dxout,
-    dmod,
+    dmod_part,
     gacc,
     sacc,
     a1_hbm,
@@ -115,6 +115,12 @@
     hid_st,
     dgu_st,
     dqkv_st,
+    mod,
+    mod_recv,
+    dmod,
+    dmod_recv,
+    mod_sems,
+    dmod_sems,
     ag_sems,
     rs_sems,
     zx_sems,
@@ -129,6 +135,8 @@
     me = lax.axis_index("tensor")
     sib = me + 1 - 2 * lax.rem(me, 2)
     across = lax.rem(me + 2, 4)
+    diag = lax.rem(sib + 2, 4)
+    peers = (sib, across, diag)
     other = 1 - section
     enc = section == 0
     dec = section == 1
@@ -147,89 +155,97 @@
     barrier = pltpu.get_barrier_semaphore()
     pl.semaphore_signal(barrier, inc=1, device_id={"tensor": sib}, device_id_type=MESH)
     pl.semaphore_signal(barrier, inc=1, device_id={"tensor": across}, device_id_type=MESH)
+    pl.semaphore_signal(barrier, inc=1, device_id={"tensor": diag}, device_id_type=MESH)
     pl.semaphore_signal(barrier, inc=1, device_id={"section": other}, device_id_type=MESH)
 
+    mod[...] = jnp.zeros_like(mod)
     gacc[...] = jnp.zeros_like(gacc)
     sacc[...] = jnp.zeros_like(sacc)
     dmod[...] = jnp.zeros_like(dmod)
 
-    @pl.when(enc)
-    def _():
-        load_x.wait()
-
-    @pl.when(dec)
-    def _():
-        load_d.wait()
-
-    pl.semaphore_wait(barrier, 3)
+    pl.semaphore_wait(barrier, 4)
 
     def remote(src, dst, send_sem, recv_sem, where):
         return pltpu.make_async_remote_copy(
             src_ref=src, dst_ref=dst, send_sem=send_sem, recv_sem=recv_sem, device_id=where, device_id_type=MESH
         )
 
-    def gather(which, buf, n):
-        over_y = remote(
-            buf.at[n, pl.ds(0, rows)],
-            buf.at[n, pl.ds(rows, rows)],
-            ag_sems.at[which, 0, n],
-            ag_sems.at[which, 1, n],
-            {"tensor": across},
+    def its_tiles(device):
+        return pl.ds(pl.multiple_of(device * (2 * LANES), LANES), 3 * LANES)
+
+    def mod_copy(k):
+        return remote(mod_cols, mod_recv.at[k], mod_sems.at[0, k], mod_sems.at[1, k], {"tensor": peers[k]})
+
+    def dmod_copy(k, n):
+        return remote(
+            dmod.at[n, :, its_tiles(peers[k])],
+            dmod_recv.at[k, n],
+            dmod_sems.at[0, k, n],
+            dmod_sems.at[1, k, n],
+            {"tensor": peers[k]},
         )
-        to_sib = remote(
-            buf.at[n, pl.ds(0, rows)],
-            buf.at[n, pl.ds(2 * rows, rows)],
-            ag_sems.at[which, 2, n],
-            ag_sems.at[which, 3, n],
-            {"tensor": sib},
+
+    for k in (1, 2, 0):
+        mod_copy(k).start()
+    mod[:, :, its_tiles(me)] = mod_cols[...]
+
+    @pl.when(enc)
+    def _():
+        load_x.wait()
+
+    @pl.when(dec)
+    def _():
+        load_d.wait()
+
+    for k in range(3):
+        mod_copy(k).wait()
+        mod[:, :, its_tiles(peers[k])] += mod_recv[k]
+
+    def gather(which, buf, n, kind):
+        src, dst, where = ((0, rows, across), (0, 2 * rows, sib), (rows, 3 * rows, sib))[kind]
+        return remote(
+            buf.at[n, pl.ds(src, rows)],
+            buf.at[n, pl.ds(dst, rows)],
+            ag_sems.at[which, 2 * kind, n],
+            ag_sems.at[which, 2 * kind + 1, n],
+            {"tensor": where},
         )
-        relay = remote(
-            buf.at[n, pl.ds(rows, rows)],
-            buf.at[n, pl.ds(3 * rows, rows)],
-            ag_sems.at[which, 4, n],
-            ag_sems.at[which, 5, n],
-            {"tensor": sib},
-        )
-        return over_y, to_sib, relay
 
     def gather_start(which, buf, n):
-        over_y, to_sib, relay = gather(which, buf, n)
-        over_y.start()
-        to_sib.start()
+        gather(which, buf, n, 0).start()
+        gather(which, buf, n, 1).start()
 
     def gather_relay(which, buf, n):
-        over_y, to_sib, relay = gather(which, buf, n)
-        over_y.wait_recv()
-        relay.start()
+        gather(which, buf, n, 0).wait_recv()
+        gather(which, buf, n, 2).start()
 
     def gather_wait(which, buf, n):
-        over_y, to_sib, relay = gather(which, buf, n)
-        to_sib.wait_recv()
-        relay.wait_recv()
+        gather(which, buf, n, 1).wait_recv()
+        gather(which, buf, n, 2).wait_recv()
 
     def gather_drain(which, buf, n):
-        over_y, to_sib, relay = gather(which, buf, n)
-        over_y.wait_send()
-        to_sib.wait_send()
-        relay.wait_send()
-
-    def scatter(which, n):
-        kind, slot = which % 2, lax.rem(n, 2)
-        to_sib = remote(
+        for kind in range(3):
+            gather(which, buf, n, kind).wait_send()
+
+    def to_sibling(which, n):
+        kind = which % 2
+        return remote(
             send_a.at[kind],
-            recv_a.at[kind, slot],
+            recv_a.at[kind, lax.rem(n, 2)],
             rs_sems.at[which, 0, n],
             rs_sems.at[which, 1, n],
             {"tensor": sib},
         )
-        over_y = remote(
+
+    def over_y(which, n):
+        kind = which % 2
+        return remote(
             send_y.at[kind],
-            recv_y.at[kind, slot],
+            recv_y.at[kind, lax.rem(n, 2)],
             rs_sems.at[which, 2, n],
             rs_sems.at[which, 3, n],
             {"tensor": across},
         )
-        return kind, slot, to_sib, over_y
 
     def scatter_put(which, at, size, values):
         kind = which % 2
@@ -237,21 +253,18 @@
         send_a[kind, :, pl.ds(at, size)] = values[2 * rows : 4 * rows].astype(BF)
 
     def scatter_start(which, n):
-        kind, slot, to_sib, over_y = scatter(which, n)
-        to_sib.start()
+        to_sibling(which, n).start()
 
     def scatter_middle(which, n):
-        kind, slot, to_sib, over_y = scatter(which, n)
-        to_sib.wait()
+        kind, slot = which % 2, lax.rem(n, 2)
+        to_sibling(which, n).wait()
         send_y[kind] = (keep[kind, rows : 2 * rows] + recv_a[kind, slot, rows : 2 * rows].astype(F32)).astype(BF)
-        over_y.start()
+        over_y(which, n).start()
 
     def scatter_end(which, n):
-        kind, slot, to_sib, over_y = scatter(which, n)
-        over_y.wait()
-        return (
-            keep[kind, 0:rows] + recv_a[kind, slot, 0:rows].astype(F32) + recv_y[kind, slot].astype(F32)
-        )
+        kind, slot = which % 2, lax.rem(n, 2)
+        over_y(which, n).wait()
+        return keep[kind, 0:rows] + recv_a[kind, slot, 0:rows].astype(F32) + recv_y[kind, slot].astype(F32)
 
     def z_copy(n):
         return remote(zout.at[n], xin.at[n], zx_sems.at[0, n], zx_sems.at[1, n], {"section": other})
@@ -293,17 +306,9 @@
         return powered * (1.0 / jnp.sum(powered, axis=-1, keepdims=True))
 
     def out_copy(which, n):
-        src, dst = (
-            (a1f.at[n], a1_hbm.at[n]),
-            (a2f.at[n], a2_hbm.at[n]),
-            (dffn.at[n], dffn_hbm.at[n]),
-            (dattn.at[n], dattn_hbm.at[n]),
-            (hid_st, hid_hbm.at[n]),
-            (mix_st, mix_hbm.at[n]),
-            (dgu_st, dgu_hbm.at[n]),
-            (dqkv_st, dqkv_hbm.at[n]),
-        )[which]
-        return pltpu.make_async_copy(src, dst, out_sems.at[which, n])
+        src = (a1f, a2f, dffn, dattn, hid_st, mix_st, dgu_st, dqkv_st)[which]
+        dst = (a1_hbm, a2_hbm, dffn_hbm, dattn_hbm, hid_hbm, mix_hbm, dgu_hbm, dqkv_hbm)[which]
+        return pltpu.make_async_copy(src.at[n] if which < 4 else src, dst.at[n], out_sems.at[which, n])
 
     def staged_ready(which, n):
         @pl.when(n > 0)
@@ -489,6 +494,9 @@
             xin[n] = grad.astype(BF)
             dz_copy(n).start()
 
+        for k in range(3):
+            dmod_copy(k, n).start()
+
     def stage(n, body):
         @pl.when((n >= 0) & (n < images))
         def _():
@@ -530,6 +538,11 @@
     def drain(n, carry):
         for which in (0, 1, 2, 3):
             out_copy(which, n).wait()
+        part = dmod[n, :, its_tiles(me)]
+        for k in range(3):
+            dmod_copy(k, n).wait()
+            part += dmod_recv[k, n]
+        dmod_part[n] = part.astype(BF)
 
         @pl.when(enc)
         def _():
@@ -544,7 +557,7 @@
     lax.fori_loop(0, images, drain, 0)
 
 
-def run_main(tok, vel, mod, cosine, sine, wqkv, wout, wgu, wdn, gains):
+def run_main(tok, vel, mod_cols, cosine, sine, wqkv, wout, wgu, wdn, gains):
     images, rows, width = tok.shape
     tokens = 4 * rows
     lanes_all = wout.shape[0]
@@ -559,7 +572,7 @@
     out_shape = (
         jax.ShapeDtypeStruct((images, rows, width), BF),
         jax.ShapeDtypeStruct((images, rows, width), F32),
-        jax.ShapeDtypeStruct((images, 8, width), F32),
+        jax.ShapeDtypeStruct((images, 8, 3 * LANES), BF),
         jax.ShapeDtypeStruct((8, lanes_all), F32),
         jax.ShapeDtypeStruct((8, width), F32),
         hbm(width),
@@ -591,6 +604,12 @@
         pltpu.VMEM((tokens, hidden), BF),
         pltpu.VMEM((tokens, 2 * hidden), BF),
         pltpu.VMEM((tokens, 3 * lanes_all), BF),
+        pltpu.VMEM((images, 8, width), F32),
+        pltpu.VMEM((3, images, 8, 3 * LANES), F32),
+        pltpu.VMEM((images, 8, width), F32),
+        pltpu.VMEM((3, images, 8, 3 * LANES), F32),
+        pltpu.SemaphoreType.DMA((2, 3)),
+        pltpu.SemaphoreType.DMA((2, 3, images)),
         pltpu.SemaphoreType.DMA((4, 6, images)),
         pltpu.SemaphoreType.DMA((4, 4, images)),
         pltpu.SemaphoreType.DMA((4, images)),
@@ -606,7 +625,466 @@
         compiler_params=pltpu.CompilerParams(
             collective_id=0, has_side_effects=True, vmem_limit_bytes=62 * 2**20
         ),
-    )(tok, vel, mod, cosine, sine, wqkv, wout, wgu, wdn, gains)
+    )(tok, vel, mod_cols, cosine, sine, wqkv, wout, wgu, wdn, gains)
+
+
+def flat_plan(width, hidden, qkv_blocks, out_rows):
+    gu_blocks, blocks = 2 * hidden // LANES, width // LANES
+    half_down = blocks * hidden // 2
+    qkv_cut, out_cut = qkv_blocks // 2, blocks - 1
+    first = (gu_blocks // 2) * width + half_down + qkv_cut * width + out_cut * out_rows
+    second = (gu_blocks - gu_blocks // 2) * width + half_down + (qkv_blocks - qkv_cut) * width
+    second += (blocks - out_cut) * out_rows
+    chunk = width // 2
+    half = -(-max(first, second) // chunk) * chunk
+
+    def pieces(segment, block):
+        if segment == 0:
+            cut = gu_blocks // 2
+            return [(block * width if block < cut else half + (block - cut) * width, 0, width)]
+        at = (gu_blocks // 2) * width
+        at_second = half + (gu_blocks - gu_blocks // 2) * width
+        if segment == 1:
+            low, high = block * hidden, (block + 1) * hidden
+            if high <= half_down:
+                return [(at + low, 0, hidden)]
+            if low >= half_down:
+                return [(at_second + low - half_down, 0, hidden)]
+            return [(at + low, 0, half_down - low), (at_second, half_down - low, high - half_down)]
+        at, at_second = at + half_down, at_second + half_down
+        if segment == 2:
+            if block < qkv_cut:
+                return [(at + block * width, 0, width)]
+            return [(at_second + (block - qkv_cut) * width, 0, width)]
+        at, at_second = at + qkv_cut * width, at_second + (qkv_blocks - qkv_cut) * width
+        if block < out_cut:
+            return [(at + block * out_rows, 0, out_rows)]
+        return [(at_second + (block - out_cut) * out_rows, 0, out_rows)]
+
+    return half, chunk, pieces
+
+
+def tail_kernel(
+    dp,
+    a2_hbm,
+    dgu_hbm,
+    hid_hbm,
+    dffn_hbm,
+    a1_hbm,
+    dqkv_hbm,
+    mix_hbm,
+    dattn_hbm,
+    pick_qkv,
+    pick_out,
+    summand,
+    dmod_low,
+    extra,
+    totals,
+    dmod_all,
+    sum_all,
+    extra_all,
+    left_a,
+    right_a,
+    left_b,
+    right_b,
+    left_c,
+    turned,
+    own,
+    arrived,
+    sum_st,
+    sum_recv,
+    load_sems,
+    part_sems,
+    total_sems,
+    sum_sems,
+    all_sems,
+):
+    section = lax.axis_index("section")
+    place = lax.axis_index("dp")
+    me = lax.axis_index("tensor")
+    sib = me + 1 - 2 * lax.rem(me, 2)
+    across = lax.rem(me + 2, 4)
+    width, hidden = left_a.shape[1], left_b.shape[1]
+    qkv_blocks, out_rows = pick_qkv.shape[1] // LANES, pick_out.shape[0]
+    half, chunk, pieces = flat_plan(width, hidden, qkv_blocks, out_rows)
+    count = half // chunk
+
+    loads = [
+        pltpu.make_async_copy(src, dst, load_sems.at[i])
+        for i, (src, dst) in enumerate(
+            (
+                (a2_hbm, left_a),
+                (dgu_hbm, right_a),
+                (hid_hbm, left_b),
+                (dffn_hbm, right_b),
+                (mix_hbm, left_c),
+                (a1_hbm, left_a),
+                (dqkv_hbm, right_a),
+                (dattn_hbm, right_b),
+            )
+        )
+    ]
+    for i in range(5):
+        loads[i].start()
+
+    barrier = pltpu.get_barrier_semaphore()
+    for where in ({"tensor": sib}, {"tensor": across}, {"section": 1 - section}):
+        pl.semaphore_signal(barrier, inc=1, device_id=where, device_id_type=MESH)
+    for k in range(1, dp):
+        pl.semaphore_signal(barrier, inc=1, device_id={"dp": lax.rem(place + k, dp)}, device_id_type=MESH)
+
+    def put(segment, block, value):
+        for at, low, size in pieces(segment, block):
+            own[at : at + size, :] = value[low : low + size].astype(BF)
+
+    def put_pair(segment, block, value):
+        for i in range(value.shape[1] // LANES):
+            put(segment, block + i, value[:, i * LANES : (i + 1) * LANES])
+
+    def turn_left(ref):
+        tokens, cols = ref.shape
+        for at in range(0, tokens, 256):
+            turned[0:cols, at : at + 256] = ref[at : at + 256, :].T
+
+    def gate_up_blocks(*blocks):
+        for block in blocks:
+            value = dot(turned[...], right_a[:, block * LANES : (block + 2) * LANES])
+            put_pair(0, block, value)
+
+    def qkv_tiles(*tiles):
+        for tile in tiles:
+            value = dot_tn(left_a[:, tile * LANES : (tile + 1) * LANES], right_a[...]).astype(BF)
+            value = dot(value, pick_qkv[...])
+            for block in range(qkv_blocks):
+                (at, _, _), = pieces(2, block)
+                cut = slice(block * LANES, (block + 1) * LANES)
+                own[at + tile * LANES : at + (tile + 1) * LANES, :] = value[:, cut].astype(BF)
+
+    def portion(i):
+        gu_blocks, tiles = right_a.shape[1] // LANES, width // LANES
+        gu_blocks = 2 * hidden // LANES
+        if i == 0:
+            loads[0].wait()
+            turn_left(left_a)
+            loads[5].start()
+            loads[1].wait()
+            gate_up_blocks(0, gu_blocks // 2)
+        elif i == 1:
+            gate_up_blocks(2, gu_blocks // 2 + 2)
+        elif i == 2:
+            gate_up_blocks(*range(4, gu_blocks // 2, 2), *range(gu_blocks // 2 + 4, gu_blocks, 2))
+            loads[6].start()
+        elif i == 3:
+            loads[2].wait()
+            turn_left(left_b)
+            loads[3].wait()
+            for block in range(0, tiles, 2):
+                cut = slice(block * LANES, min(width, (block + 2) * LANES))
+                put_pair(1, block, dot(turned[0:hidden, :], right_b[:, cut]))
+            loads[7].start()
+        elif i in (4, 5, 6):
+            if i == 4:
+                loads[5].wait()
+                loads[6].wait()
+            third = -(-tiles // 3)
+            qkv_tiles(*range((i - 4) * third, min(tiles, (i - 3) * third)))
+        elif i == 7:
+            loads[4].wait()
+            loads[7].wait()
+            value = dot(pick_out[...], dot_tn(left_c[...], right_b[...]).astype(BF))
+            put_pair(3, 0, value)
+            (at, _, size), = pieces(3, tiles - 1)
+            own[at + size :, :] = jnp.zeros((2 * half - at - size, LANES), BF)
+
+    def along(direction, onward):
+        step = 1 if (direction == 0) == onward else dp - 1
+        return {"dp": lax.rem(place + step, dp)}
+
+    def behind(direction):
+        return place if direction == 0 else dp - 1 - place
+
+    def rows_of(direction, c):
+        return pl.ds(pl.multiple_of(direction * half + c * chunk, chunk), chunk)
+
+    def part_copy(direction, c):
+        return pltpu.make_async_remote_copy(
+            src_ref=own.at[rows_of(direction, c)],
+            dst_ref=arrived.at[rows_of(direction, c)],
+            send_sem=part_sems.at[direction, 0, c],
+            recv_sem=part_sems.at[direction, 1, c],
+            device_id=along(direction, True),
+            device_id_type=MESH,
+        )
+
+    def total_copy(direction, c):
+        return pltpu.make_async_remote_copy(
+            src_ref=totals.at[rows_of(direction, c)],
+            dst_ref=totals.at[rows_of(direction, c)],
+            send_sem=total_sems.at[direction, 0, c],
+            recv_sem=total_sems.at[direction, 1, c],
+            device_id=along(direction, False),
+            device_id_type=MESH,
+        )
+
+    def add_part(direction, c):
+        begins, ends = behind(direction) == 0, behind(direction) == dp - 1
+        rows = rows_of(direction, c)
+
+        @pl.when(begins)
+        def _():
+            part_copy(direction, c).start()
+
+        @pl.when(jnp.logical_not(begins))
+        def _():
+            part_copy(direction, c).wait_recv()
+            value = (own[rows, :].astype(F32) + arrived[rows, :].astype(F32)).astype(BF)
+
+            @pl.when(ends)
+            def _():
+                totals[rows, :] = value
+                total_copy(direction, c).start()
+
+            @pl.when(jnp.logical_not(ends))
+            def _():
+                own[rows, :] = value
+                part_copy(direction, c).start()
+
+    def pass_total(direction, c):
+        begins, ends = behind(direction) == 0, behind(direction) == dp - 1
+
+        @pl.when(jnp.logical_not(ends))
+        def _():
+            total_copy(direction, c).wait_recv()
+
+            @pl.when(jnp.logical_not(begins))
+            def _():
+                total_copy(direction, c).start()
+
+    skew = 2
+
+    def chunk_step(step):
+        for direction in range(2):
+            c = step - skew * behind(direction)
+
+            @pl.when((c >= 0) & (c < count))
+            def _():
+                add_part(direction, c)
+
+        for direction in range(2):
+            u = step - skew * (2 * (dp - 1) - behind(direction))
+
+            @pl.when((u >= 0) & (u < count))
+            def _():
+                pass_total(direction, u)
+
+    def sum_copy(which):
+        where = ({"section": 1 - section}, {"tensor": sib}, {"tensor": across})[which]
+        height = (8, 16, 16)[which]
+        src = summand if which == 0 else sum_st.at[which - 1]
+        return pltpu.make_async_remote_copy(
+            src_ref=src.at[pl.ds(0, height)],
+            dst_ref=sum_recv.at[which, pl.ds(0, height)],
+            send_sem=sum_sems.at[which, 0],
+            recv_sem=sum_sems.at[which, 1],
+            device_id=where,
+            device_id_type=MESH,
+        )
+
+    def all_copy(which, k, outgoing):
+        ref = (dmod_all, sum_all, extra_all)[which]
+        peer = lax.rem(place + k, dp)
+        slot = place if outgoing else peer
+        return pltpu.make_async_remote_copy(
+            src_ref=ref.at[slot],
+            dst_ref=ref.at[slot],
+            send_sem=all_sems.at[which, 0, k],
+            recv_sem=all_sems.at[which, 1, slot],
+            device_id={"dp": peer},
+            device_id_type=MESH,
+        )
+
+    def small(step):
+        if step == 0:
+            dmod_all[place] = dmod_low[...]
+            for k in range(1, dp):
+                all_copy(0, k, True).start()
+            sum_copy(0).start()
+        elif step == 1:
+            sum_copy(0).wait()
+            sum_st[0] = summand[...]
+            sum_st[0, 0:8, :] += sum_recv[0, 0:8, :]
+            sum_copy(1).start()
+        elif step == 2:
+            sum_copy(1).wait()
+            sum_st[1] = sum_st[0] + sum_recv[1]
+            sum_copy(2).start()
+        elif step == 3:
+            sum_copy(2).wait()
+            total = sum_st[1] + sum_recv[2]
+            sum_all[place] = total.astype(BF)
+            squares = total[8:16, 0:LANES]
+            for i in range(1, width // LANES):
+                squares += total[8:16, i * LANES : (i + 1) * LANES]
+            extra_all[place, 0:8, :] = extra[...]
+            extra_all[place, 8:16, :] = jnp.zeros_like(extra)
+            extra_all[place, 8:16, 0:LANES] = squares
+            for k in range(1, dp):
+                all_copy(1, k, True).start()
+                all_copy(2, k, True).start()
+
+    portion(0)
+    pl.semaphore_wait(barrier, 3 + dp - 1)
+    for step in range(8):
+        chunk_step(step)
+        small(step)
+        portion(step + 1)
+
+    def later_step(step, carry):
+        chunk_step(step)
+        return carry
+
+    lax.fori_loop(8, count + 2 * skew * (dp - 1), later_step, 0)
+
+    for which in range(3):
+        for k in range(1, dp):
+            all_copy(which, k, True).wait_send()
+            all_copy(which, k, False).wait_recv()
+
+    def drain(c, carry):
+        for direction in range(2):
+
+            @pl.when(behind(direction) != dp - 1)
+            def _():
+                part_copy(direction, c).wait_send()
+
+            @pl.when(behind(direction) != 0)
+            def _():
+                total_copy(direction, c).wait_send()
+
+        return carry
+
+    lax.fori_loop(0, count, drain, 0)
+
+
+def run_tail(dp, a2, dgu, hid, dffn, a1, dqkv, mix, dattn, pick_qkv, pick_out, summand, dmod_low, extra):
+    tokens, width = a2.shape
+    hidden = hid.shape[1]
+    out_rows, lanes_all = pick_out.shape
+    vmem = pl.BlockSpec(memory_space=pltpu.VMEM)
+    anywhere = pl.BlockSpec(memory_space=pl.ANY)
+    half, chunk, _ = flat_plan(width, hidden, pick_qkv.shape[1] // LANES, out_rows)
+    return pl.pallas_call(
+        functools.partial(tail_kernel, dp),
+        out_shape=(
+            jax.ShapeDtypeStruct((2 * half, LANES), BF),
+            jax.ShapeDtypeStruct((dp,) + dmod_low.shape, BF),
+            jax.ShapeDtypeStruct((dp,) + summand.shape, BF),
+            jax.ShapeDtypeStruct((dp, 16, extra.shape[1]), F32),
+        ),
+        in_specs=[anywhere] * 8 + [vmem] * 5,
+        out_specs=[vmem] * 4,
+        scratch_shapes=[
+            pltpu.VMEM((tokens, width), BF),
+            pltpu.VMEM((tokens, dgu.shape[1]), BF),
+            pltpu.VMEM((tokens, hidden), BF),
+            pltpu.VMEM((tokens, width), BF),
+            pltpu.VMEM((tokens, lanes_all), BF),
+            pltpu.VMEM((width, tokens), BF),
+            pltpu.VMEM((2 * half, LANES), BF),
+            pltpu.VMEM((2 * half, LANES), BF),
+            pltpu.VMEM((2,) + summand.shape, F32),
+            pltpu.VMEM((3,) + summand.shape, F32),
+            pltpu.SemaphoreType.DMA((8,)),
+            pltpu.SemaphoreType.DMA((2, 2, half // chunk)),
+            pltpu.SemaphoreType.DMA((2, 2, half // chunk)),
+            pltpu.SemaphoreType.DMA((3, 2)),
+            pltpu.SemaphoreType.DMA((3, 2, dp)),
+        ],
+        compiler_params=pltpu.CompilerParams(
+            collective_id=1, has_side_effects=True, vmem_limit_bytes=62 * 2**20
+        ),
+    )(a2, dgu, hid, dffn, a1, dqkv, mix, dattn, pick_qkv, pick_out, summand, dmod_low, extra)
+
+
+def finish_kernel(
+    flat_hbm, gu_hbm, down_hbm, qkv_hbm, out_hbm, flat, gate_up, down, qkv, out, load_sems, store_sems
+):
+    width, hidden = gate_up.shape[1], gate_up.shape[2]
+    part, blocks = out.shape[0], width // LANES
+    whole = part // LANES * LANES
+    rest = part - whole
+    qkv_blocks = 3 * whole // LANES + 1
+    half, _, pieces = flat_plan(width, hidden, qkv_blocks, part)
+    hidden_blocks = hidden // LANES
+    groups = (
+        [(0, b) for b in range(hidden_blocks)],
+        [(0, hidden_blocks + b) for b in range(hidden_blocks)],
+        [(1, b) for b in range(blocks)],
+        [(2, b) for b in range(qkv_blocks)],
+        [(3, b) for b in range(blocks)],
+    )
+    loads = []
+    for group in groups:
+        spans = []
+        for segment, block in group:
+            for at, _, size in pieces(segment, block):
+                if spans and spans[-1][0] + spans[-1][1] == at:
+                    spans[-1][1] += size
+                else:
+                    spans.append([at, size])
+        copies = []
+        for at, size in spans:
+            rows = pl.ds(at, size)
+            sem = load_sems.at[len(loads), len(copies)]
+            copies.append(pltpu.make_async_copy(flat_hbm.at[rows], flat.at[rows], sem))
+            copies[-1].start()
+        loads.append(copies)
+    stores = (
+        pltpu.make_async_copy(gate_up.at[0], gu_hbm.at[0], store_sems.at[0]),
+        pltpu.make_async_copy(gate_up.at[1], gu_hbm.at[1], store_sems.at[1]),
+        pltpu.make_async_copy(down, down_hbm, store_sems.at[2]),
+        pltpu.make_async_copy(qkv, qkv_hbm, store_sems.at[3]),
+        pltpu.make_async_copy(out, out_hbm, store_sems.at[4]),
+    )
+    for i, group in enumerate(groups):
+        for copy in loads[i]:
+            copy.wait()
+        for segment, block in group:
+            for at, low, size in pieces(segment, block):
+                value = flat[at : at + size, :].astype(F32)
+                rows = slice(low, low + size)
+                if segment == 0:
+                    local = block % hidden_blocks
+                    gate_up[block // hidden_blocks, rows, local * LANES : (local + 1) * LANES] = value
+                elif segment == 1:
+                    down[rows, block * LANES : (block + 1) * LANES] = value
+                elif segment == 3:
+                    out[rows, block * LANES : (block + 1) * LANES] = value
+                elif block < qkv_blocks - 1:
+                    j, local = block // (whole // LANES), block % (whole // LANES)
+                    qkv[j, rows, local * LANES : (local + 1) * LANES] = value
+                else:
+                    for j in range(3):
+                        moved = value if j == 0 else pltpu.roll(value, LANES - j * rest, 1)
+                        qkv[j, rows, whole:part] = moved[:, 0:rest]
+        stores[i].start()
+    for copy in stores:
+        copy.wait()
+
+
+def run_finish(flat, width, hidden, part):
+    anywhere = pl.BlockSpec(memory_space=pl.ANY)
+    shapes = ((2, width, hidden), (hidden, width), (3, width, part), (part, width))
+    return pl.pallas_call(
+        finish_kernel,
+        out_shape=tuple(jax.ShapeDtypeStruct(shape, F32) for shape in shapes),
+        in_specs=[anywhere],
+        out_specs=[anywhere] * 4,
+        scratch_shapes=[pltpu.VMEM(flat.shape, BF)]
+        + [pltpu.VMEM(shape, F32) for shape in shapes]
+        + [pltpu.SemaphoreType.DMA((5, 2)), pltpu.SemaphoreType.DMA((5,))],
+        compiler_params=pltpu.CompilerParams(vmem_limit_bytes=48 * 2**20),
+    )(flat)
 
 
 def time_embed(bin_row, feature_count):
@@ -639,17 +1117,18 @@
     heads = q_gain.shape[1] // HEAD_DIM
     select = jnp.asarray(head_select(heads), BF)
 
-    bins_all = lax.all_gather(bins.reshape(images), "dp", axis=0, tiled=True)
-    labels_all = lax.all_gather(labels.reshape(images), "dp", axis=0, tiled=True)
-    one_hot = labels_all[:, None] == jnp.arange(class_table.shape[0], dtype=jnp.int32)[None, :]
-    cond_all = time_embed(bins_all, width) + jnp.dot(one_hot.astype(BF), class_table, preferred_element_type=F32)
-    silu_all = jax.nn.silu(cond_all).astype(BF)
-    first = lax.axis_index("dp") * images
-    cond = lax.dynamic_slice_in_dim(cond_all, first, images, 0)
-    silu_low = lax.dynamic_slice_in_dim(silu_all, first, images, 0)
+    def condition(bin_row, label_row):
+        one_hot = label_row[:, None] == jnp.arange(class_table.shape[0], dtype=jnp.int32)[None, :]
+        picked = jnp.dot(one_hot.astype(BF), class_table, preferred_element_type=F32)
+        return time_embed(bin_row, width) + picked, one_hot
+
+    cond, _ = condition(bins.reshape(images), labels.reshape(images))
+    silu_low = jax.nn.silu(cond).astype(BF)
     mod_w = mod_weight[0]
+    part = width // 4
     columns = jnp.einsum("id,djf->ijf", silu_low, mod_w, preferred_element_type=F32)
-    modulation = lax.all_gather(columns, "tensor", axis=2, tiled=True)
+    shift = me * (part - 2 * LANES)
+    mod_cols = lax.dynamic_update_slice(jnp.zeros((images, 8, 3 * LANES), F32), columns, (0, 0, shift))
 
     order = jnp.stack([me, (me + 2) % 4, me + 1 - 2 * (me % 2), (me + 2) % 4 + 1 - 2 * (me % 2)])
     placed = jnp.take(places.reshape(images, 4, rows), order, axis=1).reshape(images * 4 * rows)
@@ -665,7 +1144,7 @@
     results = run_main(
         tokens.reshape(images, rows, width),
         velocity_grad.reshape(images, rows, width),
-        modulation,
+        mod_cols,
         angles[..., :LANES],
         angles[..., LANES:],
         wqkv,
@@ -674,35 +1153,59 @@
         down_weight[0],
         gains,
     )
-    z_rows, dx_rows, dmod, gain_sums, squares, a1, a2, d_ffn, d_attn, units, mixed, d_gu, d_qkv = results
-
-    def weight_grad(left, right):
-        return jnp.einsum("ntd,ntf->df", left, right, preferred_element_type=F32).astype(BF)
-
-    hidden = units.shape[2]
-    lanes_all = heads * LANES
-    g_gate = weight_grad(a2, d_gu[..., :hidden])
-    g_up = weight_grad(a2, d_gu[..., hidden:])
-    g_down = weight_grad(units, d_ffn)
-    g_qkv = weight_grad(a1, d_qkv).reshape(width, 3, lanes_all)
-    g_qkv = jnp.einsum("djf,ef->jde", g_qkv, select, preferred_element_type=F32).astype(BF)
-    g_out = jnp.einsum("ef,fd->ed", select, weight_grad(mixed, d_attn), preferred_element_type=F32).astype(BF)
-    g_gains = jnp.einsum("jf,ef->je", gain_sums[0:2], select.astype(F32), precision=lax.Precision.HIGHEST)
-    summed = lax.psum((jnp.stack([g_gate, g_up]), g_down, g_qkv, g_out), "dp")
-    gains_sum = lax.psum(g_gains, "dp")
-    gate_up_grad, down_grad, qkv_grad, out_grad = [item.astype(F32)[None] for item in summed]
-
-    dmod_low = lax.psum_scatter(dmod[:, 0:6].astype(BF), "tensor", scatter_dimension=2, tiled=True)
-    dmod_all = lax.all_gather(dmod_low, "dp", axis=0, tiled=True)
-    mod_grad = jnp.einsum("id,ijf->djf", silu_all, dmod_all, preferred_element_type=F32)[None]
-    grad_silu = jnp.einsum("ijf,djf->id", dmod_low, mod_w, preferred_element_type=F32)
+    z_rows, dx_rows, dmod_part, gain_sums, squares, a1, a2, d_ffn, d_attn, units, mixed, d_gu, d_qkv = results
+
+    dmod_mine = lax.dynamic_slice(dmod_part, (0, 0, shift), (images, 6, part))
+    grad_silu = jnp.einsum("ijf,djf->id", dmod_mine, mod_w, preferred_element_type=F32)
     sig = jax.nn.sigmoid(cond)
     grad_cond = grad_silu * (sig + cond * sig * (1.0 - sig))
-    spread = lax.dynamic_update_slice_in_dim(jnp.zeros((dp * images, width), F32), grad_cond, first, 0)
-    spread = lax.psum(spread, ("section", "dp", "tensor"))
-    class_grad = jnp.dot(one_hot.astype(F32).T, spread, precision=lax.Precision.HIGHEST)
-
-    square_totals = lax.psum(jnp.sum(squares[0:3], axis=1), ("dp", "tensor"))
+    summand = jnp.concatenate([grad_cond, squares], axis=0)
+    lanes_all = heads * LANES
+    numbers = jnp.stack([bins.reshape(images), labels.reshape(images)]).astype(F32)
+    extra = jnp.concatenate([gain_sums[0:2], jnp.pad(numbers, ((0, 4), (0, lanes_all - images)))], axis=0)
+
+    select_np = head_select(heads)
+    full = part // LANES * LANES
+    pick = np.zeros((3 * lanes_all, 3 * full + LANES), np.float32)
+    for j in range(3):
+        rows_j = slice(j * lanes_all, (j + 1) * lanes_all)
+        pick[rows_j, j * full : (j + 1) * full] = select_np.T[:, :full]
+        rest_at = 3 * full + j * (part - full)
+        pick[rows_j, rest_at : rest_at + part - full] = select_np.T[:, full:]
+    flat = images * 4 * rows
+    flat_grads, dmod_all, sum_all, extra_all = run_tail(
+        dp,
+        a2.reshape(flat, width),
+        d_gu.reshape(flat, d_gu.shape[2]),
+        units.reshape(flat, units.shape[2]),
+        d_ffn.reshape(flat, width),
+        a1.reshape(flat, width),
+        d_qkv.reshape(flat, d_qkv.shape[2]),
+        mixed.reshape(flat, lanes_all),
+        d_attn.reshape(flat, width),
+        jnp.asarray(pick, BF),
+        select,
+        summand,
+        dmod_part.reshape(images * 8, 3 * LANES),
+        extra,
+    )
+    gate_up_grad, down_grad, qkv_grad, out_grad = [
+        item[None] for item in run_finish(flat_grads, width, units.shape[2], part)
+    ]
+
+    gains_sum = jnp.sum(extra_all[:, 0:2], axis=0)
+    gains_sum = jnp.einsum("jf,ef->je", gains_sum, select.astype(F32), precision=lax.Precision.HIGHEST)
+    bins_all = extra_all[:, 2, :images].reshape(dp * images).astype(jnp.int32)
+    labels_all = extra_all[:, 3, :images].reshape(dp * images).astype(jnp.int32)
+    cond_all, one_hot = condition(bins_all, labels_all)
+    silu_all = jax.nn.silu(cond_all).astype(BF)
+    dmod_all = lax.dynamic_slice(
+        dmod_all.reshape(dp * images, 8, 3 * LANES), (0, 0, shift), (dp * images, 6, part)
+    )
+    mod_grad = jnp.einsum("id,ijf->djf", silu_all, dmod_all, preferred_element_type=F32)[None]
+    grad_cond_all = sum_all[:, 0:8].reshape(dp * images, width)
+    class_grad = jnp.dot(one_hot.astype(BF).T, grad_cond_all, preferred_element_type=F32)
+    square_totals = jnp.sum(extra_all[:, 8:11, 0:LANES], axis=(0, 2))
     count = images * rows * width * dp * lax.axis_size("tensor")
     stats = jnp.sqrt(square_totals / count)[None, :]
     whole = (1, micro, per_micro, rows, width)

time: 954 us -> 694 us (0.73)
  waiting for transfers between devices: 334 us -> 0 us
  Pallas kernels: 387 us -> 627 us
  blocking collectives: 92.9 us -> 0 us
  matrix products: 74.2 us -> 29.2 us
  between operations: 15 us -> 1.4 us
    psum x2 -> x0, waiting for transfers between devices: 334 us -> none  [the longest x1 280 us: per_device(): summed = lax.psum((jnp.stack([g_gate, g_up]), g_down, g_qkv, g_out), 'dp')]
    pallas_call x0 -> x2, Pallas kernels: none -> 225 us  [the longest x1 219 us: run_tail(): pl.pallas_call(functools.partial(tail_kernel, dp), out_shape=(jax.ShapeDt...]
    dot_general x10 -> x4, matrix products: 56.2 us -> 9.16 us  [the longest x1 3.99 us: per_device(): jnp.dot(one_hot.astype(BF).T, grad_cond_all, preferred_element_type=F32)]
    all_gather x2 -> x0, blocking collectives: 44.6 us -> none  [the longest x1 30.8 us: per_device(): modulation = lax.all_gather(columns, 'tensor', axis=2, tiled=True)]
    psum x2 -> x0, blocking collectives: 38.4 us -> none  [the longest x1 30 us: per_device(): square_totals = lax.psum(jnp.sum(squares[0:3], axis=1), ('dp', 'tensor'))]
    pallas_call x1, Pallas kernels: 387 us -> 402 us  [run_main(): pl.pallas_call(functools.partial(main_kernel, images, heads), out_shape=o...]
    broadcast_in_dim x6 -> x0, other arithmetic: 15.1 us -> none  [the longest x5 14.6 us: per_device(): item.astype(F32)[None]]
    unnamed x1 -> x0, blocking collectives: 9.89 us -> none
  transfers between devices with their start and end apart: 3 -> 0, of which waited for: 2 -> 0; matrix products, arithmetic and copies ran while one was open for 7% -> 0% of each run, Pallas kernels for 0% -> 0%
where the time goes in v2:
time: 694 us; the launch traced here: 686 us
  Pallas kernels  627 us (90%)
  matrix products  29.2 us (4%)
  local copies, waits for them, and re-layouts  21 us (3%)
  other arithmetic  7.11 us (1%)
    pallas_call x1, Pallas kernels, run_main(): pl.pallas_call(functools.partial(main_kernel, images, heads), out_shape=o...  402 us
    pallas_call x1, Pallas kernels, run_tail(): pl.pallas_call(functools.partial(tail_kernel, dp), out_shape=(jax.ShapeDt...  219 us

profile of v2, /device:TPU:0, one launch (start us, length us, event | category | flops | bytes accessed | tf_op | source)
XLA Modules:
  0.0 686.0 jit_solution(8486559154310832240)
XLA Ops:
  0.8 0.8 convert_add_fusion
  1.8 0.8 copy.46
  2.8 0.8 copy.52
  4.2 1.7 fusion.33.gains
  5.9 0.8 reshape.405
  7.6 2.1 convolution_add_fusion.2
  9.7 3.5 fusion.2
  14.0 1.9 convolution_convert_fusion.1.wout
  15.9 1.3 fusion.12
  17.2 1.3 convolution_add_fusion
  18.5 1.5 fusion.39
  20.1 3.8 fusion.4.wqkv
  23.9 402.0 %shard_map.239 = (bf16[8,64,1152]{2,1,0:T(8,128)(2,1)}, f32[8,64,1152]{2,1,0:T(8,128)}, bf16[8,8,384]{2,1,0:T(8,128)(2,1)}, f32[8,512]{1,0:T(8,128)}, f32[8,1152...) custom-call(bf16[8,64,1152]{2,1,0:T(8,128)(2,1)} %bitcast.92, ...), custom_call_target="tpu_custom_call" | custom-call | tf_op jit(solution)/shard_map/pallas_call | solution.py:619
  425.9 0.7 slice.32
  426.6 0.6 select_maximum_fusion.extra
  427.2 0.9 constant_dynamic-slice_fusion.1
  428.1 2.8 fusion.8
  430.9 0.7 pad_maximum_fusion.summand
  431.5 218.9 %shard_map.240 = (bf16[32256,128]{1,0:T(8,128)(2,1)}, bf16[4,64,384]{2,1,0:T(8,128)(2,1)}, bf16[4,16,1152]{2,1,0:T(8,128)(2,1)}, f32[4,16,512]{2,1,0:T(8,128)}) custom-call(bf16[2048,1152]{1,0:T(8,128)(2,1)} %bitcast.83, bf16[2048,1536]{1,0:T(8,128)(2,1)} %bitcast.80, bf16[2048,768]{1,0:T(8,128)(2,1)} %bitcast.87, bf16[2048,1152]{1,0:T(8,128)(2,1)} %bitcast.84, ...), custom_call_target="tpu_custom_call" | custom-call | tf_op jit(solution)/shard_map/pallas_call | solution.py:976
  650.4 1.1 constant_dynamic-slice_fusion
  651.5 0.8 slice_reduce_fusion.1
  652.9 0.7 convert_reduce_fusion
  653.7 0.7 add_reduce_fusion
  654.4 0.9 slice_reduce_fusion
  656.6 4.0 fusion.18
  660.6 6.5 convolution_bitcast_fusion
  667.1 6.5 shard_map.241
  673.6 2.3 copy-done.2
  675.9 6.1 copy.55
  682.1 1.0 copy.65
  683.1 1.1 copy-done.5
  684.1 1.4 copy.66
  (52 shorter events, 4.7 us)
Async XLA Ops:
  0.6 19.4 %copy-start = (bf16[1,3,1152,288]{2,3,1,0:T(8,128)(2,1)S(1)}, bf16[1,3,1152,288]{2,3,1,0:T(8,128)(2,1)}, u32[]{:S(2)}) copy-start(bf16[1,3,1152,288]{2,3,1,0:T(8,128)(2,1)} %param.23) | copy-start | bytes 5971972
  9.7 4.2 copy-start.3
  9.7 4.2 copy-start.12
  13.3 2.6 copy-start.10
  13.3 3.8 copy-start.9
  14.0 4.5 copy-start.7
  18.5 1.6 copy-start.13
  23.9 402.7 %copy-start.11 = (f32[2,8]{1,0:T(2,128)S(1)}, f32[2,8]{1,0:T(2,128)}, u32[]{:S(2)}) copy-start(f32[2,8]{1,0:T(2,128)} %add_convert_fusion) | copy-start | bytes 196
  425.9 5.0 copy-start.8
  431.5 223.8 %copy-start.4 = (bf16[288,512]{1,0:T(8,128)(2,1)S(1)}, bf16[288,512]{1,0:T(8,128)(2,1)}, u32[]{:S(2)}) copy-start(bf16[288,512]{1,0:T(8,128)(2,1)} %constant.102.clone.pick_out) | copy-start | bytes 884740
  673.6 2.3 copy-start.2
  675.9 6.1 copy-start.6
  682.0 2.1 copy-start.5
  682.0 3.5 copy-start.1

commit v3 on v2

--- a/solution.py
+++ b/solution.py
@@ -18,6 +18,31 @@
 BF = jnp.bfloat16
 F32 = jnp.float32
 SCALE = HEAD_DIM**-0.5
+
+KEEP, SLOTS, PACK = 2, 4, 4
+LENT = 3
+ORDERS = (
+    (
+        0, 1, 2, 8, 3, 16, 9, 24, 4, 17, 10, 32, 25, 18, 40, 11, 26, 48,
+        33, 56, 19, 34, 41, 27, 49, 64, 12, 42, 57, 50, 35, 58, 65, 20, 5, 43,
+        28, 66, 51, 59, 13, 36, 6, 21, 67, 44, 29, 52, 60, 37, 7, 68, 14, 22,
+        45, 30, 15, 53, 61, 23, 38, 31, 69, 46, 39, 54, 47, 62, 70, 55, 63, 71,
+        72, 73, 80, 88, 81, 96, 89, 97, 104, 105, 112, 113, 120, 74, 121, 82, 128, 90,
+        98, 75, 106, 136, 83, 129, 91, 114, 76, 99, 122, 84, 107, 130, 92, 100, 115, 137,
+        77, 123, 85, 78, 108, 93, 86, 138, 101, 94, 79, 116, 102, 131, 124, 87, 109, 110,
+        95, 139, 117, 103, 132, 125, 111, 133, 118, 140, 126, 119, 141, 134, 127, 142, 135, 143,
+    ),
+    (
+        72, 73, 74, 75, 76, 77, 80, 78, 0, 8, 1, 16, 81, 9, 24, 2, 82, 83,
+        84, 17, 32, 25, 10, 18, 3, 40, 33, 85, 88, 86, 11, 26, 96, 19, 4, 34,
+        41, 48, 27, 89, 12, 104, 42, 97, 20, 35, 49, 112, 5, 28, 90, 56, 105, 79,
+        98, 43, 120, 91, 113, 36, 13, 128, 121, 106, 6, 44, 21, 7, 129, 92, 136, 14,
+        29, 87, 99, 114, 100, 15, 22, 137, 64, 30, 122, 37, 107, 23, 38, 50, 57, 45,
+        108, 115, 130, 58, 31, 93, 46, 123, 116, 138, 101, 94, 131, 39, 124, 102, 65, 139,
+        109, 132, 51, 47, 110, 66, 95, 59, 52, 117, 140, 118, 103, 125, 67, 111, 133, 126,
+        119, 60, 53, 134, 141, 61, 127, 142, 68, 54, 135, 69, 62, 55, 63, 143, 70, 71,
+    ),
+)
 
 
 def lane_of():
@@ -64,6 +89,15 @@
 
 def dot_tn(a, b):
     return lax.dot_general(a, b, (((0,), (0,)), ((), ())), preferred_element_type=F32)
+
+
+def order_words(order, base):
+    words = []
+    for at in range(0, len(order), PACK):
+        words.append(sum(entry * base**i for i, entry in enumerate(order[at : at + PACK])))
+    while len(words) & (len(words) - 1):
+        words.append(0)
+    return words
 
 
 def chunks_of(size, width):
@@ -110,8 +144,8 @@
     recv_a,
     send_y,
     recv_y,
-    dx1s,
     mix_st,
+    units_st,
     hid_st,
     dgu_st,
     dqkv_st,
@@ -228,43 +262,43 @@
             gather(which, buf, n, kind).wait_send()
 
     def to_sibling(which, n):
-        kind = which % 2
         return remote(
-            send_a.at[kind],
-            recv_a.at[kind, lax.rem(n, 2)],
+            send_a.at[which, lax.rem(n, KEEP)],
+            recv_a.at[which, lax.rem(n, SLOTS)],
             rs_sems.at[which, 0, n],
             rs_sems.at[which, 1, n],
             {"tensor": sib},
         )
 
     def over_y(which, n):
-        kind = which % 2
         return remote(
-            send_y.at[kind],
-            recv_y.at[kind, lax.rem(n, 2)],
+            send_y.at[which, lax.rem(n, KEEP)],
+            recv_y.at[which, lax.rem(n, SLOTS)],
             rs_sems.at[which, 2, n],
             rs_sems.at[which, 3, n],
             {"tensor": across},
         )
 
-    def scatter_put(which, at, size, values):
-        kind = which % 2
-        keep[kind, :, pl.ds(at, size)] = values[0 : 2 * rows]
-        send_a[kind, :, pl.ds(at, size)] = values[2 * rows : 4 * rows].astype(BF)
+    def scatter_put(which, n, at, size, values):
+        kind, own = which, lax.rem(n, KEEP)
+        keep[kind, own, :, pl.ds(at, size)] = values[0 : 2 * rows]
+        send_a[kind, own, :, pl.ds(at, size)] = values[2 * rows : 4 * rows].astype(BF)
 
     def scatter_start(which, n):
         to_sibling(which, n).start()
 
     def scatter_middle(which, n):
-        kind, slot = which % 2, lax.rem(n, 2)
+        kind, own, slot = which, lax.rem(n, KEEP), lax.rem(n, SLOTS)
         to_sibling(which, n).wait()
-        send_y[kind] = (keep[kind, rows : 2 * rows] + recv_a[kind, slot, rows : 2 * rows].astype(F32)).astype(BF)
+        theirs = recv_a[kind, slot, rows : 2 * rows].astype(F32)
+        send_y[kind, own] = (keep[kind, own, rows : 2 * rows] + theirs).astype(BF)
         over_y(which, n).start()
 
     def scatter_end(which, n):
-        kind, slot = which % 2, lax.rem(n, 2)
+        kind, own, slot = which, lax.rem(n, KEEP), lax.rem(n, SLOTS)
         over_y(which, n).wait()
-        return keep[kind, 0:rows] + recv_a[kind, slot, 0:rows].astype(F32) + recv_y[kind, slot].astype(F32)
+        mine = keep[kind, own, 0:rows] + recv_a[kind, slot, 0:rows].astype(F32)
+        return mine + recv_y[kind, slot].astype(F32)
 
     def z_copy(n):
         return remote(zout.at[n], xin.at[n], zx_sems.at[0, n], zx_sems.at[1, n], {"section": other})
@@ -332,9 +366,9 @@
         c, s = cosine[n], sine[n]
         for pair in range(heads // 2):
             span = pl.ds(pair * 2 * LANES, 2 * LANES)
-            q2 = dot(a1, wqkv[0, :, span])
-            k2 = dot(a1, wqkv[1, :, span])
-            v2 = dot(a1, wqkv[2, :, span]).astype(BF)
+            q2 = dot_nt(a1, wqkv[0, span, :])
+            k2 = dot_nt(a1, wqkv[1, span, :])
+            v2 = dot_nt(a1, wqkv[2, span, :]).astype(BF)
             for half in range(2):
                 at = (pair * 2 + half) * LANES
                 cut = slice(half * LANES, (half + 1) * LANES)
@@ -344,7 +378,7 @@
                 mix_st[:, at : at + LANES] = dot(probs, v2[:, cut]).astype(BF)
         mixed = mix_st[...]
         for at, size in wide:
-            scatter_put(0, at, size, dot(mixed, wout[:, pl.ds(at, size)]))
+            scatter_put(0, n, at, size, dot(mixed, wout[:, pl.ds(at, size)]))
         scatter_start(0, n)
         out_copy(5, n).start()
         out_copy(0, n).start()
@@ -360,16 +394,19 @@
         gather_start(1, a2f, n)
 
     def ffn_compute(n):
-        gather_wait(1, a2f, n)
+        @pl.when(enc)
+        def _():
+            gather_wait(1, a2f, n)
+
         a2 = a2f[n]
         for at, size in chunks_of(hidden, 256):
             span = pl.ds(at, size)
             gate_val = dot(a2, wgu[0, :, span])
             up_val = dot(a2, wgu[1, :, span])
-            hid_st[:, span] = (gate_val * jax.nn.sigmoid(gate_val) * up_val).astype(BF)
-        units = hid_st[...]
+            units_st[:, span] = (gate_val * jax.nn.sigmoid(gate_val) * up_val).astype(BF)
+        units = units_st[...]
         for at, size in wide:
-            scatter_put(1, at, size, dot(units, wdn[:, pl.ds(at, size)]))
+            scatter_put(1, n, at, size, dot(units, wdn[:, pl.ds(at, size)]))
         scatter_start(1, n)
         out_copy(1, n).start()
         gather_drain(1, a2f, n)
@@ -385,6 +422,15 @@
         def _():
             z_copy(n).start()
 
+        @pl.when(dec)
+        def _():
+            dmod[n, 5:6, :] = column_sum(din[n].astype(F32) * feedfwd)
+            send_dmod(n)
+
+    def send_dmod(n):
+        for k in range(3):
+            dmod_copy(k, n).start()
+
     def ffn_grad_in(n):
         @pl.when(enc)
         def _():
@@ -393,9 +439,16 @@
         grad = din[n].astype(F32)
         dffn[n, 0:rows, :] = (mod_row(n, 5) * grad).astype(BF)
         gather_start(2, dffn, n)
-        dmod[n, 5:6, :] = column_sum(grad * ffns[n].astype(F32))
+
+        @pl.when(enc)
+        def _():
+            dmod[n, 5:6, :] = column_sum(grad * ffns[n].astype(F32))
 
     def ffn_grad_compute(n):
+        @pl.when(dec)
+        def _():
+            gather_wait(1, a2f, n)
+
         gather_wait(2, dffn, n)
         staged_ready(4, n)
         staged_ready(6, n)
@@ -415,7 +468,7 @@
         d_up = dgu_st[:, hidden : 2 * hidden]
         for at, size in wide:
             span = pl.ds(at, size)
-            scatter_put(2, at, size, dot_nt(d_gate, wgu[0, span, :]) + dot_nt(d_up, wgu[1, span, :]))
+            scatter_put(2, n, at, size, dot_nt(d_gate, wgu[0, span, :]) + dot_nt(d_up, wgu[1, span, :]))
         scatter_start(2, n)
         out_copy(4, n).start()
         out_copy(6, n).start()
@@ -426,7 +479,7 @@
         d_a2 = scatter_end(2, n)
         grad, d_shift, d_scale = norm_back(x1s[n], d_a2, mod_row(n, 4))
         grad = grad + din[n].astype(F32)
-        dx1s[lax.rem(n, 2)] = grad
+        dxout[n] = grad
         dattn[n, 0:rows, :] = (mod_row(n, 2) * grad).astype(BF)
         gather_start(3, dattn, n)
         dmod[n, 2:3, :] = column_sum(grad * attns[n].astype(F32))
@@ -442,9 +495,9 @@
         lanes_all = heads * LANES
         for pair in range(heads // 2):
             span = pl.ds(pair * 2 * LANES, 2 * LANES)
-            q2 = dot(a1, wqkv[0, :, span])
-            k2 = dot(a1, wqkv[1, :, span])
-            v2 = dot(a1, wqkv[2, :, span]).astype(BF)
+            q2 = dot_nt(a1, wqkv[0, span, :])
+            k2 = dot_nt(a1, wqkv[1, span, :])
+            v2 = dot_nt(a1, wqkv[2, span, :]).astype(BF)
             d_mix2 = dot_nt(grad, wout[span, :]).astype(BF)
             for half in range(2):
                 at = (pair * 2 + half) * LANES
@@ -472,10 +525,10 @@
                 dqkv_st[:, 2 * lanes_all + at : 2 * lanes_all + at + LANES] = d_v.astype(BF)
         for at, size in wide:
             span = pl.ds(at, size)
-            total = dot_nt(dqkv_st[:, 0:lanes_all], wqkv[0, span, :])
-            total += dot_nt(dqkv_st[:, lanes_all : 2 * lanes_all], wqkv[1, span, :])
-            total += dot_nt(dqkv_st[:, 2 * lanes_all : 3 * lanes_all], wqkv[2, span, :])
-            scatter_put(3, at, size, total)
+            total = dot(dqkv_st[:, 0:lanes_all], wqkv[0, :, span])
+            total += dot(dqkv_st[:, lanes_all : 2 * lanes_all], wqkv[1, :, span])
+            total += dot(dqkv_st[:, 2 * lanes_all : 3 * lanes_all], wqkv[2, :, span])
+            scatter_put(3, n, at, size, total)
         scatter_start(3, n)
         out_copy(7, n).start()
         out_copy(3, n).start()
@@ -484,7 +537,7 @@
     def block_grad_out(n):
         d_a1 = scatter_end(3, n)
         grad, d_shift, d_scale = norm_back(xin[n].astype(F32), d_a1, mod_row(n, 1))
-        grad = grad + dx1s[lax.rem(n, 2)]
+        grad = grad + dxout[n]
         dxout[n] = grad
         dmod[n, 0:1, :] = d_shift
         dmod[n, 1:2, :] = d_scale
@@ -494,43 +547,66 @@
             xin[n] = grad.astype(BF)
             dz_copy(n).start()
 
-        for k in range(3):
-            dmod_copy(k, n).start()
-
-    def stage(n, body):
-        @pl.when((n >= 0) & (n < images))
-        def _():
-            body(n)
-
-    def forward_step(step, carry):
-        j = step - 1
-        stage(j, attn_compute)
-        stage(j - 1, lambda n: gather_relay(1, a2f, n))
-        stage(j - 2, block_out)
-        stage(j, lambda n: scatter_middle(0, n))
-        stage(j + 1, attn_in)
-        stage(j - 1, ffn_compute)
-        stage(j + 1, lambda n: gather_relay(0, a1f, n))
-        stage(j, ffn_in)
-        stage(j - 1, lambda n: scatter_middle(1, n))
+        @pl.when(enc)
+        def _():
+            send_dmod(n)
+
+    works = (
+        attn_in,
+        lambda n: gather_relay(0, a1f, n),
+        attn_compute,
+        lambda n: scatter_middle(0, n),
+        ffn_in,
+        lambda n: gather_relay(1, a2f, n),
+        ffn_compute,
+        lambda n: scatter_middle(1, n),
+        block_out,
+        ffn_grad_in,
+        lambda n: gather_relay(2, dffn, n),
+        ffn_grad_compute,
+        lambda n: scatter_middle(2, n),
+        attn_grad_in,
+        lambda n: gather_relay(3, dattn, n),
+        attn_grad_compute,
+        lambda n: scatter_middle(3, n),
+        block_grad_out,
+    )
+
+    def run_work(work, n, low, high):
+        if high - low == 1:
+            works[low](n)
+            return
+        middle = (low + high) // 2
+
+        @pl.when(work < middle)
+        def _():
+            run_work(work, n, low, middle)
+
+        @pl.when(work >= middle)
+        def _():
+            run_work(work, n, middle, high)
+
+    base = len(works) * images
+    tables = [order_words(order, base) for order in ORDERS]
+
+    def entry_of(i):
+        rest, values = i, [low + section * (high - low) for low, high in zip(*tables)]
+        while len(values) > 1:
+            bit, rest = lax.rem(rest, 2), lax.div(rest, 2)
+            values = [low + bit * (high - low) for low, high in zip(values[0::2], values[1::2])]
+        return values[0]
+
+    def word_step(i, carry):
+        def work_step(_, word):
+            entry, word = lax.rem(word, base), lax.div(word, base)
+            work, n = lax.div(entry, images), lax.rem(entry, images)
+            run_work(work, n, 0, len(works))
+            return word
+
+        lax.fori_loop(0, PACK, work_step, entry_of(i))
         return carry
 
-    lax.fori_loop(0, images + 3, forward_step, 0)
-
-    def backward_step(step, carry):
-        j = step - 1
-        stage(j, ffn_grad_compute)
-        stage(j - 1, lambda n: gather_relay(3, dattn, n))
-        stage(j - 2, block_grad_out)
-        stage(j, lambda n: scatter_middle(2, n))
-        stage(j + 1, ffn_grad_in)
-        stage(j - 1, attn_grad_compute)
-        stage(j + 1, lambda n: gather_relay(2, dffn, n))
-        stage(j, attn_grad_in)
-        stage(j - 1, lambda n: scatter_middle(3, n))
-        return carry
-
-    lax.fori_loop(0, images + 3, backward_step, 0)
+    lax.fori_loop(0, base // PACK, word_step, 0)
 
     for which in (4, 5, 6, 7):
         out_copy(which, images - 1).wait()
@@ -594,13 +670,13 @@
         pltpu.VMEM((images, rows, width), F32),
         pltpu.VMEM((images, rows, width), BF),
         pltpu.VMEM((images, rows, width), BF),
-        pltpu.VMEM((2, 2 * rows, width), F32),
-        pltpu.VMEM((2, 2 * rows, width), BF),
-        pltpu.VMEM((2, 2, 2 * rows, width), BF),
-        pltpu.VMEM((2, rows, width), BF),
-        pltpu.VMEM((2, 2, rows, width), BF),
-        pltpu.VMEM((2, rows, width), F32),
+        pltpu.VMEM((4, KEEP, 2 * rows, width), F32),
+        pltpu.VMEM((4, KEEP, 2 * rows, width), BF),
+        pltpu.VMEM((4, SLOTS, 2 * rows, width), BF),
+        pltpu.VMEM((4, KEEP, rows, width), BF),
+        pltpu.VMEM((4, SLOTS, rows, width), BF),
         pltpu.VMEM((tokens, lanes_all), BF),
+        pltpu.VMEM((tokens, hidden), BF),
         pltpu.VMEM((tokens, hidden), BF),
         pltpu.VMEM((tokens, 2 * hidden), BF),
         pltpu.VMEM((tokens, 3 * lanes_all), BF),
@@ -628,38 +704,21 @@
     )(tok, vel, mod_cols, cosine, sine, wqkv, wout, wgu, wdn, gains)
 
 
-def flat_plan(width, hidden, qkv_blocks, out_rows):
-    gu_blocks, blocks = 2 * hidden // LANES, width // LANES
-    half_down = blocks * hidden // 2
-    qkv_cut, out_cut = qkv_blocks // 2, blocks - 1
-    first = (gu_blocks // 2) * width + half_down + qkv_cut * width + out_cut * out_rows
-    second = (gu_blocks - gu_blocks // 2) * width + half_down + (qkv_blocks - qkv_cut) * width
-    second += (blocks - out_cut) * out_rows
-    chunk = width // 2
-    half = -(-max(first, second) // chunk) * chunk
+def flat_plan(width, hidden, part):
+    blocks = width // LANES
+    segments = ((2 * hidden // LANES, width), (blocks, hidden), (blocks, 3 * part), (blocks, part))
+    halves = [count * rows // 2 for count, rows in segments]
+    half, chunk = sum(halves), width // 2
+    assert half % chunk == 0
 
     def pieces(segment, block):
-        if segment == 0:
-            cut = gu_blocks // 2
-            return [(block * width if block < cut else half + (block - cut) * width, 0, width)]
-        at = (gu_blocks // 2) * width
-        at_second = half + (gu_blocks - gu_blocks // 2) * width
-        if segment == 1:
-            low, high = block * hidden, (block + 1) * hidden
-            if high <= half_down:
-                return [(at + low, 0, hidden)]
-            if low >= half_down:
-                return [(at_second + low - half_down, 0, hidden)]
-            return [(at + low, 0, half_down - low), (at_second, half_down - low, high - half_down)]
-        at, at_second = at + half_down, at_second + half_down
-        if segment == 2:
-            if block < qkv_cut:
-                return [(at + block * width, 0, width)]
-            return [(at_second + (block - qkv_cut) * width, 0, width)]
-        at, at_second = at + qkv_cut * width, at_second + (qkv_blocks - qkv_cut) * width
-        if block < out_cut:
-            return [(at + block * out_rows, 0, out_rows)]
-        return [(at_second + (block - out_cut) * out_rows, 0, out_rows)]
+        rows, cut, at = segments[segment][1], halves[segment], sum(halves[:segment])
+        low, high = block * rows, (block + 1) * rows
+        if high <= cut:
+            return [(at + low, 0, rows)]
+        if low >= cut:
+            return [(half + at + low - cut, 0, rows)]
+        return [(at + low, 0, cut - low), (half + at, cut - low, high - cut)]
 
     return half, chunk, pieces
 
@@ -674,8 +733,7 @@
     dqkv_hbm,
     mix_hbm,
     dattn_hbm,
-    pick_qkv,
-    pick_out,
+    pick,
     summand,
     dmod_low,
     extra,
@@ -687,7 +745,6 @@
     right_a,
     left_b,
     right_b,
-    left_c,
     turned,
     own,
     arrived,
@@ -698,16 +755,21 @@
     total_sems,
     sum_sems,
     all_sems,
+    x_part_sems,
+    x_total_sems,
+    here,
 ):
     section = lax.axis_index("section")
     place = lax.axis_index("dp")
     me = lax.axis_index("tensor")
     sib = me + 1 - 2 * lax.rem(me, 2)
     across = lax.rem(me + 2, 4)
+    enc, dec = section == 0, section == 1
     width, hidden = left_a.shape[1], left_b.shape[1]
-    qkv_blocks, out_rows = pick_qkv.shape[1] // LANES, pick_out.shape[0]
-    half, chunk, pieces = flat_plan(width, hidden, qkv_blocks, out_rows)
-    count = half // chunk
+    part, lanes_all = pick.shape
+    half, chunk, pieces = flat_plan(width, hidden, part)
+    whole = half // chunk
+    count = jnp.where(enc, whole - LENT, whole + LENT)
 
     loads = [
         pltpu.make_async_copy(src, dst, load_sems.at[i])
@@ -717,29 +779,36 @@
                 (dgu_hbm, right_a),
                 (hid_hbm, left_b),
                 (dffn_hbm, right_b),
-                (mix_hbm, left_c),
+                (mix_hbm, left_b.at[:, pl.ds(0, lanes_all)]),
                 (a1_hbm, left_a),
                 (dqkv_hbm, right_a),
                 (dattn_hbm, right_b),
             )
         )
     ]
-    for i in range(5):
+    for i in range(4):
         loads[i].start()
 
     barrier = pltpu.get_barrier_semaphore()
-    for where in ({"tensor": sib}, {"tensor": across}, {"section": 1 - section}):
+    for where in ({"tensor": sib}, {"tensor": across}):
         pl.semaphore_signal(barrier, inc=1, device_id=where, device_id_type=MESH)
+
+    @pl.when(dec)
+    def _():
+        pl.semaphore_signal(barrier, inc=1, device_id={"section": 0}, device_id_type=MESH)
+
     for k in range(1, dp):
         pl.semaphore_signal(barrier, inc=1, device_id={"dp": lax.rem(place + k, dp)}, device_id_type=MESH)
 
-    def put(segment, block, value):
+    def put(segment, block, first, value):
         for at, low, size in pieces(segment, block):
-            own[at : at + size, :] = value[low : low + size].astype(BF)
-
-    def put_pair(segment, block, value):
+            begin, end = max(low, first), min(low + size, first + value.shape[0])
+            if begin < end:
+                own[at + begin - low : at + end - low, :] = value[begin - first : end - first].astype(BF)
+
+    def put_wide(segment, block, first, value):
         for i in range(value.shape[1] // LANES):
-            put(segment, block + i, value[:, i * LANES : (i + 1) * LANES])
+            put(segment, block + i, first, value[:, i * LANES : (i + 1) * LANES])
 
     def turn_left(ref):
         tokens, cols = ref.shape
@@ -749,52 +818,48 @@
     def gate_up_blocks(*blocks):
         for block in blocks:
             value = dot(turned[...], right_a[:, block * LANES : (block + 2) * LANES])
-            put_pair(0, block, value)
-
-    def qkv_tiles(*tiles):
-        for tile in tiles:
-            value = dot_tn(left_a[:, tile * LANES : (tile + 1) * LANES], right_a[...]).astype(BF)
-            value = dot(value, pick_qkv[...])
-            for block in range(qkv_blocks):
-                (at, _, _), = pieces(2, block)
-                cut = slice(block * LANES, (block + 1) * LANES)
-                own[at + tile * LANES : at + (tile + 1) * LANES, :] = value[:, cut].astype(BF)
+            put_wide(0, block, 0, value)
+
+    def qkv_heads(*pairs):
+        kept = 2 * HEAD_DIM
+        for pair in pairs:
+            value = dot_tn(right_a[:, pair * 2 * LANES : (pair + 1) * 2 * LANES], left_a[...]).astype(BF)
+            put_wide(2, 0, pair * kept, dot(pick[0:kept, 0 : 2 * LANES], value))
 
     def portion(i):
-        gu_blocks, tiles = right_a.shape[1] // LANES, width // LANES
-        gu_blocks = 2 * hidden // LANES
+        tiles, gu_half = width // LANES, hidden // LANES
+        pairs = 3 * lanes_all // (2 * LANES)
         if i == 0:
             loads[0].wait()
             turn_left(left_a)
             loads[5].start()
             loads[1].wait()
-            gate_up_blocks(0, gu_blocks // 2)
+            gate_up_blocks(0, gu_half)
         elif i == 1:
-            gate_up_blocks(2, gu_blocks // 2 + 2)
+            gate_up_blocks(2, gu_half + 2)
         elif i == 2:
-            gate_up_blocks(*range(4, gu_blocks // 2, 2), *range(gu_blocks // 2 + 4, gu_blocks, 2))
+            gate_up_blocks(*range(4, gu_half, 2), *range(gu_half + 4, 2 * gu_half, 2))
             loads[6].start()
         elif i == 3:
             loads[2].wait()
             turn_left(left_b)
+            loads[4].start()
             loads[3].wait()
             for block in range(0, tiles, 2):
                 cut = slice(block * LANES, min(width, (block + 2) * LANES))
-                put_pair(1, block, dot(turned[0:hidden, :], right_b[:, cut]))
+                put_wide(1, block, 0, dot(turned[0:hidden, :], right_b[:, cut]))
             loads[7].start()
-        elif i in (4, 5, 6):
-            if i == 4:
-                loads[5].wait()
-                loads[6].wait()
-            third = -(-tiles // 3)
-            qkv_tiles(*range((i - 4) * third, min(tiles, (i - 3) * third)))
-        elif i == 7:
+        elif i == 4:
+            loads[5].wait()
+            loads[6].wait()
+            qkv_heads(*range(0, pairs // 2))
+        elif i == 5:
+            qkv_heads(*range(pairs // 2, pairs))
+        elif i == 6:
             loads[4].wait()
             loads[7].wait()
-            value = dot(pick_out[...], dot_tn(left_c[...], right_b[...]).astype(BF))
-            put_pair(3, 0, value)
-            (at, _, size), = pieces(3, tiles - 1)
-            own[at + size :, :] = jnp.zeros((2 * half - at - size, LANES), BF)
+            value = dot(pick[...], dot_tn(left_b[:, 0:lanes_all], right_b[...]).astype(BF))
+            put_wide(3, 0, 0, value)
 
     def along(direction, onward):
         step = 1 if (direction == 0) == onward else dp - 1
@@ -804,7 +869,26 @@
         return place if direction == 0 else dp - 1 - place
 
     def rows_of(direction, c):
-        return pl.ds(pl.multiple_of(direction * half + c * chunk, chunk), chunk)
+        lent = 2 * half + (direction * LENT + c - whole) * chunk
+        return pl.ds(pl.multiple_of(jnp.where(c < whole, direction * half + c * chunk, lent), chunk), chunk)
+
+    def lent_copy(ref, sems, direction, i, to_decoder):
+        mine = rows_of(direction, whole - LENT + i)
+        theirs = rows_of(direction, whole + i)
+        return pltpu.make_async_remote_copy(
+            src_ref=ref.at[mine if to_decoder else theirs],
+            dst_ref=ref.at[theirs if to_decoder else mine],
+            send_sem=sems.at[direction, 0, i],
+            recv_sem=sems.at[direction, 1, i],
+            device_id={"section": 1 if to_decoder else 0},
+            device_id_type=MESH,
+        )
+
+    def lent_part(direction, i):
+        return lent_copy(own, x_part_sems, direction, i, True)
+
+    def lent_total(direction, i):
+        return lent_copy(totals, x_total_sems, direction, i, False)
 
     def part_copy(direction, c):
         return pltpu.make_async_remote_copy(
@@ -830,6 +914,10 @@
         begins, ends = behind(direction) == 0, behind(direction) == dp - 1
         rows = rows_of(direction, c)
 
+        @pl.when(c >= whole)
+        def _():
+            lent_part(direction, c - whole).wait_recv()
+
         @pl.when(begins)
         def _():
             part_copy(direction, c).start()
@@ -860,6 +948,10 @@
             def _():
                 total_copy(direction, c).start()
 
+        @pl.when(c >= whole)
+        def _():
+            lent_total(direction, c - whole).start()
+
     skew = 2
 
     def chunk_step(step):
@@ -876,6 +968,12 @@
             @pl.when((u >= 0) & (u < count))
             def _():
                 pass_total(direction, u)
+
+        for i in range(4):
+
+            @pl.when(step == jnp.where(enc, 4, 12) + i)
+            def _():
+                small(i)
 
     def sum_copy(which):
         where = ({"section": 1 - section}, {"tensor": sib}, {"tensor": across})[which]
@@ -908,6 +1006,11 @@
             dmod_all[place] = dmod_low[...]
             for k in range(1, dp):
                 all_copy(0, k, True).start()
+
+            @pl.when(dec)
+            def _():
+                pl.semaphore_wait(here, 1)
+
             sum_copy(0).start()
         elif step == 1:
             sum_copy(0).wait()
@@ -933,17 +1036,46 @@
                 all_copy(2, k, True).start()
 
     portion(0)
-    pl.semaphore_wait(barrier, 3 + dp - 1)
-    for step in range(8):
+    pl.semaphore_wait(barrier, jnp.where(enc, dp + 2, dp + 1))
+
+    @pl.when(enc)
+    def _():
+        pl.semaphore_signal(here, inc=1, device_id={"section": 1}, device_id_type=MESH)
+
+    for step in range(6):
         chunk_step(step)
-        small(step)
         portion(step + 1)
+
+    def lend(i, carry):
+        for direction in range(2):
+            lent_part(direction, i).start()
+        return carry
+
+    @pl.when(enc)
+    def _():
+        lax.fori_loop(0, LENT, lend, 0)
 
     def later_step(step, carry):
         chunk_step(step)
         return carry
 
-    lax.fori_loop(8, count + 2 * skew * (dp - 1), later_step, 0)
+    lax.fori_loop(6, whole + LENT + 2 * skew * (dp - 1), later_step, 0)
+
+    def lent_back(i, carry):
+        for direction in range(2):
+
+            @pl.when(enc)
+            def _():
+                lent_part(direction, i).wait_send()
+                lent_total(direction, i).wait_recv()
+
+            @pl.when(dec)
+            def _():
+                lent_total(direction, i).wait_send()
+
+        return carry
+
+    lax.fori_loop(0, LENT, lent_back, 0)
 
     for which in range(3):
         for k in range(1, dp):
@@ -966,61 +1098,59 @@
     lax.fori_loop(0, count, drain, 0)
 
 
-def run_tail(dp, a2, dgu, hid, dffn, a1, dqkv, mix, dattn, pick_qkv, pick_out, summand, dmod_low, extra):
+def run_tail(dp, a2, dgu, hid, dffn, a1, dqkv, mix, dattn, pick, summand, dmod_low, extra):
     tokens, width = a2.shape
     hidden = hid.shape[1]
-    out_rows, lanes_all = pick_out.shape
     vmem = pl.BlockSpec(memory_space=pltpu.VMEM)
     anywhere = pl.BlockSpec(memory_space=pl.ANY)
-    half, chunk, _ = flat_plan(width, hidden, pick_qkv.shape[1] // LANES, out_rows)
+    half, chunk, _ = flat_plan(width, hidden, pick.shape[0])
+    flat_rows, chunks = 2 * (half + LENT * chunk), half // chunk + LENT
     return pl.pallas_call(
         functools.partial(tail_kernel, dp),
         out_shape=(
-            jax.ShapeDtypeStruct((2 * half, LANES), BF),
+            jax.ShapeDtypeStruct((flat_rows, LANES), BF),
             jax.ShapeDtypeStruct((dp,) + dmod_low.shape, BF),
             jax.ShapeDtypeStruct((dp,) + summand.shape, BF),
             jax.ShapeDtypeStruct((dp, 16, extra.shape[1]), F32),
         ),
-        in_specs=[anywhere] * 8 + [vmem] * 5,
+        in_specs=[anywhere] * 8 + [vmem] * 4,
         out_specs=[vmem] * 4,
         scratch_shapes=[
             pltpu.VMEM((tokens, width), BF),
             pltpu.VMEM((tokens, dgu.shape[1]), BF),
             pltpu.VMEM((tokens, hidden), BF),
             pltpu.VMEM((tokens, width), BF),
-            pltpu.VMEM((tokens, lanes_all), BF),
             pltpu.VMEM((width, tokens), BF),
-            pltpu.VMEM((2 * half, LANES), BF),
-            pltpu.VMEM((2 * half, LANES), BF),
+            pltpu.VMEM((flat_rows, LANES), BF),
+            pltpu.VMEM((flat_rows, LANES), BF),
             pltpu.VMEM((2,) + summand.shape, F32),
             pltpu.VMEM((3,) + summand.shape, F32),
             pltpu.SemaphoreType.DMA((8,)),
-            pltpu.SemaphoreType.DMA((2, 2, half // chunk)),
-            pltpu.SemaphoreType.DMA((2, 2, half // chunk)),
+            pltpu.SemaphoreType.DMA((2, 2, chunks)),
+            pltpu.SemaphoreType.DMA((2, 2, chunks)),
             pltpu.SemaphoreType.DMA((3, 2)),
             pltpu.SemaphoreType.DMA((3, 2, dp)),
+            pltpu.SemaphoreType.DMA((2, 2, LENT)),
+            pltpu.SemaphoreType.DMA((2, 2, LENT)),
+            pltpu.SemaphoreType.REGULAR,
         ],
         compiler_params=pltpu.CompilerParams(
             collective_id=1, has_side_effects=True, vmem_limit_bytes=62 * 2**20
         ),
-    )(a2, dgu, hid, dffn, a1, dqkv, mix, dattn, pick_qkv, pick_out, summand, dmod_low, extra)
+    )(a2, dgu, hid, dffn, a1, dqkv, mix, dattn, pick, summand, dmod_low, extra)
 
 
 def finish_kernel(
     flat_hbm, gu_hbm, down_hbm, qkv_hbm, out_hbm, flat, gate_up, down, qkv, out, load_sems, store_sems
 ):
     width, hidden = gate_up.shape[1], gate_up.shape[2]
-    part, blocks = out.shape[0], width // LANES
-    whole = part // LANES * LANES
-    rest = part - whole
-    qkv_blocks = 3 * whole // LANES + 1
-    half, _, pieces = flat_plan(width, hidden, qkv_blocks, part)
-    hidden_blocks = hidden // LANES
+    part, blocks, hidden_blocks = out.shape[0], width // LANES, hidden // LANES
+    _, _, pieces = flat_plan(width, hidden, part)
     groups = (
         [(0, b) for b in range(hidden_blocks)],
         [(0, hidden_blocks + b) for b in range(hidden_blocks)],
         [(1, b) for b in range(blocks)],
-        [(2, b) for b in range(qkv_blocks)],
+        [(2, b) for b in range(blocks)],
         [(3, b) for b in range(blocks)],
     )
     loads = []
@@ -1053,20 +1183,16 @@
             for at, low, size in pieces(segment, block):
                 value = flat[at : at + size, :].astype(F32)
                 rows = slice(low, low + size)
+                cols = slice(block * LANES, (block + 1) * LANES)
                 if segment == 0:
                     local = block % hidden_blocks
                     gate_up[block // hidden_blocks, rows, local * LANES : (local + 1) * LANES] = value
                 elif segment == 1:
-                    down[rows, block * LANES : (block + 1) * LANES] = value
-                elif segment == 3:
-                    out[rows, block * LANES : (block + 1) * LANES] = value
-                elif block < qkv_blocks - 1:
-                    j, local = block // (whole // LANES), block % (whole // LANES)
-                    qkv[j, rows, local * LANES : (local + 1) * LANES] = value
+                    down[rows, cols] = value
+                elif segment == 2:
+                    qkv[rows, cols] = value
                 else:
-                    for j in range(3):
-                        moved = value if j == 0 else pltpu.roll(value, LANES - j * rest, 1)
-                        qkv[j, rows, whole:part] = moved[:, 0:rest]
+                    out[rows, cols] = value
         stores[i].start()
     for copy in stores:
         copy.wait()
@@ -1074,7 +1200,7 @@
 
 def run_finish(flat, width, hidden, part):
     anywhere = pl.BlockSpec(memory_space=pl.ANY)
-    shapes = ((2, width, hidden), (hidden, width), (3, width, part), (part, width))
+    shapes = ((2, width, hidden), (hidden, width), (3 * part, width), (part, width))
     return pl.pallas_call(
         finish_kernel,
         out_shape=tuple(jax.ShapeDtypeStruct(shape, F32) for shape in shapes),
@@ -1137,7 +1263,7 @@
     angles = jnp.dot(marks, jnp.asarray(angle_table()), precision=lax.Precision.HIGHEST)
     angles = angles.reshape(images, 4 * rows, 2 * LANES)
 
-    wqkv = jnp.einsum("jde,ef->jdf", qkv_weight[0], select, preferred_element_type=F32).astype(BF)
+    wqkv = jnp.einsum("ef,jde->jfd", select, qkv_weight[0], preferred_element_type=F32).astype(BF)
     wout = jnp.einsum("ef,ed->fd", select, out_weight[0], preferred_element_type=F32).astype(BF)
     gains = jnp.dot(jnp.concatenate([q_gain, k_gain], axis=0), select, preferred_element_type=F32)
 
@@ -1164,14 +1290,6 @@
     numbers = jnp.stack([bins.reshape(images), labels.reshape(images)]).astype(F32)
     extra = jnp.concatenate([gain_sums[0:2], jnp.pad(numbers, ((0, 4), (0, lanes_all - images)))], axis=0)
 
-    select_np = head_select(heads)
-    full = part // LANES * LANES
-    pick = np.zeros((3 * lanes_all, 3 * full + LANES), np.float32)
-    for j in range(3):
-        rows_j = slice(j * lanes_all, (j + 1) * lanes_all)
-        pick[rows_j, j * full : (j + 1) * full] = select_np.T[:, :full]
-        rest_at = 3 * full + j * (part - full)
-        pick[rows_j, rest_at : rest_at + part - full] = select_np.T[:, full:]
     flat = images * 4 * rows
     flat_grads, dmod_all, sum_all, extra_all = run_tail(
         dp,
@@ -1183,15 +1301,14 @@
         d_qkv.reshape(flat, d_qkv.shape[2]),
         mixed.reshape(flat, lanes_all),
         d_attn.reshape(flat, width),
-        jnp.asarray(pick, BF),
         select,
         summand,
         dmod_part.reshape(images * 8, 3 * LANES),
         extra,
     )
-    gate_up_grad, down_grad, qkv_grad, out_grad = [
-        item[None] for item in run_finish(flat_grads, width, units.shape[2], part)
-    ]
+    finished = run_finish(flat_grads, width, units.shape[2], part)
+    gate_up_grad, down_grad, out_grad = finished[0][None], finished[1][None], finished[3][None]
+    qkv_grad = jnp.transpose(finished[2].reshape(3, part, width), (0, 2, 1))[None]
 
     gains_sum = jnp.sum(extra_all[:, 0:2], axis=0)
     gains_sum = jnp.einsum("jf,ef->je", gains_sum, select.astype(F32), precision=lax.Precision.HIGHEST)

time: 694 us -> 577 us (0.83)
  Pallas kernels: 627 us -> 521 us
  local copies, waits for them, and re-layouts: 21 us -> 12.5 us
    pallas_call x1, Pallas kernels: 402 us -> 315 us  [run_main(): pl.pallas_call(functools.partial(main_kernel, images, heads), out_shape=o...]
    pallas_call x1, Pallas kernels: 219 us -> 198 us  [run_tail(): pl.pallas_call(functools.partial(tail_kernel, dp), out_shape=(jax.ShapeDt...]
    unnamed x33 -> x30, local copies, waits for them, and re-layouts: 13.5 us -> 5.07 us
where the time goes in v3:
time: 577 us; the launch traced here: 572 us
  Pallas kernels  521 us (90%)
  matrix products  29.3 us (5%)
  local copies, waits for them, and re-layouts  12.5 us (2%)
  other arithmetic  7.11 us (1%)
    pallas_call x1, Pallas kernels, run_main(): pl.pallas_call(functools.partial(main_kernel, images, heads), out_shape=o...  315 us
    pallas_call x1, Pallas kernels, run_tail(): pl.pallas_call(functools.partial(tail_kernel, dp), out_shape=(jax.ShapeDt...  198 us

profile of v3, /device:TPU:0, one launch (start us, length us, event | category | flops | bytes accessed | tf_op | source)
XLA Modules:
  0.0 571.7 jit_solution(13461329845236443931)
XLA Ops:
  0.8 0.8 convert_add_fusion
  1.8 0.8 copy.41
  2.8 0.8 copy.46
  4.2 1.7 fusion.33.gains
  5.9 0.8 reshape.408
  7.6 2.1 convolution_add_fusion.2
  9.7 3.5 fusion.2
  13.4 0.6 dynamic_update_slice.3.mod_cols
  14.0 1.9 convolution_convert_fusion.1.wout
  15.9 1.3 fusion.12
  17.2 1.3 convolution_add_fusion
  18.5 1.5 fusion.39
  20.1 3.9 fusion.4.wqkv
  23.9 315.3 %shard_map.230 = (bf16[8,64,1152]{2,1,0:T(8,128)(2,1)}, f32[8,64,1152]{2,1,0:T(8,128)}, bf16[8,8,384]{2,1,0:T(8,128)(2,1)}, f32[8,512]{1,0:T(8,128)}, f32[8,1152...) custom-call(bf16[8,64,1152]{2,1,0:T(8,128)(2,1)} %bitcast.95, ...), custom_call_target="tpu_custom_call" | custom-call | tf_op jit(solution)/shard_map/pallas_call | solution.py:695
  339.3 0.7 slice.32
  340.0 0.6 select_maximum_fusion.extra
  340.6 0.9 constant_dynamic-slice_fusion.1
  341.5 2.8 fusion.8
  344.3 0.7 pad_maximum_fusion.summand
  344.9 198.1 %shard_map.231 = (bf16[34560,128]{1,0:T(8,128)(2,1)}, bf16[4,64,384]{2,1,0:T(8,128)(2,1)}, bf16[4,16,1152]{2,1,0:T(8,128)(2,1)}, f32[4,16,512]{2,1,0:T(8,128)}) custom-call(bf16[2048,1152]{1,0:T(8,128)(2,1)} %bitcast.86, bf16[2048,1536]{1,0:T(8,128)(2,1)} %bitcast.83, bf16[2048,768]{1,0:T(8,128)(2,1)} %bitcast.90, bf16[2048,1152]{1,0:T(8,128)(2,1)} %bitcast.87, ...), custom_call_target="tpu_custom_call" | custom-call | tf_op jit(solution)/shard_map/pallas_call | solution.py:1108
  543.0 1.1 constant_dynamic-slice_fusion
  544.1 0.8 slice_reduce_fusion.1
  545.4 0.7 convert_reduce_fusion
  546.3 0.7 add_reduce_fusion
  547.0 0.9 slice_reduce_fusion
  548.3 0.6 fusion.40
  549.2 4.0 fusion.18
  553.2 6.5 %convolution_bitcast_fusion = f32[1,1152,6,288]{1,3,2,0:T(8,128)} fusion(bf16[32,6,288]{2,1,0:T(8,128)(2,1)S(1)} %constant_dynamic-slice_fusion, bf16[1000,1152]{1,0:T(8,128)(2,1)} %param.20, f32[32,576]{1,0:T(8,128)S(1)} %get-tuple-element.58, f32[32,576]{1,0:T(8,128)S(1)} %get-tuple-element.57, s32[32]{0:T(128)S(1)} %convert_element_type.67), kind=kOutput, calls=%fused_computation.1 | convolution fusion | flops 201420032 | bytes 10524800 | tf_op jit(solution)/shard_map/id,ijf->djf/dot_general | solution.py:1322
  559.7 8.0 %shard_map.232 = (f32[2,1152,768]{2,1,0:T(8,128)}, f32[768,1152]{1,0:T(8,128)}, f32[864,1152]{1,0:T(8,128)}, f32[288,1152]{1,0:T(8,128)}) custom-call(bf16[34560,128]{1,0:T(8,128)(2,1)} %get-tuple-element.47.flat_hbm), custom_call_target="tpu_custom_call" | custom-call | tf_op jit(solution)/shard_map/pallas_call | solution.py:1204
  567.8 1.0 copy.57
  568.8 1.0 copy-done.4
  569.8 1.4 copy.58
  (49 shorter events, 3.6 us)
Async XLA Ops:
  0.6 19.4 %copy-start = (bf16[1,3,1152,288]{2,3,1,0:T(8,128)(2,1)S(1)}, bf16[1,3,1152,288]{2,3,1,0:T(8,128)(2,1)}, u32[]{:S(2)}) copy-start(bf16[1,3,1152,288]{2,3,1,0:T(8,128)(2,1)} %param.22) | copy-start | bytes 5971972
  9.7 4.2 copy-start.2
  9.7 4.2 copy-start.11
  13.3 2.6 copy-start.9
  13.3 3.8 copy-start.8
  14.0 4.5 copy-start.6
  18.5 1.6 copy-start.12
  23.9 316.1 %copy-start.10 = (f32[2,8]{1,0:T(2,128)S(1)}, f32[2,8]{1,0:T(2,128)}, u32[]{:S(2)}) copy-start(f32[2,8]{1,0:T(2,128)} %add_convert_fusion) | copy-start | bytes 196
  339.3 5.0 copy-start.7
  344.9 203.0 %copy-start.3 = (bf16[288,512]{1,0:T(8,128)(2,1)S(1)}, bf16[288,512]{1,0:T(8,128)(2,1)}, u32[]{:S(2)}) copy-start(bf16[288,512]{1,0:T(8,128)(2,1)} %constant.100.clone.pick) | copy-start | bytes 884740
  559.7 8.0 %copy-start.5 = (bf16[8,64,1152]{2,1,0:T(8,128)(2,1)S(1)}, bf16[8,64,1152]{2,1,0:T(8,128)(2,1)}, u32[]{:S(2)}) copy-start(bf16[8,64,1152]{2,1,0:T(8,128)(2,1)} %get-tuple-element.32) | copy-start | bytes 3538948
  567.7 2.1 copy-start.4
  567.8 3.5 copy-start.1

commit v4 on v3

--- a/solution.py
+++ b/solution.py
@@ -18,29 +18,30 @@
 BF = jnp.bfloat16
 F32 = jnp.float32
 SCALE = HEAD_DIM**-0.5
+LOG2E = math.log2(math.e)
 
 KEEP, SLOTS, PACK = 2, 4, 4
-LENT = 3
+LENT = 4
 ORDERS = (
     (
-        0, 1, 2, 8, 3, 16, 9, 24, 4, 17, 10, 32, 25, 18, 40, 11, 26, 48,
-        33, 56, 19, 34, 41, 27, 49, 64, 12, 42, 57, 50, 35, 58, 65, 20, 5, 43,
-        28, 66, 51, 59, 13, 36, 6, 21, 67, 44, 29, 52, 60, 37, 7, 68, 14, 22,
-        45, 30, 15, 53, 61, 23, 38, 31, 69, 46, 39, 54, 47, 62, 70, 55, 63, 71,
-        72, 73, 80, 88, 81, 96, 89, 97, 104, 105, 112, 113, 120, 74, 121, 82, 128, 90,
-        98, 75, 106, 136, 83, 129, 91, 114, 76, 99, 122, 84, 107, 130, 92, 100, 115, 137,
-        77, 123, 85, 78, 108, 93, 86, 138, 101, 94, 79, 116, 102, 131, 124, 87, 109, 110,
-        95, 139, 117, 103, 132, 125, 111, 133, 118, 140, 126, 119, 141, 134, 127, 142, 135, 143,
+        0, 1, 8, 2, 3, 16, 9, 24, 10, 4, 17, 32, 11, 25, 18, 40, 26, 48, 33,
+        56, 19, 34, 12, 41, 64, 49, 27, 57, 42, 144, 50, 35, 65, 58, 20, 43, 5, 145,
+        66, 28, 51, 13, 146, 59, 36, 6, 21, 67, 44, 52, 60, 147, 14, 7, 29, 68, 22,
+        15, 37, 148, 30, 23, 38, 31, 45, 53, 61, 39, 46, 54, 69, 62, 149, 70, 47, 72,
+        55, 80, 63, 150, 88, 71, 151, 96, 104, 73, 81, 89, 112, 74, 97, 120, 82, 128, 105,
+        90, 136, 98, 113, 75, 121, 83, 106, 91, 114, 129, 99, 122, 76, 130, 137, 107, 84, 92,
+        77, 115, 100, 138, 123, 78, 85, 108, 93, 86, 79, 131, 94, 116, 101, 102, 124, 87, 109,
+        132, 95, 139, 117, 103, 110, 125, 111, 140, 133, 118, 126, 119, 141, 134, 127, 135, 142, 143,
     ),
     (
-        72, 73, 74, 75, 76, 77, 80, 78, 0, 8, 1, 16, 81, 9, 24, 2, 82, 83,
-        84, 17, 32, 25, 10, 18, 3, 40, 33, 85, 88, 86, 11, 26, 96, 19, 4, 34,
-        41, 48, 27, 89, 12, 104, 42, 97, 20, 35, 49, 112, 5, 28, 90, 56, 105, 79,
-        98, 43, 120, 91, 113, 36, 13, 128, 121, 106, 6, 44, 21, 7, 129, 92, 136, 14,
-        29, 87, 99, 114, 100, 15, 22, 137, 64, 30, 122, 37, 107, 23, 38, 50, 57, 45,
-        108, 115, 130, 58, 31, 93, 46, 123, 116, 138, 101, 94, 131, 39, 124, 102, 65, 139,
-        109, 132, 51, 47, 110, 66, 95, 59, 52, 117, 140, 118, 103, 125, 67, 111, 133, 126,
-        119, 60, 53, 134, 141, 61, 127, 142, 68, 54, 135, 69, 62, 55, 63, 143, 70, 71,
+        72, 73, 74, 80, 75, 81, 82, 76, 83, 77, 0, 8, 78, 16, 1, 24, 84, 9, 32,
+        79, 17, 40, 85, 2, 25, 88, 10, 33, 48, 56, 18, 96, 41, 3, 86, 26, 89, 11,
+        104, 97, 19, 4, 64, 112, 34, 27, 49, 120, 42, 105, 57, 90, 12, 113, 35, 98, 20,
+        65, 128, 43, 121, 28, 50, 106, 136, 91, 5, 36, 13, 129, 114, 58, 99, 21, 122, 44,
+        51, 66, 29, 59, 130, 6, 92, 14, 37, 107, 22, 7, 137, 67, 138, 30, 15, 87, 52,
+        60, 45, 100, 115, 23, 38, 123, 31, 108, 93, 53, 131, 46, 68, 61, 39, 94, 116, 139,
+        101, 102, 124, 47, 69, 109, 132, 95, 117, 144, 110, 103, 125, 140, 54, 133, 145, 118, 146,
+        55, 111, 62, 126, 141, 119, 134, 63, 127, 147, 135, 142, 148, 70, 149, 71, 150, 143, 151,
     ),
 )
 
@@ -110,13 +111,14 @@
     tok,
     vel,
     mod_cols,
-    cosine,
-    sine,
-    wqkv,
-    wout,
-    wgu,
-    wdn,
-    gains,
+    turns,
+    qkv_hbm,
+    out_hbm,
+    wgu_hbm,
+    wdn_hbm,
+    q_gain,
+    k_gain,
+    select,
     zout,
     dxout,
     dmod_part,
@@ -130,6 +132,11 @@
     mix_hbm,
     dgu_hbm,
     dqkv_hbm,
+    wqkv,
+    wout,
+    wgu,
+    wdn,
+    gains,
     xin,
     din,
     a1f,
@@ -152,7 +159,7 @@
     mod,
     mod_recv,
     dmod,
-    dmod_recv,
+    dmod_sum,
     mod_sems,
     dmod_sems,
     ag_sems,
@@ -177,6 +184,19 @@
 
     load_x = pltpu.make_async_copy(tok, xin, in_sems.at[0])
     load_d = pltpu.make_async_copy(vel, din, in_sems.at[1])
+    tokens, part = dattn.shape[1], out_hbm.shape[0]
+    groups = [qkv_hbm.at[j] for j in range(3)] + [out_hbm]
+    load_w = [
+        pltpu.make_async_copy(wgu_hbm, wgu, in_sems.at[2]),
+        pltpu.make_async_copy(wdn_hbm, wdn, in_sems.at[3]),
+    ]
+    load_raw = []
+    for j, group in enumerate(groups):
+        for i, (at, size) in enumerate(((0, tokens), (tokens, part - tokens))):
+            src, dst = group.at[pl.ds(at, size)], dattn.at[2 * j + i, pl.ds(0, size)]
+            load_raw.append(pltpu.make_async_copy(src, dst, in_sems.at[4 + 2 * j + i]))
+    for copy in load_raw:
+        copy.start()
 
     @pl.when(enc)
     def _():
@@ -213,7 +233,7 @@
     def dmod_copy(k, n):
         return remote(
             dmod.at[n, :, its_tiles(peers[k])],
-            dmod_recv.at[k, n],
+            mod_recv.at[k, n],
             dmod_sems.at[0, k, n],
             dmod_sems.at[1, k, n],
             {"tensor": peers[k]},
@@ -221,7 +241,21 @@
 
     for k in (1, 2, 0):
         mod_copy(k).start()
+    for copy in load_w:
+        copy.start()
     mod[:, :, its_tiles(me)] = mod_cols[...]
+
+    gains[0:1, :] = dot(q_gain[...], select[...])
+    gains[1:2, :] = dot(k_gain[...], select[...])
+    for j in range(4):
+        load_raw[2 * j].wait()
+        load_raw[2 * j + 1].wait()
+        ref = wqkv.at[j] if j < 3 else wout
+        for at, size in wide:
+            span = pl.ds(at, size)
+            value = dot_tn(select[0:tokens, :], dattn[2 * j, :, span])
+            value += dot_tn(select[tokens:part, :], dattn[2 * j + 1, 0 : part - tokens, span])
+            ref[:, span] = value.astype(BF)
 
     @pl.when(enc)
     def _():
@@ -253,6 +287,19 @@
         gather(which, buf, n, 0).wait_recv()
         gather(which, buf, n, 2).start()
 
+    def attn_relay(n):
+        @pl.when(enc)
+        def _():
+            gather(0, a1f, n, 0).wait_recv()
+
+        @pl.when(dec)
+        def _():
+            zy_pass(n).wait_recv()
+            values = a1f[n, rows : 2 * rows, :].astype(F32)
+            a1f[n, rows : 2 * rows, :] = modulated(values, mod_row(n, 0), mod_row(n, 1)).astype(BF)
+
+        gather(0, a1f, n, 2).start()
+
     def gather_wait(which, buf, n):
         gather(which, buf, n, 1).wait_recv()
         gather(which, buf, n, 2).wait_recv()
@@ -303,6 +350,20 @@
     def z_copy(n):
         return remote(zout.at[n], xin.at[n], zx_sems.at[0, n], zx_sems.at[1, n], {"section": other})
 
+    def zy_copy(n):
+        return remote(
+            zout.at[n], dattn.at[n, pl.ds(rows, rows)], zx_sems.at[4, n], zx_sems.at[5, n], {"tensor": across}
+        )
+
+    def zy_pass(n):
+        return remote(
+            dattn.at[n, pl.ds(rows, rows)],
+            a1f.at[n, pl.ds(rows, rows)],
+            zx_sems.at[6, n],
+            zx_sems.at[7, n],
+            {"section": other},
+        )
+
     def dz_copy(n):
         return remote(xin.at[n], din.at[n], zx_sems.at[2, n], zx_sems.at[3, n], {"section": other})
 
@@ -335,9 +396,9 @@
     def turn_back(values, c, s):
         return values * c - pltpu.roll(values, 64, 1) * s
 
-    def softmax(scores):
-        powered = jnp.exp(scores - jnp.max(scores, axis=-1, keepdims=True))
-        return powered * (1.0 / jnp.sum(powered, axis=-1, keepdims=True))
+    def softmax_parts(scaled, k):
+        powered = jnp.exp2(dot_nt(scaled, k))
+        return powered, 1.0 / jnp.sum(powered, axis=-1, keepdims=True)
 
     def out_copy(which, n):
         src = (a1f, a2f, dffn, dattn, hid_st, mix_st, dgu_st, dqkv_st)[which]
@@ -357,13 +418,18 @@
         values = xin[n].astype(F32)
         sacc[0:1, :] += column_sum(values * values)
         a1f[n, 0:rows, :] = modulated(values, mod_row(n, 0), mod_row(n, 1)).astype(BF)
-        gather_start(0, a1f, n)
+
+        @pl.when(enc)
+        def _():
+            gather(0, a1f, n, 0).start()
+
+        gather(0, a1f, n, 1).start()
 
     def attn_compute(n):
         gather_wait(0, a1f, n)
         staged_ready(5, n)
         a1 = a1f[n]
-        c, s = cosine[n], sine[n]
+        c, s = turns[n, :, 0:LANES], turns[n, :, LANES : 2 * LANES]
         for pair in range(heads // 2):
             span = pl.ds(pair * 2 * LANES, 2 * LANES)
             q2 = dot_nt(a1, wqkv[0, span, :])
@@ -372,17 +438,23 @@
             for half in range(2):
                 at = (pair * 2 + half) * LANES
                 cut = slice(half * LANES, (half + 1) * LANES)
-                q = turn(head_norm(q2[:, cut])[1] * gains[0:1, at : at + LANES], c, s).astype(BF)
+                q_gain = gains[0:1, at : at + LANES] * (SCALE * LOG2E)
+                q = turn(head_norm(q2[:, cut])[1] * q_gain, c, s).astype(BF)
                 k = turn(head_norm(k2[:, cut])[1] * gains[1:2, at : at + LANES], c, s).astype(BF)
-                probs = softmax(dot_nt(q, k) * SCALE).astype(BF)
-                mix_st[:, at : at + LANES] = dot(probs, v2[:, cut]).astype(BF)
+                powered, inverse = softmax_parts(q, k)
+                mix_st[:, at : at + LANES] = (dot(powered.astype(BF), v2[:, cut]) * inverse).astype(BF)
         mixed = mix_st[...]
         for at, size in wide:
             scatter_put(0, n, at, size, dot(mixed, wout[:, pl.ds(at, size)]))
         scatter_start(0, n)
         out_copy(5, n).start()
         out_copy(0, n).start()
-        gather_drain(0, a1f, n)
+        gather(0, a1f, n, 1).wait_send()
+        gather(0, a1f, n, 2).wait_send()
+
+        @pl.when(enc)
+        def _():
+            gather(0, a1f, n, 0).wait_send()
 
     def ffn_in(n):
         attended = scatter_end(0, n)
@@ -393,23 +465,32 @@
         a2f[n, 0:rows, :] = modulated(values, mod_row(n, 3), mod_row(n, 4)).astype(BF)
         gather_start(1, a2f, n)
 
-    def ffn_compute(n):
-        @pl.when(enc)
-        def _():
-            gather_wait(1, a2f, n)
-
-        a2 = a2f[n]
-        for at, size in chunks_of(hidden, 256):
-            span = pl.ds(at, size)
-            gate_val = dot(a2, wgu[0, :, span])
-            up_val = dot(a2, wgu[1, :, span])
-            units_st[:, span] = (gate_val * jax.nn.sigmoid(gate_val) * up_val).astype(BF)
-        units = units_st[...]
+    def ffn_down(n, units):
         for at, size in wide:
             scatter_put(1, n, at, size, dot(units, wdn[:, pl.ds(at, size)]))
         scatter_start(1, n)
         out_copy(1, n).start()
         gather_drain(1, a2f, n)
+
+    def first_ffn(n):
+        gather_wait(1, a2f, n)
+
+        @pl.when(n == 0)
+        def _():
+            load_w[0].wait()
+            load_w[1].wait()
+
+    def ffn_compute(n):
+        @pl.when(enc)
+        def _():
+            first_ffn(n)
+            a2 = a2f[n]
+            for at, size in chunks_of(hidden, 256):
+                span = pl.ds(at, size)
+                gate_val = dot(a2, wgu[0, :, span])
+                up_val = dot(a2, wgu[1, :, span])
+                units_st[:, span] = (gate_val * jax.nn.sigmoid(gate_val) * up_val).astype(BF)
+            ffn_down(n, units_st[...])
 
     def block_out(n):
         feedfwd = scatter_end(1, n)
@@ -421,10 +502,20 @@
         @pl.when(enc)
         def _():
             z_copy(n).start()
+            zy_copy(n).start()
 
         @pl.when(dec)
         def _():
             dmod[n, 5:6, :] = column_sum(din[n].astype(F32) * feedfwd)
+
+    def pass_on(n):
+        @pl.when(enc)
+        def _():
+            zy_copy(n).wait_recv()
+            zy_pass(n).start()
+
+        @pl.when(dec)
+        def _():
             send_dmod(n)
 
     def send_dmod(n):
@@ -434,6 +525,8 @@
     def ffn_grad_in(n):
         @pl.when(enc)
         def _():
+            zy_copy(n).wait_send()
+            zy_pass(n).wait_send()
             dz_copy(n).wait_recv()
 
         grad = din[n].astype(F32)
@@ -447,7 +540,7 @@
     def ffn_grad_compute(n):
         @pl.when(dec)
         def _():
-            gather_wait(1, a2f, n)
+            first_ffn(n)
 
         gather_wait(2, dffn, n)
         staged_ready(4, n)
@@ -470,6 +563,11 @@
             span = pl.ds(at, size)
             scatter_put(2, n, at, size, dot_nt(d_gate, wgu[0, span, :]) + dot_nt(d_up, wgu[1, span, :]))
         scatter_start(2, n)
+
+        @pl.when(dec)
+        def _():
+            ffn_down(n, hid_st[...])
+
         out_copy(4, n).start()
         out_copy(6, n).start()
         out_copy(2, n).start()
@@ -491,29 +589,33 @@
         staged_ready(7, n)
         grad = dattn[n]
         a1 = a1f[n]
-        c, s = cosine[n], sine[n]
+        c, s = turns[n, :, 0:LANES], turns[n, :, LANES : 2 * LANES]
         lanes_all = heads * LANES
         for pair in range(heads // 2):
             span = pl.ds(pair * 2 * LANES, 2 * LANES)
             q2 = dot_nt(a1, wqkv[0, span, :])
             k2 = dot_nt(a1, wqkv[1, span, :])
             v2 = dot_nt(a1, wqkv[2, span, :]).astype(BF)
-            d_mix2 = dot_nt(grad, wout[span, :]).astype(BF)
+            d_mix2 = dot_nt(grad, wout[span, :])
             for half in range(2):
                 at = (pair * 2 + half) * LANES
                 cut = slice(half * LANES, (half + 1) * LANES)
                 q_gain, k_gain = gains[0:1, at : at + LANES], gains[1:2, at : at + LANES]
                 q_inv, q_norm = head_norm(q2[:, cut])
                 k_inv, k_norm = head_norm(k2[:, cut])
-                q = turn(q_norm * q_gain, c, s).astype(BF)
+                q = turn(q_norm * (q_gain * (SCALE * LOG2E)), c, s).astype(BF)
                 k = turn(k_norm * k_gain, c, s).astype(BF)
-                v, d_mix = v2[:, cut], d_mix2[:, cut]
-                probs = softmax(dot_nt(q, k) * SCALE)
-                d_probs = dot_nt(d_mix, v)
-                d_v = dot_tn(probs.astype(BF), d_mix)
-                d_scores = (probs * (d_probs - jnp.sum(probs * d_probs, axis=-1, keepdims=True))).astype(BF)
+                v = v2[:, cut]
+                powered, inverse = softmax_parts(q, k)
+                low = powered.astype(BF)
+                mixed = dot(low, v) * inverse
+                d_mix = d_mix2[:, cut] * inverse
+                d_mix = d_mix.astype(BF)
+                taken = jnp.sum(d_mix.astype(F32) * mixed, axis=-1, keepdims=True)
+                d_v = dot_tn(low, d_mix)
+                d_scores = (powered * (dot_nt(d_mix, v) - taken)).astype(BF)
                 d_q = turn_back(dot(d_scores, k) * SCALE, c, s)
-                d_k = turn_back(dot_tn(d_scores, q) * SCALE, c, s)
+                d_k = turn_back(dot_tn(d_scores, q) * (1.0 / LOG2E), c, s)
                 gacc[0:1, at : at + LANES] += column_sum(d_q * q_norm)
                 gacc[1:2, at : at + LANES] += column_sum(d_k * k_norm)
                 d_q = d_q * q_gain
@@ -553,7 +655,7 @@
 
     works = (
         attn_in,
-        lambda n: gather_relay(0, a1f, n),
+        attn_relay,
         attn_compute,
         lambda n: scatter_middle(0, n),
         ffn_in,
@@ -570,6 +672,7 @@
         attn_grad_compute,
         lambda n: scatter_middle(3, n),
         block_grad_out,
+        pass_on,
     )
 
     def run_work(work, n, low, high):
@@ -617,8 +720,9 @@
         part = dmod[n, :, its_tiles(me)]
         for k in range(3):
             dmod_copy(k, n).wait()
-            part += dmod_recv[k, n]
-        dmod_part[n] = part.astype(BF)
+            part += mod_recv[k, n]
+        for j in range(8):
+            dmod_sum[j, pl.ds(n, 1), :] = part[j : j + 1]
 
         @pl.when(enc)
         def _():
@@ -631,12 +735,13 @@
         return carry
 
     lax.fori_loop(0, images, drain, 0)
-
-
-def run_main(tok, vel, mod_cols, cosine, sine, wqkv, wout, wgu, wdn, gains):
+    dmod_part[...] = dmod_sum[...].astype(BF)
+
+
+def run_main(tok, vel, mod_cols, turns, qkv, out, wgu, wdn, q_gain, k_gain, select):
     images, rows, width = tok.shape
     tokens = 4 * rows
-    lanes_all = wout.shape[0]
+    lanes_all = select.shape[1]
     heads = lanes_all // LANES
     hidden = wdn.shape[0]
     vmem = pl.BlockSpec(memory_space=pltpu.VMEM)
@@ -648,7 +753,7 @@
     out_shape = (
         jax.ShapeDtypeStruct((images, rows, width), BF),
         jax.ShapeDtypeStruct((images, rows, width), F32),
-        jax.ShapeDtypeStruct((images, 8, 3 * LANES), BF),
+        jax.ShapeDtypeStruct((8, images, 3 * LANES), BF),
         jax.ShapeDtypeStruct((8, lanes_all), F32),
         jax.ShapeDtypeStruct((8, width), F32),
         hbm(width),
@@ -661,6 +766,11 @@
         hbm(3 * lanes_all),
     )
     scratch = [
+        pltpu.VMEM((3, lanes_all, width), BF),
+        pltpu.VMEM((lanes_all, width), BF),
+        pltpu.VMEM(wgu.shape, BF),
+        pltpu.VMEM(wdn.shape, BF),
+        pltpu.VMEM((8, lanes_all), F32),
         pltpu.VMEM((images, rows, width), BF),
         pltpu.VMEM((images, rows, width), BF),
         pltpu.VMEM((images, tokens, width), BF),
@@ -683,25 +793,25 @@
         pltpu.VMEM((images, 8, width), F32),
         pltpu.VMEM((3, images, 8, 3 * LANES), F32),
         pltpu.VMEM((images, 8, width), F32),
-        pltpu.VMEM((3, images, 8, 3 * LANES), F32),
+        pltpu.VMEM((8, images, 3 * LANES), F32),
         pltpu.SemaphoreType.DMA((2, 3)),
         pltpu.SemaphoreType.DMA((2, 3, images)),
         pltpu.SemaphoreType.DMA((4, 6, images)),
         pltpu.SemaphoreType.DMA((4, 4, images)),
-        pltpu.SemaphoreType.DMA((4, images)),
         pltpu.SemaphoreType.DMA((8, images)),
-        pltpu.SemaphoreType.DMA((2,)),
+        pltpu.SemaphoreType.DMA((8, images)),
+        pltpu.SemaphoreType.DMA((12,)),
     ]
     return pl.pallas_call(
         functools.partial(main_kernel, images, heads),
         out_shape=out_shape,
-        in_specs=[anywhere, anywhere] + [vmem] * 8,
+        in_specs=[anywhere, anywhere] + [vmem] * 2 + [anywhere] * 4 + [vmem] * 3,
         out_specs=[vmem] * 5 + [anywhere] * 8,
         scratch_shapes=scratch,
         compiler_params=pltpu.CompilerParams(
             collective_id=0, has_side_effects=True, vmem_limit_bytes=62 * 2**20
         ),
-    )(tok, vel, mod_cols, cosine, sine, wqkv, wout, wgu, wdn, gains)
+    )(tok, vel, mod_cols, turns, qkv, out, wgu, wdn, q_gain, k_gain, select)
 
 
 def flat_plan(width, hidden, part):
@@ -733,10 +843,14 @@
     dqkv_hbm,
     mix_hbm,
     dattn_hbm,
+    mod_hbm,
     pick,
-    summand,
+    cond,
+    squares,
+    silu,
     dmod_low,
-    extra,
+    gain_sums,
+    labels,
     totals,
     dmod_all,
     sum_all,
@@ -748,6 +862,8 @@
     turned,
     own,
     arrived,
+    mod_w,
+    summand,
     sum_st,
     sum_recv,
     load_sems,
@@ -771,12 +887,29 @@
     whole = half // chunk
     count = jnp.where(enc, whole - LENT, whole + LENT)
 
+    tokens, ahead = left_a.shape[0], 2 * LANES
+    quarter = tokens // 4
+
+    def some_rows(i):
+        rows = pl.ds(i * quarter, quarter)
+        return a2_hbm.at[rows], left_a.at[rows]
+
+    def some_columns(at, size):
+        cols = pl.ds(at, size)
+        return dgu_hbm.at[:, cols], right_a.at[:, cols]
+
     loads = [
         pltpu.make_async_copy(src, dst, load_sems.at[i])
         for i, (src, dst) in enumerate(
             (
-                (a2_hbm, left_a),
-                (dgu_hbm, right_a),
+                some_rows(0),
+                some_rows(1),
+                some_rows(2),
+                some_rows(3),
+                some_columns(0, ahead),
+                some_columns(hidden, ahead),
+                some_columns(ahead, hidden - ahead),
+                some_columns(hidden + ahead, hidden - ahead),
                 (hid_hbm, left_b),
                 (dffn_hbm, right_b),
                 (mix_hbm, left_b.at[:, pl.ds(0, lanes_all)]),
@@ -786,8 +919,14 @@
             )
         )
     ]
-    for i in range(4):
+    for i in range(10):
         loads[i].start()
+
+    mod_w[...] = jnp.zeros_like(mod_w)
+    mine = pl.ds(pl.multiple_of(me * (part - 2 * LANES), 16), part)
+    mod_loads = [pltpu.make_async_copy(mod_hbm.at[j], mod_w.at[j, mine], load_sems.at[14 + j]) for j in range(6)]
+    for copy in mod_loads:
+        copy.start()
 
     barrier = pltpu.get_barrier_semaphore()
     for where in ({"tensor": sib}, {"tensor": across}):
@@ -810,9 +949,9 @@
         for i in range(value.shape[1] // LANES):
             put(segment, block + i, first, value[:, i * LANES : (i + 1) * LANES])
 
-    def turn_left(ref):
-        tokens, cols = ref.shape
-        for at in range(0, tokens, 256):
+    def turn_left(ref, first, last):
+        cols = ref.shape[1]
+        for at in range(first, last, 256):
             turned[0:cols, at : at + 256] = ref[at : at + 256, :].T
 
     def gate_up_blocks(*blocks):
@@ -830,34 +969,39 @@
         tiles, gu_half = width // LANES, hidden // LANES
         pairs = 3 * lanes_all // (2 * LANES)
         if i == 0:
-            loads[0].wait()
-            turn_left(left_a)
-            loads[5].start()
-            loads[1].wait()
-            gate_up_blocks(0, gu_half)
+            for k in range(4):
+                loads[k].wait()
+                turn_left(left_a, k * quarter, (k + 1) * quarter)
+            loads[11].start()
+            loads[4].wait()
+            gate_up_blocks(0)
+            loads[5].wait()
+            gate_up_blocks(gu_half)
         elif i == 1:
+            loads[6].wait()
+            loads[7].wait()
             gate_up_blocks(2, gu_half + 2)
         elif i == 2:
             gate_up_blocks(*range(4, gu_half, 2), *range(gu_half + 4, 2 * gu_half, 2))
-            loads[6].start()
+            loads[12].start()
         elif i == 3:
-            loads[2].wait()
-            turn_left(left_b)
-            loads[4].start()
-            loads[3].wait()
+            loads[8].wait()
+            turn_left(left_b, 0, tokens)
+            loads[10].start()
+            loads[9].wait()
             for block in range(0, tiles, 2):
                 cut = slice(block * LANES, min(width, (block + 2) * LANES))
                 put_wide(1, block, 0, dot(turned[0:hidden, :], right_b[:, cut]))
-            loads[7].start()
+            loads[13].start()
         elif i == 4:
-            loads[5].wait()
-            loads[6].wait()
+            loads[11].wait()
+            loads[12].wait()
             qkv_heads(*range(0, pairs // 2))
         elif i == 5:
             qkv_heads(*range(pairs // 2, pairs))
         elif i == 6:
-            loads[4].wait()
-            loads[7].wait()
+            loads[10].wait()
+            loads[13].wait()
             value = dot(pick[...], dot_tn(left_b[:, 0:lanes_all], right_b[...]).astype(BF))
             put_wide(3, 0, 0, value)
 
@@ -971,7 +1115,7 @@
 
         for i in range(4):
 
-            @pl.when(step == jnp.where(enc, 4, 12) + i)
+            @pl.when(step == jnp.where(enc, 12, 22) + i)
             def _():
                 small(i)
 
@@ -1006,6 +1150,17 @@
             dmod_all[place] = dmod_low[...]
             for k in range(1, dp):
                 all_copy(0, k, True).start()
+
+            for copy in mod_loads:
+                copy.wait()
+            images = cond.shape[0]
+            grads = dmod_low[...].astype(F32)
+            d_silu = dot(grads[0:images].astype(BF), mod_w[0])
+            for j in range(1, 6):
+                d_silu += dot(grads[j * images : (j + 1) * images].astype(BF), mod_w[j])
+            sig = jax.nn.sigmoid(cond[...])
+            summand[0:8, :] = d_silu * (sig + cond[...] * sig * (1.0 - sig))
+            summand[8:16, :] = squares[...]
 
             @pl.when(dec)
             def _():
@@ -1024,13 +1179,16 @@
         elif step == 3:
             sum_copy(2).wait()
             total = sum_st[1] + sum_recv[2]
-            sum_all[place] = total.astype(BF)
-            squares = total[8:16, 0:LANES]
+            sum_all[place, 0:8, :] = total[0:8].astype(BF)
+            sum_all[place, 8:16, :] = silu[...]
+            square = total[8:16, 0:LANES]
             for i in range(1, width // LANES):
-                squares += total[8:16, i * LANES : (i + 1) * LANES]
-            extra_all[place, 0:8, :] = extra[...]
-            extra_all[place, 8:16, :] = jnp.zeros_like(extra)
-            extra_all[place, 8:16, 0:LANES] = squares
+                square += total[8:16, i * LANES : (i + 1) * LANES]
+            extra_all[place, 0:8, :] = gain_sums[...]
+            extra_all[place, 8:16, :] = jnp.zeros_like(gain_sums)
+            extra_all[place, 8:16, 0:LANES] = square
+            for i in range(8):
+                extra_all[place, 8 + i : 9 + i, LANES : 2 * LANES] = jnp.full((1, LANES), labels[i].astype(F32))
             for k in range(1, dp):
                 all_copy(1, k, True).start()
                 all_copy(2, k, True).start()
@@ -1098,7 +1256,7 @@
     lax.fori_loop(0, count, drain, 0)
 
 
-def run_tail(dp, a2, dgu, hid, dffn, a1, dqkv, mix, dattn, pick, summand, dmod_low, extra):
+def run_tail(dp, a2, dgu, hid, dffn, a1, dqkv, mix, dattn, mod_w, pick, cond, squares, silu, dmod_low, gain_sums, labels):
     tokens, width = a2.shape
     hidden = hid.shape[1]
     vmem = pl.BlockSpec(memory_space=pltpu.VMEM)
@@ -1110,10 +1268,10 @@
         out_shape=(
             jax.ShapeDtypeStruct((flat_rows, LANES), BF),
             jax.ShapeDtypeStruct((dp,) + dmod_low.shape, BF),
-            jax.ShapeDtypeStruct((dp,) + summand.shape, BF),
-            jax.ShapeDtypeStruct((dp, 16, extra.shape[1]), F32),
+            jax.ShapeDtypeStruct((dp, 16, width), BF),
+            jax.ShapeDtypeStruct((dp, 16, gain_sums.shape[1]), F32),
         ),
-        in_specs=[anywhere] * 8 + [vmem] * 4,
+        in_specs=[anywhere] * 9 + [vmem] * 6 + [pl.BlockSpec(memory_space=pltpu.SMEM)],
         out_specs=[vmem] * 4,
         scratch_shapes=[
             pltpu.VMEM((tokens, width), BF),
@@ -1123,9 +1281,11 @@
             pltpu.VMEM((width, tokens), BF),
             pltpu.VMEM((flat_rows, LANES), BF),
             pltpu.VMEM((flat_rows, LANES), BF),
-            pltpu.VMEM((2,) + summand.shape, F32),
-            pltpu.VMEM((3,) + summand.shape, F32),
-            pltpu.SemaphoreType.DMA((8,)),
+            pltpu.VMEM((6, 3 * LANES, width), BF),
+            pltpu.VMEM((16, width), F32),
+            pltpu.VMEM((2, 16, width), F32),
+            pltpu.VMEM((3, 16, width), F32),
+            pltpu.SemaphoreType.DMA((20,)),
             pltpu.SemaphoreType.DMA((2, 2, chunks)),
             pltpu.SemaphoreType.DMA((2, 2, chunks)),
             pltpu.SemaphoreType.DMA((3, 2)),
@@ -1137,11 +1297,40 @@
         compiler_params=pltpu.CompilerParams(
             collective_id=1, has_side_effects=True, vmem_limit_bytes=62 * 2**20
         ),
-    )(a2, dgu, hid, dffn, a1, dqkv, mix, dattn, pick, summand, dmod_low, extra)
+    )(a2, dgu, hid, dffn, a1, dqkv, mix, dattn, mod_w, pick, cond, squares, silu, dmod_low, gain_sums, labels)
 
 
 def finish_kernel(
-    flat_hbm, gu_hbm, down_hbm, qkv_hbm, out_hbm, flat, gate_up, down, qkv, out, load_sems, store_sems
+    count,
+    flat_hbm,
+    z_hbm,
+    dx_hbm,
+    dmod_all,
+    sum_all,
+    extra_all,
+    select,
+    gu_hbm,
+    down_hbm,
+    qkv_hbm,
+    out_hbm,
+    z_out,
+    dx_out,
+    mod_hbm,
+    class_hbm,
+    q_gain_out,
+    k_gain_out,
+    stats_out,
+    flat,
+    gate_up,
+    down,
+    qkv,
+    out,
+    mod,
+    classes,
+    z_rows,
+    dx_rows,
+    load_sems,
+    store_sems,
 ):
     width, hidden = gate_up.shape[1], gate_up.shape[2]
     part, blocks, hidden_blocks = out.shape[0], width // LANES, hidden // LANES
@@ -1169,6 +1358,57 @@
             copies.append(pltpu.make_async_copy(flat_hbm.at[rows], flat.at[rows], sem))
             copies[-1].start()
         loads.append(copies)
+    inward = (
+        pltpu.make_async_copy(z_hbm, z_rows, load_sems.at[0, 2]),
+        pltpu.make_async_copy(dx_hbm, dx_rows, load_sems.at[1, 2]),
+    )
+    outward = (
+        pltpu.make_async_copy(z_rows, z_out, store_sems.at[5]),
+        pltpu.make_async_copy(dx_rows, dx_out, store_sems.at[6]),
+    )
+    for copy in inward:
+        copy.start()
+
+    dp, images = dmod_all.shape[0], dmod_all.shape[1] // 8
+    me = lax.axis_index("tensor")
+    silu = jnp.concatenate([sum_all[p].astype(F32)[8:16] for p in range(dp)], axis=0).astype(BF)
+    grad_cond = jnp.concatenate([sum_all[p].astype(F32)[0:8] for p in range(dp)], axis=0).astype(BF)
+    dmods = [dmod_all[p].astype(F32) for p in range(dp)]
+    mod_stores = []
+    for j in range(6):
+        grads = jnp.concatenate([dmods[p][j * images : (j + 1) * images] for p in range(dp)], axis=0).astype(BF)
+        mod[j] = dot_tn(grads, silu)
+        mine = pl.ds(pl.multiple_of(me * (part - 2 * LANES), 8), part)
+        mod_stores.append(pltpu.make_async_copy(mod.at[j, mine], mod_hbm.at[j], store_sems.at[8 + j]))
+        mod_stores[-1].start()
+    labels = jnp.concatenate([extra_all[p, 8:16, LANES : LANES + 1] for p in range(dp)], axis=0)
+    lanes = lax.broadcasted_iota(jnp.int32, (dp * images, classes.shape[0]), 1)
+    one_hot = jnp.where(lanes == labels.astype(jnp.int32), 1.0, 0.0).astype(BF)
+    for at, size in chunks_of(width, 384):
+        classes[:, at : at + size] = dot_tn(one_hot, grad_cond[:, at : at + size])
+    class_store = pltpu.make_async_copy(classes.at[pl.ds(0, class_hbm.shape[0])], class_hbm, store_sems.at[7])
+    class_store.start()
+
+    for i in range(2):
+        inward[i].wait()
+        outward[i].start()
+
+    gain_sum, squares = extra_all[0, 0:8, :], extra_all[0, 8:16, 0:LANES]
+    for p in range(1, dp):
+        gain_sum += extra_all[p, 0:8, :]
+        squares += extra_all[p, 8:16, 0:LANES]
+    gain_sum = lax.dot_general(
+        gain_sum,
+        select[...].astype(F32),
+        (((1,), (1,)), ((), ())),
+        precision=lax.Precision.HIGHEST,
+        preferred_element_type=F32,
+    )
+    q_gain_out[...] = gain_sum[0:1]
+    k_gain_out[...] = gain_sum[1:2]
+    for i in range(3):
+        stats_out[0:1, i : i + 1] = jnp.sqrt(jnp.sum(squares[i : i + 1], axis=1, keepdims=True) * (1.0 / count))
+
     stores = (
         pltpu.make_async_copy(gate_up.at[0], gu_hbm.at[0], store_sems.at[0]),
         pltpu.make_async_copy(gate_up.at[1], gu_hbm.at[1], store_sems.at[1]),
@@ -1194,23 +1434,41 @@
                 else:
                     out[rows, cols] = value
         stores[i].start()
-    for copy in stores:
+    for copy in (*stores, *outward, *mod_stores, class_store):
         copy.wait()
 
 
-def run_finish(flat, width, hidden, part):
+def run_finish(count, class_count, hidden, flat, z_rows, dx_rows, dmod_all, sum_all, extra_all, select):
+    part, width = select.shape[0], sum_all.shape[2]
+    vmem = pl.BlockSpec(memory_space=pltpu.VMEM)
     anywhere = pl.BlockSpec(memory_space=pl.ANY)
     shapes = ((2, width, hidden), (hidden, width), (3 * part, width), (part, width))
     return pl.pallas_call(
-        finish_kernel,
-        out_shape=tuple(jax.ShapeDtypeStruct(shape, F32) for shape in shapes),
-        in_specs=[anywhere],
-        out_specs=[anywhere] * 4,
+        functools.partial(finish_kernel, count),
+        out_shape=tuple(jax.ShapeDtypeStruct(shape, F32) for shape in shapes)
+        + (
+            jax.ShapeDtypeStruct(z_rows.shape, BF),
+            jax.ShapeDtypeStruct(dx_rows.shape, F32),
+            jax.ShapeDtypeStruct((6, part, width), F32),
+            jax.ShapeDtypeStruct((class_count, width), F32),
+            jax.ShapeDtypeStruct((1, part), F32),
+            jax.ShapeDtypeStruct((1, part), F32),
+            jax.ShapeDtypeStruct((1, 3), F32),
+        ),
+        in_specs=[anywhere] * 3 + [vmem] * 4,
+        out_specs=[anywhere] * 8 + [vmem] * 3,
         scratch_shapes=[pltpu.VMEM(flat.shape, BF)]
         + [pltpu.VMEM(shape, F32) for shape in shapes]
-        + [pltpu.SemaphoreType.DMA((5, 2)), pltpu.SemaphoreType.DMA((5,))],
-        compiler_params=pltpu.CompilerParams(vmem_limit_bytes=48 * 2**20),
-    )(flat)
+        + [
+            pltpu.VMEM((6, 3 * LANES, width), F32),
+            pltpu.VMEM((-(-class_count // LANES) * LANES, width), F32),
+            pltpu.VMEM(z_rows.shape, BF),
+            pltpu.VMEM(dx_rows.shape, F32),
+            pltpu.SemaphoreType.DMA((5, 3)),
+            pltpu.SemaphoreType.DMA((14,)),
+        ],
+        compiler_params=pltpu.CompilerParams(vmem_limit_bytes=60 * 2**20),
+    )(flat, z_rows, dx_rows, dmod_all, sum_all, extra_all, select)
 
 
 def time_embed(bin_row, feature_count):
@@ -1243,12 +1501,10 @@
     heads = q_gain.shape[1] // HEAD_DIM
     select = jnp.asarray(head_select(heads), BF)
 
-    def condition(bin_row, label_row):
-        one_hot = label_row[:, None] == jnp.arange(class_table.shape[0], dtype=jnp.int32)[None, :]
-        picked = jnp.dot(one_hot.astype(BF), class_table, preferred_element_type=F32)
-        return time_embed(bin_row, width) + picked, one_hot
-
-    cond, _ = condition(bins.reshape(images), labels.reshape(images))
+    label_row = labels.reshape(images)
+    one_hot = label_row[:, None] == jnp.arange(class_table.shape[0], dtype=jnp.int32)[None, :]
+    picked = jnp.dot(one_hot.astype(BF), class_table, preferred_element_type=F32)
+    cond = time_embed(bins.reshape(images), width) + picked
     silu_low = jax.nn.silu(cond).astype(BF)
     mod_w = mod_weight[0]
     part = width // 4
@@ -1258,38 +1514,31 @@
 
     order = jnp.stack([me, (me + 2) % 4, me + 1 - 2 * (me % 2), (me + 2) % 4 + 1 - 2 * (me % 2)])
     placed = jnp.take(places.reshape(images, 4, rows), order, axis=1).reshape(images * 4 * rows)
-    grid = jnp.arange(GRID, dtype=jnp.int32)[None, :]
-    marks = jnp.concatenate([placed[:, None] // GRID == grid, placed[:, None] % GRID == grid], axis=1).astype(F32)
-    angles = jnp.dot(marks, jnp.asarray(angle_table()), precision=lax.Precision.HIGHEST)
-    angles = angles.reshape(images, 4 * rows, 2 * LANES)
-
-    wqkv = jnp.einsum("ef,jde->jfd", select, qkv_weight[0], preferred_element_type=F32).astype(BF)
-    wout = jnp.einsum("ef,ed->fd", select, out_weight[0], preferred_element_type=F32).astype(BF)
-    gains = jnp.dot(jnp.concatenate([q_gain, k_gain], axis=0), select, preferred_element_type=F32)
+    spot = jnp.arange(6 * GRID, dtype=jnp.int32)[None, :] % (2 * GRID)
+    marks = (jnp.where(spot < GRID, placed[:, None] // GRID, placed[:, None] % GRID + GRID) == spot).astype(BF)
+    table, table_parts = angle_table(), []
+    for _ in range(3):
+        table_parts.append(table.astype(BF))
+        table = table - table_parts[-1].astype(np.float32)
+    turns = jnp.dot(marks, jnp.asarray(np.concatenate(table_parts)), preferred_element_type=F32)
+    turns = turns.reshape(images, 4 * rows, 2 * LANES)
 
     results = run_main(
         tokens.reshape(images, rows, width),
         velocity_grad.reshape(images, rows, width),
         mod_cols,
-        angles[..., :LANES],
-        angles[..., LANES:],
-        wqkv,
-        wout,
+        turns,
+        jnp.transpose(qkv_weight[0], (0, 2, 1)),
+        out_weight[0],
         gate_up_weight[0],
         down_weight[0],
-        gains,
+        q_gain,
+        k_gain,
+        select,
     )
     z_rows, dx_rows, dmod_part, gain_sums, squares, a1, a2, d_ffn, d_attn, units, mixed, d_gu, d_qkv = results
 
-    dmod_mine = lax.dynamic_slice(dmod_part, (0, 0, shift), (images, 6, part))
-    grad_silu = jnp.einsum("ijf,djf->id", dmod_mine, mod_w, preferred_element_type=F32)
-    sig = jax.nn.sigmoid(cond)
-    grad_cond = grad_silu * (sig + cond * sig * (1.0 - sig))
-    summand = jnp.concatenate([grad_cond, squares], axis=0)
     lanes_all = heads * LANES
-    numbers = jnp.stack([bins.reshape(images), labels.reshape(images)]).astype(F32)
-    extra = jnp.concatenate([gain_sums[0:2], jnp.pad(numbers, ((0, 4), (0, lanes_all - images)))], axis=0)
-
     flat = images * 4 * rows
     flat_grads, dmod_all, sum_all, extra_all = run_tail(
         dp,
@@ -1301,41 +1550,40 @@
         d_qkv.reshape(flat, d_qkv.shape[2]),
         mixed.reshape(flat, lanes_all),
         d_attn.reshape(flat, width),
+        jnp.transpose(mod_w, (1, 2, 0)),
         select,
-        summand,
-        dmod_part.reshape(images * 8, 3 * LANES),
-        extra,
+        cond,
+        squares,
+        silu_low,
+        dmod_part.reshape(8 * images, 3 * LANES),
+        gain_sums,
+        label_row,
     )
-    finished = run_finish(flat_grads, width, units.shape[2], part)
-    gate_up_grad, down_grad, out_grad = finished[0][None], finished[1][None], finished[3][None]
-    qkv_grad = jnp.transpose(finished[2].reshape(3, part, width), (0, 2, 1))[None]
-
-    gains_sum = jnp.sum(extra_all[:, 0:2], axis=0)
-    gains_sum = jnp.einsum("jf,ef->je", gains_sum, select.astype(F32), precision=lax.Precision.HIGHEST)
-    bins_all = extra_all[:, 2, :images].reshape(dp * images).astype(jnp.int32)
-    labels_all = extra_all[:, 3, :images].reshape(dp * images).astype(jnp.int32)
-    cond_all, one_hot = condition(bins_all, labels_all)
-    silu_all = jax.nn.silu(cond_all).astype(BF)
-    dmod_all = lax.dynamic_slice(
-        dmod_all.reshape(dp * images, 8, 3 * LANES), (0, 0, shift), (dp * images, 6, part)
+    count = images * rows * width * dp * lax.axis_size("tensor")
+    finished = run_finish(
+        count,
+        class_table.shape[0],
+        units.shape[2],
+        flat_grads,
+        z_rows,
+        dx_rows,
+        dmod_all,
+        sum_all,
+        extra_all,
+        select,
     )
-    mod_grad = jnp.einsum("id,ijf->djf", silu_all, dmod_all, preferred_element_type=F32)[None]
-    grad_cond_all = sum_all[:, 0:8].reshape(dp * images, width)
-    class_grad = jnp.dot(one_hot.astype(BF).T, grad_cond_all, preferred_element_type=F32)
-    square_totals = jnp.sum(extra_all[:, 8:11, 0:LANES], axis=(0, 2))
-    count = images * rows * width * dp * lax.axis_size("tensor")
-    stats = jnp.sqrt(square_totals / count)[None, :]
+    gate_up_grad, down_grad, qkv_grad, out_grad, z_out, dx_out, mod_grad, class_grad, q_grad, k_grad, stats = finished
     whole = (1, micro, per_micro, rows, width)
     return (
-        z_rows.reshape(whole),
-        dx_rows.reshape(whole),
-        mod_grad,
-        qkv_grad,
-        out_grad,
-        gate_up_grad,
-        down_grad,
-        gains_sum[0:1],
-        gains_sum[1:2],
+        z_out.reshape(whole),
+        dx_out.reshape(whole),
+        jnp.transpose(mod_grad, (2, 0, 1))[None],
+        jnp.transpose(qkv_grad.reshape(3, part, width), (0, 2, 1))[None],
+        out_grad[None],
+        gate_up_grad[None],
+        down_grad[None],
+        q_grad,
+        k_grad,
         class_grad,
         stats,
     )

time: 577 us -> 538 us (0.932)
  matrix products: 29.3 us -> 8.92 us
  local copies, waits for them, and re-layouts: 12.5 us -> 3.11 us
  other arithmetic: 7.11 us -> 1.12 us
    dot_general x10 -> x2, matrix products: 25.7 us -> 5.47 us  [the longest x1 2.73 us: per_device(): jnp.dot(one_hot.astype(BF), class_table, preferred_element_type=F32)]
    pallas_call x1, Pallas kernels: 8.02 us -> 17.5 us  [run_finish(): pl.pallas_call(functools.partial(finish_kernel, count), out_shape=tuple((...]
    pallas_call x1, Pallas kernels: 315 us -> 308 us  [run_main(): pl.pallas_call(functools.partial(main_kernel, images, heads), out_shape=o...]
where the time goes in v4:
time: 538 us; the launch traced here: 534 us
  Pallas kernels  519 us (96%)
  matrix products  8.92 us (2%)
    pallas_call x1, Pallas kernels, run_main(): pl.pallas_call(functools.partial(main_kernel, images, heads), out_shape=o...  308 us
    pallas_call x1, Pallas kernels, run_tail(): pl.pallas_call(functools.partial(tail_kernel, dp), out_shape=(jax.ShapeDt...  194 us
    pallas_call x1, Pallas kernels, run_finish(): pl.pallas_call(functools.partial(finish_kernel, count), out_shape=tuple((...  17.5 us

profile of v4, /device:TPU:0, one launch (start us, length us, event | category | flops | bytes accessed | tf_op | source)
XLA Modules:
  0.0 533.9 jit_solution(12942008753623478424)
XLA Ops:
  0.7 0.1 compare_and_fusion
  0.7 0.1 fusion.12
  0.8 0.7 convert_add_fusion
  1.5 0.1 copy.32
  1.6 0.1 add.97
  1.7 0.8 copy.33
  2.5 0.1 eq.32.labels
  2.6 0.0 copy-start.3
  2.6 0.8 reshape.393
  3.4 0.5 gather_fusion
  3.9 0.1 select_bitcast_fusion
  4.0 0.0 copy-start.2
  4.0 0.1 select_n.110
  4.1 0.2 multiply_cosine_fusion
  4.3 2.7 multiply_convert_fusion
  7.0 0.0 copy-start.1
  7.0 3.5 fusion
  10.5 0.6 dynamic_update_slice.3.mod_cols
  11.1 0.0 copy-done.3
  11.1 0.0 copy-done.2
  11.1 0.0 copy-start
  11.2 2.7 fusion.2
  13.9 0.0 copy-done
  13.9 307.5 %shard_map.230 = (bf16[8,64,1152]{2,1,0:T(8,128)(2,1)}, f32[8,64,1152]{2,1,0:T(8,128)}, bf16[8,8,384]{2,1,0:T(8,128)(2,1)}, f32[8,512]{1,0:T(8,128)}, f32[8,1152...) custom-call(bf16[8,64,1152]{2,1,0:T(8,128)(2,1)} %bitcast.66, ...), custom_call_target="tpu_custom_call" | custom-call | tf_op jit(solution)/shard_map/pallas_call | solution.py:805
  321.4 0.0 copy-done.1
  321.4 194.3 %shard_map.231 = (bf16[35712,128]{1,0:T(8,128)(2,1)}, bf16[4,64,384]{2,1,0:T(8,128)(2,1)}, bf16[4,16,1152]{2,1,0:T(8,128)(2,1)}, f32[4,16,512]{2,1,0:T(8,128)}) custom-call(bf16[2048,1152]{1,0:T(8,128)(2,1)} %bitcast.58, bf16[2048,1536]{1,0:T(8,128)(2,1)} %bitcast.55, bf16[2048,768]{1,0:T(8,128)(2,1)} %bitcast.62, bf16[2048,1152]{1,0:T(8,128)(2,1)} %bitcast.59, ...), custom_call_target="tpu_custom_call" | custom-call | tf_op jit(solution)/shard_map/pallas_call | solution.py:1266
  515.8 17.5 %shard_map.232 = (f32[2,1152,768]{2,1,0:T(8,128)}, f32[768,1152]{1,0:T(8,128)}, f32[864,1152]{1,0:T(8,128)}, f32[288,1152]{1,0:T(8,128)}, bf16[8,64,1152]{2,1,0:...) custom-call(bf16[35712,128]{1,0:T(8,128)(2,1)} %get-tuple-element.50, ...), custom_call_target="tpu_custom_call" | custom-call | tf_op jit(solution)/shard_map/pallas_call | solution.py:1446
  (9 shorter events, 0.1 us)
Async XLA Ops:
  2.6 8.6 %copy-start.3 = (s32[8]{0:T(128)}, s32[8]{0:T(128)S(1)}, u32[]{:S(2)}) copy-start(s32[8]{0:T(128)S(1)} %eq.32.labels) | copy-start | bytes 100
  4.0 7.1 %copy-start.2 = (bf16[96,256]{1,0:T(8,128)(2,1)S(1)}, bf16[96,256]{1,0:T(8,128)(2,1)}, u32[]{:S(2)}) copy-start(bf16[96,256]{1,0:T(8,128)(2,1)} %constant.107.clone) | copy-start | bytes 147460
  7.0 314.4 %copy-start.1 = (bf16[8,1152]{1,0:T(8,128)(2,1)}, bf16[8,1152]{1,0:T(8,128)(2,1)S(1)}, u32[]{:S(2)}) copy-start(bf16[8,1152]{1,0:T(8,128)(2,1)S(1)} %get-tuple-element.71.silu) | copy-start | bytes 55300
  11.1 2.7 copy-start

commit v5 on v4

--- a/solution.py
+++ b/solution.py
@@ -111,7 +111,8 @@
     tok,
     vel,
     mod_cols,
-    turns,
+    places,
+    angles,
     qkv_hbm,
     out_hbm,
     wgu_hbm,
@@ -132,6 +133,7 @@
     mix_hbm,
     dgu_hbm,
     dqkv_hbm,
+    turns,
     wqkv,
     wout,
     wgu,
@@ -152,14 +154,12 @@
     send_y,
     recv_y,
     mix_st,
-    units_st,
     hid_st,
     dgu_st,
     dqkv_st,
     mod,
     mod_recv,
     dmod,
-    dmod_sum,
     mod_sems,
     dmod_sems,
     ag_sems,
@@ -224,6 +224,16 @@
             src_ref=src, dst_ref=dst, send_sem=send_sem, recv_sem=recv_sem, device_id=where, device_id_type=MESH
         )
 
+    def gather(which, buf, n, kind):
+        src, dst, where = ((0, rows, across), (0, 2 * rows, sib), (rows, 3 * rows, sib))[kind]
+        return remote(
+            buf.at[n, pl.ds(src, rows)],
+            buf.at[n, pl.ds(dst, rows)],
+            ag_sems.at[which, 2 * kind, n],
+            ag_sems.at[which, 2 * kind + 1, n],
+            {"tensor": where},
+        )
+
     def its_tiles(device):
         return pl.ds(pl.multiple_of(device * (2 * LANES), LANES), 3 * LANES)
 
@@ -241,6 +251,18 @@
 
     for k in (1, 2, 0):
         mod_copy(k).start()
+
+    @pl.when(enc)
+    def _():
+        load_x.wait()
+        a1f[0, 0:rows, :] = xin[0]
+        gather(0, a1f, 0, 0).start()
+        gather(0, a1f, 0, 1).start()
+
+    @pl.when(dec)
+    def _():
+        load_d.wait()
+
     for copy in load_w:
         copy.start()
     mod[:, :, its_tiles(me)] = mod_cols[...]
@@ -257,27 +279,24 @@
             value += dot_tn(select[tokens:part, :], dattn[2 * j + 1, 0 : part - tokens, span])
             ref[:, span] = value.astype(BF)
 
-    @pl.when(enc)
-    def _():
-        load_x.wait()
-
-    @pl.when(dec)
-    def _():
-        load_d.wait()
+    spots = jnp.concatenate([places[i] for i in range(places.shape[0])], axis=0).astype(F32).T
+    lane = lax.broadcasted_iota(jnp.int32, (rows, LANES), 1)
+    spot = lax.rem(lane, 2 * GRID)
+    by_row, used = spot < GRID, lane < 6 * GRID
+    spot = jnp.where(by_row, spot, spot - GRID).astype(F32)
+    for block in range(4):
+        high, low, my_high, my_low = block // 2, block % 2, lax.div(me, 2), lax.rem(me, 2)
+        at = high + my_high - 2 * high * my_high + 2 * (low + my_low - 2 * low * my_low)
+        here = pl.ds(pl.multiple_of(at * rows, rows), rows)
+        mine = slice(block * rows, (block + 1) * rows)
+        for n in range(images):
+            row = jnp.floor(spots[mine, n : n + 1] * (1.0 / GRID))
+            marks = jnp.where(by_row, row, spots[mine, n : n + 1] - GRID * row) == spot
+            turns[n, here, :] = dot(jnp.where(marks & used, 1.0, 0.0).astype(BF), angles[...])
 
     for k in range(3):
         mod_copy(k).wait()
         mod[:, :, its_tiles(peers[k])] += mod_recv[k]
-
-    def gather(which, buf, n, kind):
-        src, dst, where = ((0, rows, across), (0, 2 * rows, sib), (rows, 3 * rows, sib))[kind]
-        return remote(
-            buf.at[n, pl.ds(src, rows)],
-            buf.at[n, pl.ds(dst, rows)],
-            ag_sems.at[which, 2 * kind, n],
-            ag_sems.at[which, 2 * kind + 1, n],
-            {"tensor": where},
-        )
 
     def gather_start(which, buf, n):
         gather(which, buf, n, 0).start()
@@ -417,16 +436,35 @@
 
         values = xin[n].astype(F32)
         sacc[0:1, :] += column_sum(values * values)
-        a1f[n, 0:rows, :] = modulated(values, mod_row(n, 0), mod_row(n, 1)).astype(BF)
+
+        @pl.when(dec | (n > 0))
+        def _():
+            a1f[n, 0:rows, :] = modulated(values, mod_row(n, 0), mod_row(n, 1)).astype(BF)
+
+            @pl.when(enc)
+            def _():
+                gather(0, a1f, n, 0).start()
+
+            gather(0, a1f, n, 1).start()
+
+    def attn_drain(n):
+        gather(0, a1f, n, 1).wait_send()
+        gather(0, a1f, n, 2).wait_send()
 
         @pl.when(enc)
         def _():
-            gather(0, a1f, n, 0).start()
-
-        gather(0, a1f, n, 1).start()
+            gather(0, a1f, n, 0).wait_send()
 
     def attn_compute(n):
         gather_wait(0, a1f, n)
+
+        @pl.when(enc & (n == 0))
+        def _():
+            attn_drain(n)
+            for at in range(0, 4 * rows, rows):
+                values = a1f[0, at : at + rows, :].astype(F32)
+                a1f[0, at : at + rows, :] = modulated(values, mod_row(0, 0), mod_row(0, 1)).astype(BF)
+
         staged_ready(5, n)
         a1 = a1f[n]
         c, s = turns[n, :, 0:LANES], turns[n, :, LANES : 2 * LANES]
@@ -449,12 +487,10 @@
         scatter_start(0, n)
         out_copy(5, n).start()
         out_copy(0, n).start()
-        gather(0, a1f, n, 1).wait_send()
-        gather(0, a1f, n, 2).wait_send()
-
-        @pl.when(enc)
-        def _():
-            gather(0, a1f, n, 0).wait_send()
+
+        @pl.when(dec | (n > 0))
+        def _():
+            attn_drain(n)
 
     def ffn_in(n):
         attended = scatter_end(0, n)
@@ -489,8 +525,8 @@
                 span = pl.ds(at, size)
                 gate_val = dot(a2, wgu[0, :, span])
                 up_val = dot(a2, wgu[1, :, span])
-                units_st[:, span] = (gate_val * jax.nn.sigmoid(gate_val) * up_val).astype(BF)
-            ffn_down(n, units_st[...])
+                hid_st[:, span] = (gate_val * jax.nn.sigmoid(gate_val) * up_val).astype(BF)
+            ffn_down(n, hid_st[...])
 
     def block_out(n):
         feedfwd = scatter_end(1, n)
@@ -722,7 +758,7 @@
             dmod_copy(k, n).wait()
             part += mod_recv[k, n]
         for j in range(8):
-            dmod_sum[j, pl.ds(n, 1), :] = part[j : j + 1]
+            mod[j, pl.ds(n, 1), 0 : 3 * LANES] = part[j : j + 1]
 
         @pl.when(enc)
         def _():
@@ -735,10 +771,10 @@
         return carry
 
     lax.fori_loop(0, images, drain, 0)
-    dmod_part[...] = dmod_sum[...].astype(BF)
-
-
-def run_main(tok, vel, mod_cols, turns, qkv, out, wgu, wdn, q_gain, k_gain, select):
+    dmod_part[...] = mod[:, :, 0 : 3 * LANES].astype(BF)
+
+
+def run_main(tok, vel, mod_cols, places, angles, qkv, out, wgu, wdn, q_gain, k_gain, select):
     images, rows, width = tok.shape
     tokens = 4 * rows
     lanes_all = select.shape[1]
@@ -766,6 +802,7 @@
         hbm(3 * lanes_all),
     )
     scratch = [
+        pltpu.VMEM((images, tokens, 2 * LANES), F32),
         pltpu.VMEM((3, lanes_all, width), BF),
         pltpu.VMEM((lanes_all, width), BF),
         pltpu.VMEM(wgu.shape, BF),
@@ -787,13 +824,11 @@
         pltpu.VMEM((4, SLOTS, rows, width), BF),
         pltpu.VMEM((tokens, lanes_all), BF),
         pltpu.VMEM((tokens, hidden), BF),
-        pltpu.VMEM((tokens, hidden), BF),
         pltpu.VMEM((tokens, 2 * hidden), BF),
         pltpu.VMEM((tokens, 3 * lanes_all), BF),
         pltpu.VMEM((images, 8, width), F32),
         pltpu.VMEM((3, images, 8, 3 * LANES), F32),
         pltpu.VMEM((images, 8, width), F32),
-        pltpu.VMEM((8, images, 3 * LANES), F32),
         pltpu.SemaphoreType.DMA((2, 3)),
         pltpu.SemaphoreType.DMA((2, 3, images)),
         pltpu.SemaphoreType.DMA((4, 6, images)),
@@ -805,13 +840,13 @@
     return pl.pallas_call(
         functools.partial(main_kernel, images, heads),
         out_shape=out_shape,
-        in_specs=[anywhere, anywhere] + [vmem] * 2 + [anywhere] * 4 + [vmem] * 3,
+        in_specs=[anywhere, anywhere] + [vmem] * 3 + [anywhere] * 4 + [vmem] * 3,
         out_specs=[vmem] * 5 + [anywhere] * 8,
         scratch_shapes=scratch,
         compiler_params=pltpu.CompilerParams(
-            collective_id=0, has_side_effects=True, vmem_limit_bytes=62 * 2**20
+            collective_id=0, has_side_effects=True, vmem_limit_bytes=63 * 2**20
         ),
-    )(tok, vel, mod_cols, turns, qkv, out, wgu, wdn, q_gain, k_gain, select)
+    )(tok, vel, mod_cols, places, angles, qkv, out, wgu, wdn, q_gain, k_gain, select)
 
 
 def flat_plan(width, hidden, part):
@@ -1083,16 +1118,18 @@
 
     def pass_total(direction, c):
         begins, ends = behind(direction) == 0, behind(direction) == dp - 1
-
-        @pl.when(jnp.logical_not(ends))
+        passes = jnp.logical_not(begins) & jnp.logical_not(ends)
+        back = c >= whole
+
+        @pl.when(passes | (back & jnp.logical_not(ends)))
         def _():
             total_copy(direction, c).wait_recv()
 
-            @pl.when(jnp.logical_not(begins))
-            def _():
-                total_copy(direction, c).start()
-
-        @pl.when(c >= whole)
+        @pl.when(passes)
+        def _():
+            total_copy(direction, c).start()
+
+        @pl.when(back)
         def _():
             lent_total(direction, c - whole).start()
 
@@ -1250,6 +1287,10 @@
             @pl.when(behind(direction) != 0)
             def _():
                 total_copy(direction, c).wait_send()
+
+            @pl.when((behind(direction) == 0) & (c < whole))
+            def _():
+                total_copy(direction, c).wait_recv()
 
         return carry
 
@@ -1512,22 +1553,18 @@
     shift = me * (part - 2 * LANES)
     mod_cols = lax.dynamic_update_slice(jnp.zeros((images, 8, 3 * LANES), F32), columns, (0, 0, shift))
 
-    order = jnp.stack([me, (me + 2) % 4, me + 1 - 2 * (me % 2), (me + 2) % 4 + 1 - 2 * (me % 2)])
-    placed = jnp.take(places.reshape(images, 4, rows), order, axis=1).reshape(images * 4 * rows)
-    spot = jnp.arange(6 * GRID, dtype=jnp.int32)[None, :] % (2 * GRID)
-    marks = (jnp.where(spot < GRID, placed[:, None] // GRID, placed[:, None] % GRID + GRID) == spot).astype(BF)
     table, table_parts = angle_table(), []
     for _ in range(3):
         table_parts.append(table.astype(BF))
         table = table - table_parts[-1].astype(np.float32)
-    turns = jnp.dot(marks, jnp.asarray(np.concatenate(table_parts)), preferred_element_type=F32)
-    turns = turns.reshape(images, 4 * rows, 2 * LANES)
+    table_parts.append(np.zeros((LANES - 6 * GRID, 2 * LANES), BF))
 
     results = run_main(
         tokens.reshape(images, rows, width),
         velocity_grad.reshape(images, rows, width),
         mod_cols,
-        turns,
+        places,
+        jnp.asarray(np.concatenate(table_parts)),
         jnp.transpose(qkv_weight[0], (0, 2, 1)),
         out_weight[0],
         gate_up_weight[0],

time: 538 us -> 531 us (0.987)
  no operation moved by 1% of the time
where the time goes in v5:
time: 531 us; the launch traced here: 527 us
  Pallas kernels  516 us (97%)
  matrix products  6.19 us (1%)
    pallas_call x1, Pallas kernels, run_main(): pl.pallas_call(functools.partial(main_kernel, images, heads), out_shape=o...  305 us
    pallas_call x1, Pallas kernels, run_tail(): pl.pallas_call(functools.partial(tail_kernel, dp), out_shape=(jax.ShapeDt...  194 us
    pallas_call x1, Pallas kernels, run_finish(): pl.pallas_call(functools.partial(finish_kernel, count), out_shape=tuple((...  17.5 us

profile of v5, /device:TPU:0, one launch (start us, length us, event | category | flops | bytes accessed | tf_op | source)
XLA Modules:
  0.0 526.8 jit_solution(3489024922394358243)
XLA Ops:
  0.6 0.7 convert_add_fusion
  1.3 0.1 copy.29
  1.4 0.1 add.21
  1.5 0.8 copy.30
  2.3 0.1 eq.15.labels
  2.4 0.0 copy-start.2
  2.4 0.2 multiply_cosine_fusion
  2.5 2.7 multiply_convert_fusion
  5.3 0.0 copy-start.1
  5.3 3.5 fusion
  8.8 0.6 dynamic_update_slice.3.mod_cols
  9.4 0.0 copy-start
  9.4 0.6 copy-done
  10.0 304.7 %shard_map.230 = (bf16[8,64,1152]{2,1,0:T(8,128)(2,1)}, f32[8,64,1152]{2,1,0:T(8,128)}, bf16[8,8,384]{2,1,0:T(8,128)(2,1)}, f32[8,512]{1,0:T(8,128)}, f32[8,1152...) custom-call(bf16[8,64,1152]{2,1,0:T(8,128)(2,1)} %bitcast.51, ...), custom_call_target="tpu_custom_call" | custom-call | tf_op jit(solution)/shard_map/pallas_call | solution.py:840
  314.8 0.0 copy-done.2
  314.8 0.0 copy-done.1
  314.8 193.9 %shard_map.231 = (bf16[35712,128]{1,0:T(8,128)(2,1)}, bf16[4,64,384]{2,1,0:T(8,128)(2,1)}, bf16[4,16,1152]{2,1,0:T(8,128)(2,1)}, f32[4,16,512]{2,1,0:T(8,128)}) custom-call(bf16[2048,1152]{1,0:T(8,128)(2,1)} %bitcast.43, bf16[2048,1536]{1,0:T(8,128)(2,1)} %bitcast.40, bf16[2048,768]{1,0:T(8,128)(2,1)} %bitcast.47, bf16[2048,1152]{1,0:T(8,128)(2,1)} %bitcast.44, ...), custom_call_target="tpu_custom_call" | custom-call | tf_op jit(solution)/shard_map/pallas_call | solution.py:1307
  508.7 17.5 %shard_map.232 = (f32[2,1152,768]{2,1,0:T(8,128)}, f32[768,1152]{1,0:T(8,128)}, f32[864,1152]{1,0:T(8,128)}, f32[288,1152]{1,0:T(8,128)}, bf16[8,64,1152]{2,1,0:...) custom-call(bf16[35712,128]{1,0:T(8,128)(2,1)} %get-tuple-element.50, ...), custom_call_target="tpu_custom_call" | custom-call | tf_op jit(solution)/shard_map/pallas_call | solution.py:1487
  (3 shorter events, 0.1 us)
Async XLA Ops:
  2.4 312.4 %copy-start.2 = (s32[8]{0:T(128)}, s32[8]{0:T(128)S(1)}, u32[]{:S(2)}) copy-start(s32[8]{0:T(128)S(1)} %eq.15.labels) | copy-start | bytes 100
  5.3 309.5 %copy-start.1 = (bf16[8,1152]{1,0:T(8,128)(2,1)}, bf16[8,1152]{1,0:T(8,128)(2,1)S(1)}, u32[]{:S(2)}) copy-start(bf16[8,1152]{1,0:T(8,128)(2,1)S(1)} %get-tuple-element.69.silu) | copy-start | bytes 55300
  9.4 0.6 copy-start

commit v6 on v5

--- a/solution.py
+++ b/solution.py
@@ -1014,27 +1014,34 @@
             gate_up_blocks(gu_half)
         elif i == 1:
             loads[6].wait()
+            gate_up_blocks(2)
+        elif i == 2:
             loads[7].wait()
-            gate_up_blocks(2, gu_half + 2)
-        elif i == 2:
-            gate_up_blocks(*range(4, gu_half, 2), *range(gu_half + 4, 2 * gu_half, 2))
+            gate_up_blocks(gu_half + 2)
+        elif i == 3:
+            gate_up_blocks(*range(4, gu_half, 2))
+        elif i == 4:
+            gate_up_blocks(*range(gu_half + 4, 2 * gu_half, 2))
             loads[12].start()
-        elif i == 3:
-            loads[8].wait()
-            turn_left(left_b, 0, tokens)
-            loads[10].start()
-            loads[9].wait()
-            for block in range(0, tiles, 2):
+        elif i in (5, 6):
+            if i == 5:
+                loads[8].wait()
+                turn_left(left_b, 0, tokens)
+                loads[10].start()
+                loads[9].wait()
+            split = tiles // 4 * 2
+            for block in range(0, split, 2) if i == 5 else range(split, tiles, 2):
                 cut = slice(block * LANES, min(width, (block + 2) * LANES))
                 put_wide(1, block, 0, dot(turned[0:hidden, :], right_b[:, cut]))
-            loads[13].start()
-        elif i == 4:
-            loads[11].wait()
-            loads[12].wait()
-            qkv_heads(*range(0, pairs // 2))
-        elif i == 5:
-            qkv_heads(*range(pairs // 2, pairs))
-        elif i == 6:
+            if i == 6:
+                loads[13].start()
+        elif i in (7, 8, 9):
+            if i == 7:
+                loads[11].wait()
+                loads[12].wait()
+            third = -(-pairs // 3)
+            qkv_heads(*range((i - 7) * third, min(pairs, (i - 6) * third)))
+        elif i == 10:
             loads[10].wait()
             loads[13].wait()
             value = dot(pick[...], dot_tn(left_b[:, 0:lanes_all], right_b[...]).astype(BF))
@@ -1237,7 +1244,7 @@
     def _():
         pl.semaphore_signal(here, inc=1, device_id={"section": 1}, device_id_type=MESH)
 
-    for step in range(6):
+    for step in range(10):
         chunk_step(step)
         portion(step + 1)
 
@@ -1254,7 +1261,7 @@
         chunk_step(step)
         return carry
 
-    lax.fori_loop(6, whole + LENT + 2 * skew * (dp - 1), later_step, 0)
+    lax.fori_loop(10, whole + LENT + 2 * skew * (dp - 1), later_step, 0)
 
     def lent_back(i, carry):
         for direction in range(2):

time: 531 us -> 525 us (0.989)
  no operation moved by 1% of the time
where the time goes in v6:
time: 525 us; the launch traced here: 521 us
  Pallas kernels  511 us (97%)
  matrix products  6.19 us (1%)
    pallas_call x1, Pallas kernels, run_main(): pl.pallas_call(functools.partial(main_kernel, images, heads), out_shape=o...  305 us
    pallas_call x1, Pallas kernels, run_tail(): pl.pallas_call(functools.partial(tail_kernel, dp), out_shape=(jax.ShapeDt...  189 us
    pallas_call x1, Pallas kernels, run_finish(): pl.pallas_call(functools.partial(finish_kernel, count), out_shape=tuple((...  17.5 us

profile of v6, /device:TPU:0, one launch (start us, length us, event | category | flops | bytes accessed | tf_op | source)
XLA Modules:
  0.0 521.2 jit_solution(4335310751195185074)
XLA Ops:
  0.6 0.7 convert_add_fusion
  1.3 0.1 copy.29
  1.4 0.1 add.21
  1.5 0.8 copy.30
  2.3 0.1 eq.15.labels
  2.4 0.0 copy-start.2
  2.4 0.2 multiply_cosine_fusion
  2.5 2.7 multiply_convert_fusion
  5.3 0.0 copy-start.1
  5.3 3.5 fusion
  8.8 0.6 dynamic_update_slice.3.mod_cols
  9.4 0.0 copy-start
  9.4 0.6 copy-done
  10.0 304.7 %shard_map.230 = (bf16[8,64,1152]{2,1,0:T(8,128)(2,1)}, f32[8,64,1152]{2,1,0:T(8,128)}, bf16[8,8,384]{2,1,0:T(8,128)(2,1)}, f32[8,512]{1,0:T(8,128)}, f32[8,1152...) custom-call(bf16[8,64,1152]{2,1,0:T(8,128)(2,1)} %bitcast.51, ...), custom_call_target="tpu_custom_call" | custom-call | tf_op jit(solution)/shard_map/pallas_call | solution.py:840
  314.8 0.0 copy-done.2
  314.8 0.0 copy-done.1
  314.8 188.7 %shard_map.231 = (bf16[35712,128]{1,0:T(8,128)(2,1)}, bf16[4,64,384]{2,1,0:T(8,128)(2,1)}, bf16[4,16,1152]{2,1,0:T(8,128)(2,1)}, f32[4,16,512]{2,1,0:T(8,128)}) custom-call(bf16[2048,1152]{1,0:T(8,128)(2,1)} %bitcast.43, bf16[2048,1536]{1,0:T(8,128)(2,1)} %bitcast.40, bf16[2048,768]{1,0:T(8,128)(2,1)} %bitcast.47, bf16[2048,1152]{1,0:T(8,128)(2,1)} %bitcast.44, ...), custom_call_target="tpu_custom_call" | custom-call | tf_op jit(solution)/shard_map/pallas_call | solution.py:1314
  503.5 17.5 %shard_map.232 = (f32[2,1152,768]{2,1,0:T(8,128)}, f32[768,1152]{1,0:T(8,128)}, f32[864,1152]{1,0:T(8,128)}, f32[288,1152]{1,0:T(8,128)}, bf16[8,64,1152]{2,1,0:...) custom-call(bf16[35712,128]{1,0:T(8,128)(2,1)} %get-tuple-element.50, ...), custom_call_target="tpu_custom_call" | custom-call | tf_op jit(solution)/shard_map/pallas_call | solution.py:1494
  (3 shorter events, 0.1 us)
Async XLA Ops:
  2.4 312.4 %copy-start.2 = (s32[8]{0:T(128)}, s32[8]{0:T(128)S(1)}, u32[]{:S(2)}) copy-start(s32[8]{0:T(128)S(1)} %eq.15.labels) | copy-start | bytes 100
  5.3 309.5 %copy-start.1 = (bf16[8,1152]{1,0:T(8,128)(2,1)}, bf16[8,1152]{1,0:T(8,128)(2,1)S(1)}, u32[]{:S(2)}) copy-start(bf16[8,1152]{1,0:T(8,128)(2,1)S(1)} %get-tuple-element.69.silu) | copy-start | bytes 55300
  9.4 0.6 copy-start

commit v7 on v6

--- a/solution.py
+++ b/solution.py
@@ -771,7 +771,7 @@
         return carry
 
     lax.fori_loop(0, images, drain, 0)
-    dmod_part[...] = mod[:, :, 0 : 3 * LANES].astype(BF)
+    dmod_part[...] = mod[0:6, :, 0 : 3 * LANES].astype(BF)
 
 
 def run_main(tok, vel, mod_cols, places, angles, qkv, out, wgu, wdn, q_gain, k_gain, select):
@@ -789,7 +789,7 @@
     out_shape = (
         jax.ShapeDtypeStruct((images, rows, width), BF),
         jax.ShapeDtypeStruct((images, rows, width), F32),
-        jax.ShapeDtypeStruct((8, images, 3 * LANES), BF),
+        jax.ShapeDtypeStruct((6, images, 3 * LANES), BF),
         jax.ShapeDtypeStruct((8, lanes_all), F32),
         jax.ShapeDtypeStruct((8, width), F32),
         hbm(width),
@@ -957,12 +957,8 @@
     for i in range(10):
         loads[i].start()
 
-    mod_w[...] = jnp.zeros_like(mod_w)
     mine = pl.ds(pl.multiple_of(me * (part - 2 * LANES), 16), part)
     mod_loads = [pltpu.make_async_copy(mod_hbm.at[j], mod_w.at[j, mine], load_sems.at[14 + j]) for j in range(6)]
-    for copy in mod_loads:
-        copy.start()
-
     barrier = pltpu.get_barrier_semaphore()
     for where in ({"tensor": sib}, {"tensor": across}):
         pl.semaphore_signal(barrier, inc=1, device_id=where, device_id_type=MESH)
@@ -1023,6 +1019,9 @@
         elif i == 4:
             gate_up_blocks(*range(gu_half + 4, 2 * gu_half, 2))
             loads[12].start()
+            mod_w[...] = jnp.zeros_like(mod_w)
+            for copy in mod_loads:
+                copy.start()
         elif i in (5, 6):
             if i == 5:
                 loads[8].wait()
@@ -1163,6 +1162,12 @@
             def _():
                 small(i)
 
+        for k in range(1, dp):
+
+            @pl.when(step == jnp.where(enc, 15, 25) + 2 * k)
+            def _():
+                hop(k)
+
     def sum_copy(which):
         where = ({"section": 1 - section}, {"tensor": sib}, {"tensor": across})[which]
         height = (8, 16, 16)[which]
@@ -1176,24 +1181,36 @@
             device_id_type=MESH,
         )
 
-    def all_copy(which, k, outgoing):
+    def all_copy(which, direction, slot):
         ref = (dmod_all, sum_all, extra_all)[which]
-        peer = lax.rem(place + k, dp)
-        slot = place if outgoing else peer
         return pltpu.make_async_remote_copy(
             src_ref=ref.at[slot],
             dst_ref=ref.at[slot],
-            send_sem=all_sems.at[which, 0, k],
-            recv_sem=all_sems.at[which, 1, slot],
-            device_id={"dp": peer},
+            send_sem=all_sems.at[which, direction, slot],
+            recv_sem=all_sems.at[which, 2, slot],
+            device_id=along(direction, True),
             device_id_type=MESH,
         )
+
+    def hop(k):
+        for direction in range(2):
+            slot = place - k if direction == 0 else place + k
+            there = (slot >= 0) & (slot < dp)
+
+            @pl.when(there)
+            def _():
+                for which in range(3):
+                    if k > 0:
+                        all_copy(which, direction, slot).wait_recv()
+
+            @pl.when(there & (behind(direction) < dp - 1))
+            def _():
+                for which in range(3):
+                    all_copy(which, direction, slot).start()
 
     def small(step):
         if step == 0:
             dmod_all[place] = dmod_low[...]
-            for k in range(1, dp):
-                all_copy(0, k, True).start()
 
             for copy in mod_loads:
                 copy.wait()
@@ -1233,9 +1250,7 @@
             extra_all[place, 8:16, 0:LANES] = square
             for i in range(8):
                 extra_all[place, 8 + i : 9 + i, LANES : 2 * LANES] = jnp.full((1, LANES), labels[i].astype(F32))
-            for k in range(1, dp):
-                all_copy(1, k, True).start()
-                all_copy(2, k, True).start()
+            hop(0)
 
     portion(0)
     pl.semaphore_wait(barrier, jnp.where(enc, dp + 2, dp + 1))
@@ -1279,10 +1294,14 @@
 
     lax.fori_loop(0, LENT, lent_back, 0)
 
-    for which in range(3):
-        for k in range(1, dp):
-            all_copy(which, k, True).wait_send()
-            all_copy(which, k, False).wait_recv()
+    for k in range(dp):
+        for direction in range(2):
+            slot = place - k if direction == 0 else place + k
+
+            @pl.when((slot >= 0) & (slot < dp) & (behind(direction) < dp - 1))
+            def _():
+                for which in range(3):
+                    all_copy(which, direction, slot).wait_send()
 
     def drain(c, carry):
         for direction in range(2):
@@ -1337,7 +1356,7 @@
             pltpu.SemaphoreType.DMA((2, 2, chunks)),
             pltpu.SemaphoreType.DMA((2, 2, chunks)),
             pltpu.SemaphoreType.DMA((3, 2)),
-            pltpu.SemaphoreType.DMA((3, 2, dp)),
+            pltpu.SemaphoreType.DMA((3, 3, dp)),
             pltpu.SemaphoreType.DMA((2, 2, LENT)),
             pltpu.SemaphoreType.DMA((2, 2, LENT)),
             pltpu.SemaphoreType.REGULAR,
@@ -1417,7 +1436,7 @@
     for copy in inward:
         copy.start()
 
-    dp, images = dmod_all.shape[0], dmod_all.shape[1] // 8
+    dp, images = dmod_all.shape[0], dmod_all.shape[1] // 6
     me = lax.axis_index("tensor")
     silu = jnp.concatenate([sum_all[p].astype(F32)[8:16] for p in range(dp)], axis=0).astype(BF)
     grad_cond = jnp.concatenate([sum_all[p].astype(F32)[0:8] for p in range(dp)], axis=0).astype(BF)
@@ -1599,7 +1618,7 @@
         cond,
         squares,
         silu_low,
-        dmod_part.reshape(8 * images, 3 * LANES),
+        dmod_part.reshape(6 * images, 3 * LANES),
         gain_sums,
         label_row,
     )

time: 525 us -> 525 us (level)
  no operation moved by 1% of the time
where the time goes in v7:
time: 525 us; the launch traced here: 521 us
  Pallas kernels  510 us (97%)
  matrix products  6.19 us (1%)
    pallas_call x1, Pallas kernels, run_main(): pl.pallas_call(functools.partial(main_kernel, images, heads), out_shape=o...  305 us
    pallas_call x1, Pallas kernels, run_tail(): pl.pallas_call(functools.partial(tail_kernel, dp), out_shape=(jax.ShapeDt...  188 us
    pallas_call x1, Pallas kernels, run_finish(): pl.pallas_call(functools.partial(finish_kernel, count), out_shape=tuple((...  17.5 us

profile of v7, /device:TPU:0, one launch (start us, length us, event | category | flops | bytes accessed | tf_op | source)
XLA Modules:
  0.0 520.8 jit_solution(14216510509695462398)
XLA Ops:
  0.6 0.7 convert_add_fusion
  1.3 0.1 copy.29
  1.4 0.1 add.21
  1.5 0.8 copy.30
  2.3 0.1 eq.15.labels
  2.4 0.0 copy-start.2
  2.4 0.2 multiply_cosine_fusion
  2.5 2.7 multiply_convert_fusion
  5.3 0.0 copy-start.1
  5.3 3.5 fusion
  8.8 0.6 dynamic_update_slice.3.mod_cols
  9.4 0.0 copy-start
  9.4 0.6 copy-done
  10.0 304.9 %shard_map.230 = (bf16[8,64,1152]{2,1,0:T(8,128)(2,1)}, f32[8,64,1152]{2,1,0:T(8,128)}, bf16[6,8,384]{2,1,0:T(8,128)(2,1)}, f32[8,512]{1,0:T(8,128)}, f32[8,1152...) custom-call(bf16[8,64,1152]{2,1,0:T(8,128)(2,1)} %bitcast.51, ...), custom_call_target="tpu_custom_call" | custom-call | tf_op jit(solution)/shard_map/pallas_call | solution.py:840
  314.9 0.0 copy-done.2
  314.9 0.0 copy-done.1
  315.0 188.0 %shard_map.231 = (bf16[35712,128]{1,0:T(8,128)(2,1)}, bf16[4,48,384]{2,1,0:T(8,128)(2,1)}, bf16[4,16,1152]{2,1,0:T(8,128)(2,1)}, f32[4,16,512]{2,1,0:T(8,128)}) custom-call(bf16[2048,1152]{1,0:T(8,128)(2,1)} %bitcast.43, bf16[2048,1536]{1,0:T(8,128)(2,1)} %bitcast.40, bf16[2048,768]{1,0:T(8,128)(2,1)} %bitcast.47, bf16[2048,1152]{1,0:T(8,128)(2,1)} %bitcast.44, ...), custom_call_target="tpu_custom_call" | custom-call | tf_op jit(solution)/shard_map/pallas_call | solution.py:1333
  503.0 17.5 %shard_map.232 = (f32[2,1152,768]{2,1,0:T(8,128)}, f32[768,1152]{1,0:T(8,128)}, f32[864,1152]{1,0:T(8,128)}, f32[288,1152]{1,0:T(8,128)}, bf16[8,64,1152]{2,1,0:...) custom-call(bf16[35712,128]{1,0:T(8,128)(2,1)} %get-tuple-element.50, ...), custom_call_target="tpu_custom_call" | custom-call | tf_op jit(solution)/shard_map/pallas_call | solution.py:1513
  (3 shorter events, 0.1 us)
Async XLA Ops:
  2.4 312.6 %copy-start.2 = (s32[8]{0:T(128)}, s32[8]{0:T(128)S(1)}, u32[]{:S(2)}) copy-start(s32[8]{0:T(128)S(1)} %eq.15.labels) | copy-start | bytes 100
  5.3 309.7 %copy-start.1 = (bf16[8,1152]{1,0:T(8,128)(2,1)}, bf16[8,1152]{1,0:T(8,128)(2,1)S(1)}, u32[]{:S(2)}) copy-start(bf16[8,1152]{1,0:T(8,128)(2,1)S(1)} %get-tuple-element.69.silu) | copy-start | bytes 55300
  9.4 0.6 copy-start
